TPU v7x, 32 devices: a whole 2x2x4 slice. The times are simulated.
32 devices in a mesh: ctx: 4 (over x, core), exp: 8 (over z, y).
Axes of the slice: x: 2, y: 2, z: 4, core: 2. Of those that a mesh axis runs over, the one named last changes fastest.
Arguments:
- queries: bfloat16 [8, 512, 1024], P('exp', 'ctx'), may hold values from -6 to 6
- keys: bfloat16 [8, 512, 1024], P('exp', 'ctx'), may hold values from -6 to 6
- values: bfloat16 [8, 512, 2048], P('exp', 'ctx'), may hold values from -6 to 6
- out_gate: bfloat16 [8, 512, 2048], P('exp', 'ctx'), may hold values from -6 to 6
- write_rate: float32 [8, 512, 16], P('exp', 'ctx'), may hold values from 0.02 to 0.2
- decay: float32 [8, 512, 16], P('exp', 'ctx'), may hold values from 0.6 to 1
- head_gain: float32 [128], replicated, may hold values from 0.1 to 1.9
- residual: bfloat16 [8, 512, 2048], P('exp', 'ctx'), may hold values from -6 to 6
- out_proj: bfloat16 [2048, 2048], P('ctx'), may hold values from -0.125 to 0.125
- ffn_gain: float32 [2048], replicated, may hold values from 0.25 to 1.75
- expert_ids: int32 [8, 512, 10], P('exp', 'ctx'), may hold values from 0 to 511, all different within a row; in each aligned block of 128 rows (0 to 127, 128 to 255, ..., all dimensions but the last counted through in order) at most 4 rows name the same one
- route_weight: float32 [8, 512, 10], P('exp', 'ctx'), may hold values from 0.1 to 0.4
- w_gate: bfloat16 [32, 2048, 512], P(('ctx', 'exp')), may hold values from -0.125 to 0.125
- w_up: bfloat16 [32, 2048, 512], P(('ctx', 'exp')), may hold values from -0.125 to 0.125
- w_down: bfloat16 [32, 512, 2048], P(('ctx', 'exp')), may hold values from -0.25 to 0.25
- ablate_mask: int32 [8, 512], P('exp', 'ctx'), may hold values 0 or 1
- direction: float32 [2048], replicated, may hold values from -6 to 6
Outputs:
- layer_out: bfloat16 [8, 512, 2048], P('exp', 'ctx')
Inputs may be any that keep to these rules, and one draw needn't show every extreme that they name: `expert_ids`: A token's 10 experts differ; within the rows of one device (aligned blocks of 128 tokens of a sequence) no expert is named more than 4 times.
All inputs are finite; a program needn't handle non-finite values. No bound on the sum of `ablate_mask` on one device may be relied on, other than what follows from the above.
Results may differ from a plain program's by a relative error of at most 0.0044.
Values may be sent and summed in bfloat16 or wider, within the bound.
No kernel may reach another device: no remote copies, remote signals or barrier semaphores. Data moves between devices by JAX's collectives and lax.ppermute only.
A program may use at most 128 MiB of HBM per device.

v0:
```python
import functools

import jax
import jax.numpy as jnp
from jax import lax
from jax.experimental import pallas as pl
from jax.experimental.pallas import tpu as pltpu
from jax.sharding import PartitionSpec as P

DK = 128
CAP = 4
EPS = 1e-06
LANES = 128

bf16 = jnp.bfloat16
f32 = jnp.float32


def mm(a, b):
    return jnp.dot(a, b, preferred_element_type=f32)


def mm_nt(a, b):
    return lax.dot_general(a, b, (((1,), (1,)), ((), ())), preferred_element_type=f32)


def mm_tn(a, b):
    return lax.dot_general(a, b, (((0,), (0,)), ((), ())), preferred_element_type=f32)


def split2(x):
    hi = x.astype(bf16)
    return hi, (x - hi.astype(f32)).astype(bf16)


def split3(x):
    hi = x.astype(bf16)
    rest = x - hi.astype(f32)
    mid = rest.astype(bf16)
    return hi, mid, (rest - mid.astype(f32)).astype(bf16)


def mm3(a, b):
    (ah, al), (bh, bl) = a, b
    return mm(jnp.concatenate([ah, al, ah], axis=1), jnp.concatenate([bh, bh, bl], axis=0))


def iota(shape, dim):
    return lax.broadcasted_iota(jnp.int32, shape, dim)


def compiler_params(mib):
    return pltpu.CompilerParams(vmem_limit_bytes=mib * 1024 * 1024)


def pack_kernel(n, kw, vw, k_ref, q_ref, v_ref, g_ref, w_ref, d_ref, *outs):
    me = lax.axis_index("ctx")
    tokens = k_ref.shape[1]
    heads = d_ref.shape[1]
    ones = (iota((tokens, tokens), 0) <= iota((tokens, tokens), 1)).astype(bf16)
    logs = jnp.log(d_ref[0])
    sums = sum(mm(piece, ones) for piece in reversed(split3(logs)))
    pieces = [*split3(sums), *split3(w_ref[0])]
    aux = jnp.concatenate([p.astype(f32) for p in pieces], axis=0)
    aux = jnp.concatenate([aux, jnp.zeros((LANES - 6 * heads, tokens), f32)], axis=0).astype(bf16)
    for step, out in enumerate(outs):
        to = lax.rem(me + step, n)
        kat = pl.ds(pl.multiple_of(to * kw, LANES), kw)
        vat = pl.ds(pl.multiple_of(to * vw, LANES), vw)
        out[:, 0:kw] = k_ref[0, :, kat]
        out[:, kw : 2 * kw] = q_ref[0, :, kat]
        out[:, 2 * kw : 2 * kw + vw] = v_ref[0, :, vat]
        out[:, 2 * kw + vw : 2 * kw + 2 * vw] = g_ref[0, :, vat]
        out[:, 2 * kw + 2 * vw :] = aux


def mixer_kernel(n, heads, kw, vw, *refs):
    pieces = refs[:n]
    gain_ref, proj_ref = refs[n : n + 2]
    keeps = refs[n + 2 : n + 2 + n // 2]
    gives = refs[n + 2 + n // 2 : n + 2 + n]
    x_ref, inv_ref, score_ref, state_ref, mixed_ref, sems = refs[n + 2 + n :]
    me = lax.axis_index("ctx")
    tokens = pieces[0].shape[0]
    local = vw // DK
    group = vw // kw
    copies = []
    for step in range(n):
        came = lax.rem(me - step + n, n)
        copy = pltpu.make_async_copy(pieces[step], x_ref.at[came], sems.at[step])
        copy.start()
        copies.append(copy)
    for copy in copies:
        copy.wait()

    row, col = iota((tokens, tokens), 0), iota((tokens, tokens), 1)
    apart = lax.bitwise_xor(row, col)
    eye = (row == col).astype(f32)
    r, l = iota((LANES, LANES), 0), iota((LANES, LANES), 1)
    kind = r // heads
    wanted = me * local + lax.rem(l, local)
    pick = (
        (lax.rem(r, heads) == wanted)
        & (l < 2 * local)
        & (kind // 3 == l // local)
    ).astype(bf16)

    def rates(block):
        aux = x_ref[block, :, 2 * kw + 2 * vw :]
        return mm_tn(aux, pick), mm_tn(pick, aux)

    def unit_scales(raw):
        raw_f = raw.astype(f32)
        return lax.rsqrt(jnp.sum(raw_f * raw_f, axis=1, keepdims=True) + EPS)

    def prepare(block, carry):
        as_cols, as_rows = rates(block)
        systems, all_scores = [], []
        for g in range(local // group):
            k = x_ref[block, :, g * DK : (g + 1) * DK]
            q = x_ref[block, :, kw + g * DK : kw + (g + 1) * DK]
            dots = mm_nt(k, k)
            scores = mm_nt(q, k)
            diag = dots * eye
            k_row = lax.rsqrt(jnp.sum(diag, axis=0, keepdims=True) + EPS)
            k_col = lax.rsqrt(jnp.sum(diag, axis=1, keepdims=True) + EPS)
            q_col = unit_scales(q) * DK ** (-0.5)
            dots = dots * k_row * k_col
            scores = scores * k_row * q_col
            for h in range(g * group, (g + 1) * group):
                gap = as_cols[:, h : h + 1] - as_rows[h : h + 1, :]
                ratios = jnp.exp(jnp.minimum(gap, 0.0))
                write = as_cols[:, local + h : local + h + 1]
                systems.append(jnp.where(row > col, write * ratios * dots, 0.0))
                all_scores.append(jnp.where(row >= col, ratios * scores, 0.0))
        near = [jnp.where(apart < 16, s, 0.0) for s in systems]
        inverse = [eye - s for s in near]
        power = [split2(s) for s in near]
        for _ in range(3):
            power = [split2(mm3(p, p)) for p in power]
            inverse = [x + mm3(split2(x), p) for x, p in zip(inverse, power)]
        size = 16
        while size < tokens:
            off = [split2(jnp.where((apart >= size) & (apart < 2 * size), s, 0.0)) for s in systems]
            halves = [split2(x) for x in inverse]
            left = [split2(mm3(x, o)) for x, o in zip(halves, off)]
            inverse = [x - mm3(a, xs) for x, a, xs in zip(inverse, left, halves)]
            size *= 2
        for h in range(local):
            hi, lo = split2(inverse[h])
            inv_ref[block, h, 0] = hi
            inv_ref[block, h, 1] = lo
            score_ref[block, h] = all_scores[h]
        return carry

    lax.fori_loop(0, n, prepare, 0)
    state_ref[...] = jnp.zeros_like(state_ref)
    gain = gain_ref[...]

    def advance(block, carry):
        as_cols, as_rows = rates(block)
        cumulative = jnp.exp(as_cols)
        rows_at = pl.ds(pl.multiple_of(block * tokens, tokens), tokens)
        for g in range(local // group):
            k = x_ref[block, :, g * DK : (g + 1) * DK]
            q = x_ref[block, :, kw + g * DK : kw + (g + 1) * DK]
            k_col = unit_scales(k)
            q_col = unit_scales(q) * DK ** (-0.5)
            both = jnp.concatenate([k, q], axis=0)
            for h in range(g * group, (g + 1) * group):
                state = state_ref[h]
                high, low = split2(state)
                seen = mm(jnp.concatenate([both, both], axis=1), jnp.concatenate([high, low], axis=0))
                v = x_ref[block, :, 2 * kw + h * DK : 2 * kw + (h + 1) * DK].astype(f32)
                cum = cumulative[:, h : h + 1]
                write = as_cols[:, local + h : local + h + 1]
                rhs = write * (v - (cum * k_col) * seen[:tokens])
                delta = mm3((inv_ref[block, h, 0], inv_ref[block, h, 1]), split2(rhs))
                out = (cum * q_col) * seen[tokens:] + mm3(split2(score_ref[block, h]), split2(delta))
                last = as_cols[tokens - 1 : tokens, h : h + 1]
                kept = jnp.exp(last - as_cols[:, h : h + 1]) * k_col
                dh, dl = split2(kept * delta)
                state_ref[h] = jnp.exp(last) * state + mm_tn(
                    jnp.concatenate([k, k], axis=0), jnp.concatenate([dh, dl], axis=0)
                )
                gate = x_ref[
                    block, :, 2 * kw + vw + h * DK : 2 * kw + vw + (h + 1) * DK
                ].astype(f32)
                mean = jnp.mean(out * out, axis=1, keepdims=True)
                normed = out * lax.rsqrt(mean + EPS) * gain * (gate / (1.0 + jnp.exp(-gate)))
                mixed_ref[rows_at, h * DK : (h + 1) * DK] = normed.astype(bf16)
        return carry

    lax.fori_loop(0, n, advance, 0)

    core = lax.rem(me, 2)
    for j in range(n // 2):
        chip = lax.rem(me // 2 + j, n // 2)
        for refs_out, half in ((gives, 1 - core), (keeps, core)):
            at = pl.multiple_of((chip * 2 + half) * tokens, tokens)
            mine = mixed_ref[pl.ds(at, tokens), :]
            width = 512
            for c in range(0, proj_ref.shape[1], width):
                part = mm(mine, proj_ref[:, c : c + width])
                refs_out[j][:, c : c + width] = part.astype(refs_out[j].dtype)


def dispatch_kernel(parts, *refs):
    residual_ref, gain_ref, ids_ref, weight_ref = refs[:4]
    part_refs = refs[4 : 4 + parts]
    hidden_ref, rows_ref, table_ref, flat_ref = refs[4 + parts :]
    tokens, width = hidden_ref.shape
    slots = table_ref.shape[0]
    chunks = width // LANES
    hidden = residual_ref[0].astype(f32)
    for part in part_refs:
        hidden = hidden + part[...].astype(f32)
    hidden_ref[...] = hidden
    mean = jnp.mean(hidden * hidden, axis=1, keepdims=True)
    normed = (hidden * lax.rsqrt(mean + EPS) * gain_ref[...]).astype(bf16)
    slot = iota((slots, tokens), 0)
    expert = slot // CAP
    named = jnp.zeros((slots, tokens), f32)
    weight = jnp.zeros((slots, tokens), f32)
    for j in range(ids_ref.shape[0]):
        hit = ids_ref[j] == expert
        named = named + hit.astype(f32)
        weight = weight + jnp.where(hit, weight_ref[j], 0.0)
    before = (iota((tokens, tokens), 0) < iota((tokens, tokens), 1)).astype(bf16)
    rank = mm(named.astype(bf16), before)
    chosen = jnp.where(rank == lax.rem(slot, CAP).astype(f32), named, 0.0)
    table_ref[...] = chosen * weight
    picker = chosen.astype(bf16)
    step = 512
    for c in range(0, width, step):
        rows = mm(picker, normed[:, c : c + step])
        for i in range(step // LANES):
            flat_ref[pl.ds(c // LANES + i, slots, stride=chunks), :] = rows[:, i * LANES : (i + 1) * LANES]
    rows_ref[...] = flat_ref[...].astype(bf16).reshape(rows_ref.shape)


def expert_kernel(rows_ref, gate_ref, up_ref, down_ref, out_ref, flat_ref, x_ref):
    slots = flat_ref.shape[0] * LANES // x_ref.shape[1]
    width = x_ref.shape[1]
    chunks = width // LANES
    flat_ref[...] = rows_ref[...].reshape(flat_ref.shape).astype(f32)
    for c in range(chunks):
        x_ref[:, c * LANES : (c + 1) * LANES] = flat_ref[pl.ds(c, slots, stride=chunks), :].astype(bf16)
    tile = 128

    def one(t, carry):
        x = x_ref[pl.ds(pl.multiple_of(t * tile, tile), tile), :]
        gate = mm(x, gate_ref[0])
        up = mm(x, up_ref[0])
        act = (gate / (1.0 + jnp.exp(-gate)) * up).astype(bf16)
        step = 512
        for c in range(0, width, step):
            y = mm(act, down_ref[0, :, c : c + step])
            for i in range(step // LANES):
                flat_ref[pl.ds(t * tile * chunks + c // LANES + i, tile, stride=chunks), :] = y[
                    :, i * LANES : (i + 1) * LANES
                ]
        return carry

    lax.fori_loop(0, slots // tile, one, 0)
    out_ref[...] = flat_ref[...].astype(bf16).reshape(out_ref.shape)


def combine_kernel(hidden_ref, table_ref, back_ref, mask_ref, dir_ref, out_ref, flat_ref, ret_ref):
    tokens, width = hidden_ref.shape
    slots = table_ref.shape[0]
    chunks = width // LANES
    flat_ref[...] = back_ref[...].reshape(flat_ref.shape).astype(f32)
    for c in range(chunks):
        got = flat_ref[pl.ds(c, slots, stride=chunks), :].astype(bf16)
        ret_ref[0:slots, c * LANES : (c + 1) * LANES] = got
        ret_ref[slots : 2 * slots, c * LANES : (c + 1) * LANES] = got
    high, low = split2(table_ref[...])
    moe = mm_tn(jnp.concatenate([high, low], axis=0), ret_ref[...])
    combined = hidden_ref[...] + moe
    direction = dir_ref[...]
    unit = direction / jnp.sqrt(jnp.sum(direction * direction, axis=1, keepdims=True) + EPS)
    along = jnp.sum(combined * unit, axis=1, keepdims=True)
    eye = iota((tokens, tokens), 0) == iota((tokens, tokens), 1)
    mask = jnp.sum(jnp.where(eye, mask_ref[...].astype(f32), 0.0), axis=1, keepdims=True)
    out_ref[0] = (combined - (mask * along) * unit).astype(bf16)


def local_part(
    n,
    devices,
    queries,
    keys,
    values,
    out_gate,
    write_rate,
    decay,
    head_gain,
    residual,
    out_proj,
    ffn_gain,
    expert_ids,
    route_weight,
    w_gate,
    w_up,
    w_down,
    ablate_mask,
    direction,
):
    tokens = queries.shape[1]
    heads = write_rate.shape[2]
    width = residual.shape[2]
    kw, vw = keys.shape[2] // n, values.shape[2] // n
    payload = 2 * kw + 2 * vw + LANES
    chips = n // 2
    slots = devices * CAP
    chunks = width // LANES
    shape = jax.ShapeDtypeStruct

    with jax.named_scope("pack"):
        packed = pl.pallas_call(
            functools.partial(pack_kernel, n, kw, vw),
            out_shape=[shape((tokens, payload), bf16)] * n,
            compiler_params=compiler_params(16),
        )(keys, queries, values, out_gate, write_rate.transpose(0, 2, 1), decay.transpose(0, 2, 1))
    with jax.named_scope("heads_exchange"):
        arrived = [packed[0]] + [
            lax.ppermute(packed[s], "ctx", [(i, (i + s) % n) for i in range(n)]) for s in range(1, n)
        ]
    with jax.named_scope("mixer"):
        vmem = pl.BlockSpec(memory_space=pltpu.VMEM)
        local = vw // DK
        outs = pl.pallas_call(
            functools.partial(mixer_kernel, n, heads, kw, vw),
            in_specs=[pl.BlockSpec(memory_space=pl.ANY)] * n + [vmem] * 2,
            out_shape=[shape((tokens, width), f32)] * chips + [shape((tokens, width), bf16)] * chips,
            scratch_shapes=[
                pltpu.VMEM((n, tokens, payload), bf16),
                pltpu.VMEM((n, local, 2, tokens, tokens), bf16),
                pltpu.VMEM((n, local, tokens, tokens), f32),
                pltpu.VMEM((local, DK, DK), f32),
                pltpu.VMEM((n * tokens, vw), bf16),
                pltpu.SemaphoreType.DMA((n,)),
            ],
            compiler_params=compiler_params(40),
        )(*arrived, head_gain.reshape(1, -1), out_proj)
    keeps, gives = outs[:chips], outs[chips:]
    with jax.named_scope("projection_sum"):
        sibling = [(i, i ^ 1) for i in range(n)]
        parts = []
        for j in range(chips - 1, 0, -1):
            pair = keeps[j] + lax.ppermute(gives[j], "ctx", sibling).astype(f32)
            parts.append(lax.ppermute(pair.astype(bf16), "ctx", [(i, (i + 2 * j) % n) for i in range(n)]))
        parts = [keeps[0], lax.ppermute(gives[0], "ctx", sibling)] + parts
    with jax.named_scope("dispatch"):
        hidden, rows, table = pl.pallas_call(
            functools.partial(dispatch_kernel, len(parts)),
            out_shape=[
                shape((tokens, width), f32),
                shape((devices, CAP * chunks, LANES), bf16),
                shape((slots, tokens), f32),
            ],
            scratch_shapes=[pltpu.VMEM((slots * chunks, LANES), f32)],
            compiler_params=compiler_params(48),
        )(
            residual,
            ffn_gain.reshape(1, -1),
            expert_ids.transpose(2, 0, 1),
            route_weight.transpose(2, 0, 1),
            *parts,
        )
    with jax.named_scope("to_experts"):
        came = lax.all_to_all(rows, ("ctx", "exp"), 0, 0, tiled=True)
    with jax.named_scope("experts"):
        done = pl.pallas_call(
            expert_kernel,
            out_shape=shape((devices, CAP * chunks, LANES), bf16),
            scratch_shapes=[pltpu.VMEM((slots * chunks, LANES), f32), pltpu.VMEM((slots, width), bf16)],
            compiler_params=compiler_params(48),
        )(came, w_gate, w_up, w_down)
    with jax.named_scope("from_experts"):
        back = lax.all_to_all(done, ("ctx", "exp"), 0, 0, tiled=True)
    with jax.named_scope("combine"):
        return pl.pallas_call(
            combine_kernel,
            out_shape=shape((1, tokens, width), bf16),
            scratch_shapes=[
                pltpu.VMEM((slots * chunks, LANES), f32),
                pltpu.VMEM((2 * slots, width), bf16),
            ],
            compiler_params=compiler_params(48),
        )(hidden, table, back, ablate_mask, direction.reshape(1, -1))


def solution(mesh):
    seq = P("exp", "ctx", None)
    owned = P(("ctx", "exp"), None, None)
    placed = (
        (seq,) * 6 + (P(), seq, P("ctx", None), P(), seq, seq) + (owned,) * 3 + (P("exp", "ctx"), P())
    )
    n = mesh.shape["ctx"]
    return jax.shard_map(
        functools.partial(local_part, n, n * mesh.shape["exp"]),
        mesh=mesh,
        in_specs=placed,
        out_specs=seq,
        check_vma=False,
    )
```

profile of v0, /device:TPU:0, one launch (start us, length us, event | category | flops | bytes accessed | tf_op | source)
XLA Modules:
  0.0 112.0 jit_solution(3994323792095926289)
XLA Ops:
  0.0 0.0 copy-start.3
  0.0 1.0 copy-done.3
  1.0 0.0 copy-start.4
  1.0 1.0 copy-done.4
  2.1 0.0 copy-start.6
  2.1 0.9 copy-done.6
  3.0 0.0 copy-start.7
  3.0 0.9 copy-done.7
  4.0 0.0 copy-start.8
  4.0 0.7 copy-done.8
  4.7 0.0 copy-start.9
  4.7 0.7 copy-done.9
  5.4 0.2 pack.1
  5.6 0.5 collective-permute-start
  6.1 2.6 %collective-permute-start.1 = (bf16[128,1664]{1,0:T(8,128)(2,1)S(1)}, bf16[128,1664]{1,0:T(8,128)(2,1)S(1)}, u32[]{:S(2)}, u32[]{:S(2)}) collective-permute-start(bf16[128,1664]{1,0:T(8,128)(2,1)S(1)} %get-tuple-element.18), channel_id=1, source_target_pairs={{0,16},{8,24},{16,0},{24,8},{1,17},{9,25},{17,1},{25,9},{2,18},{10... | collective-permute-start | bytes 1277960 | tf_op jit(solution)/shard_map/heads_exchange/ppermute | solution.py:328
  8.6 1.4 %collective-permute-start.2 = (bf16[128,1664]{1,0:T(8,128)(2,1)S(1)}, bf16[128,1664]{1,0:T(8,128)(2,1)S(1)}, u32[]{:S(2)}, u32[]{:S(2)}) collective-permute-start(bf16[128,1664]{1,0:T(8,128)(2,1)S(1)} %get-tuple-element.19), channel_id=1, source_target_pairs={{0,24},{8,0},{16,8},{24,16},{1,25},{9,1},{17,9},{25,17},{2,26},{10... | collective-permute-start | bytes 1277960 | tf_op jit(solution)/shard_map/heads_exchange/ppermute | solution.py:328
  10.0 7.4 %collective-permute-done.refs_1_ = bf16[128,1664]{1,0:T(8,128)(2,1)S(1)} collective-permute-done((bf16[128,1664]{1,0:T(8,128)(2,1)S(1)}, bf16[128,1664]{1,0:T(8,128)(2,1)S(1)}, u32[]{:S(2)}, u32[]{:S(2)}) %collective-permute-start) | collective-permute-done | bytes 426016 | tf_op jit(solution)/shard_map/heads_exchange/ppermute | solution.py:328
  17.5 1.8 %collective-permute-done.1.refs_2_ = bf16[128,1664]{1,0:T(8,128)(2,1)S(1)} collective-permute-done((bf16[128,1664]{1,0:T(8,128)(2,1)S(1)}, bf16[128,1664]{1,0:T(8,128)(2,1)S(1)}, u32[]{:S(2)}, u32[]{:S(2)}) %collective-permute-start.1) | collective-permute-done | bytes 426016 | tf_op jit(solution)/shard_map/heads_exchange/ppermute | solution.py:328
  19.3 8.0 %collective-permute-done.2.refs_3_ = bf16[128,1664]{1,0:T(8,128)(2,1)S(1)} collective-permute-done((bf16[128,1664]{1,0:T(8,128)(2,1)S(1)}, bf16[128,1664]{1,0:T(8,128)(2,1)S(1)}, u32[]{:S(2)}, u32[]{:S(2)}) %collective-permute-start.2) | collective-permute-done | bytes 426016 | tf_op jit(solution)/shard_map/heads_exchange/ppermute | solution.py:328
  27.3 0.0 copy-start.2
  27.3 1.6 %copy-done.2 = bf16[512,2048]{1,0:T(8,128)(2,1)S(1)} copy-done((bf16[512,2048]{1,0:T(8,128)(2,1)S(1)}, bf16[512,2048]{1,0:T(8,128)(2,1)}, u32[]{:S(2)}) %copy-start.2) | copy-done | bytes 2097176
  28.9 0.0 copy-start.14
  28.9 0.7 copy-done.14
  29.6 0.0 copy-start.5
  29.6 0.0 copy-start.10
  29.6 0.0 copy-start.12
  29.6 0.0 copy-start.13
  29.6 19.1 %mixer.1 = (f32[128,2048]{1,0:T(8,128)S(1)}, f32[128,2048]{1,0:T(8,128)S(1)}, bf16[128,2048]{1,0:T(8,128)(2,1)S(1)}, bf16[128,2048]{1,0:T(8,128)(2,1)S(1)}) custom-call(bf16[128,1664]{1,0:T(8,128)(2,1)S(1)} %get-tuple-element.16.refs_0_, bf16[128,1664]{1,0:T(8,128)(2,1)S(1)} %collective-permute-done.refs_1_, ...), custom_call_target="tpu_custom_call" | custom-call | tf_op jit(solution)/shard_map/mixer/pallas_call | solution.py:333
  48.7 0.1 collective-permute-start.4
  48.8 0.5 collective-permute-start.3
  49.3 1.4 %collective-permute-done.4 = bf16[128,2048]{1,0:T(8,128)(2,1)S(1)} collective-permute-done((bf16[128,2048]{1,0:T(8,128)(2,1)S(1)}, bf16[128,2048]{1,0:T(8,128)(2,1)S(1)}, u32[]{:S(2)}, u32[]{:S(2)}) %collective-permute-start.4) | collective-permute-done | bytes 524320 | tf_op jit(solution)/shard_map/projection_sum/ppermute | solution.py:352
  50.7 0.0 copy-start.1
  50.7 0.1 add_convert_fusion
  50.8 0.0 copy-start
  50.8 2.0 %collective-permute-start.5 = (bf16[128,2048]{1,0:T(8,128)(2,1)S(1)}, bf16[128,2048]{1,0:T(8,128)(2,1)S(1)}, u32[]{:S(2)}, u32[]{:S(2)}) collective-permute-start(bf16[128,2048]{1,0:T(8,128)(2,1)S(1)} %add_convert_fusion), channel_id=1, source_target_pairs={{0,16},{8,24},{16,0},{24,8},{1,17},{9,25},{17,1},{25,9},{2,18},{10... | collective-permute-start | bytes 1572872 | tf_op jit(solution)/shard_map/projection_sum/ppermute | solution.py:353
  52.9 0.0 collective-permute-done.3.refs_5_
  52.9 12.4 %collective-permute-done.5.refs_6_ = bf16[128,2048]{1,0:T(8,128)(2,1)S(1)} collective-permute-done((bf16[128,2048]{1,0:T(8,128)(2,1)S(1)}, bf16[128,2048]{1,0:T(8,128)(2,1)S(1)}, u32[]{:S(2)}, u32[]{:S(2)}) %collective-permute-start.5) | collective-permute-done | bytes 524320 | tf_op jit(solution)/shard_map/projection_sum/ppermute | solution.py:353
  65.3 0.0 copy-done.5
  65.3 0.0 copy-done.10
  65.3 0.0 copy-done.12
  65.3 0.0 copy-done.13
  65.3 1.0 dispatch.1
  66.3 22.3 %all_to_all.10.rows_ref = bf16[32,64,128]{2,1,0:T(8,128)(2,1)S(1)} all-to-all(bf16[32,64,128]{2,1,0:T(8,128)(2,1)S(1)} %get-tuple-element.26), channel_id=1, replica_groups=mesh['ctx'=4,'exp'=8] {'ctx','exp'}, dimensions={0} | all-to-all | bytes 1048576 | tf_op jit(solution)/shard_map/to_experts/all_to_all | solution.py:373
  88.5 0.0 copy-done.1
  88.6 0.0 copy-done
  88.6 0.0 copy-start.11
  88.6 0.0 copy-start.15
  88.6 3.2 %experts.1 = bf16[32,64,128]{2,1,0:T(8,128)(2,1)S(1)} custom-call(bf16[32,64,128]{2,1,0:T(8,128)(2,1)S(1)} %all_to_all.10.rows_ref, bf16[1,2048,512]{2,1,0:T(8,128)(2,1)S(1)} %copy-done, bf16[1,2048,512]{2,1,0:T(8,128)(2,1)S(1)} %copy-done.1, bf16[1,512,2048]{2,1,0:T(8,128)(2,1)} %down_ref.1), custom_call_target="tpu_custom_call" | custom-call | tf_op jit(solution)/shard_map/experts/pallas_call | solution.py:375
  91.8 18.4 %all_to_all.11.back_ref = bf16[32,64,128]{2,1,0:T(8,128)(2,1)S(1)} all-to-all(bf16[32,64,128]{2,1,0:T(8,128)(2,1)S(1)} %experts.1), channel_id=1, replica_groups=mesh['ctx'=4,'exp'=8] {'ctx','exp'}, dimensions={0} | all-to-all | bytes 1048576 | tf_op jit(solution)/shard_map/from_experts/all_to_all | solution.py:382
  110.2 0.0 copy-done.11
  110.2 0.0 copy-done.15
  110.2 1.7 %combine.1 = bf16[1,128,2048]{2,1,0:T(8,128)(2,1)} custom-call(f32[128,2048]{1,0:T(8,128)S(1)} %get-tuple-element.24.hidden_ref, f32[128,128]{1,0:T(8,128)S(1)} %get-tuple-element.25.table_ref, bf16[32,64,128]{2,1,0:T(8,128)(2,1)S(1)} %all_to_all.11.back_ref, s32[1,128]{1,0:T(1,128)S(1)} %copy-done.15, f32[1,2048]{1,0:T(1,128)S(1)} %bitcast.10), custom_call_target="tpu_custom_call" | custom-call | tf_op jit(solution)/shard_map/combine/pallas_call | solution.py:384
Async XLA Ops:
  0.0 1.0 copy-start.3
  1.0 1.0 copy-start.4
  2.1 0.9 copy-start.6
  3.0 0.9 copy-start.7
  4.0 0.7 copy-start.8
  4.7 0.7 copy-start.9
  5.6 11.9 %collective-permute-start = (bf16[128,1664]{1,0:T(8,128)(2,1)S(1)}, bf16[128,1664]{1,0:T(8,128)(2,1)S(1)}, u32[]{:S(2)}, u32[]{:S(2)}) collective-permute-start(bf16[128,1664]{1,0:T(8,128)(2,1)S(1)} %get-tuple-element.17), channel_id=1, source_target_pairs={{0,8},{8,16},{16,24},{24,0},{1,9},{9,17},{17,25},{25,1},{2,10},{10... | collective-permute-start | bytes 1277960 | tf_op jit(solution)/shard_map/heads_exchange/ppermute | solution.py:328
  6.1 13.2 %collective-permute-start.1 = (bf16[128,1664]{1,0:T(8,128)(2,1)S(1)}, bf16[128,1664]{1,0:T(8,128)(2,1)S(1)}, u32[]{:S(2)}, u32[]{:S(2)}) collective-permute-start(bf16[128,1664]{1,0:T(8,128)(2,1)S(1)} %get-tuple-element.18), channel_id=1, source_target_pairs={{0,16},{8,24},{16,0},{24,8},{1,17},{9,25},{17,1},{25,9},{2,18},{10... | collective-permute-start | bytes 1277960 | tf_op jit(solution)/shard_map/heads_exchange/ppermute | solution.py:328
  8.6 18.7 %collective-permute-start.2 = (bf16[128,1664]{1,0:T(8,128)(2,1)S(1)}, bf16[128,1664]{1,0:T(8,128)(2,1)S(1)}, u32[]{:S(2)}, u32[]{:S(2)}) collective-permute-start(bf16[128,1664]{1,0:T(8,128)(2,1)S(1)} %get-tuple-element.19), channel_id=1, source_target_pairs={{0,24},{8,0},{16,8},{24,16},{1,25},{9,1},{17,9},{25,17},{2,26},{10... | collective-permute-start | bytes 1277960 | tf_op jit(solution)/shard_map/heads_exchange/ppermute | solution.py:328
  27.3 1.6 %copy-start.2 = (bf16[512,2048]{1,0:T(8,128)(2,1)S(1)}, bf16[512,2048]{1,0:T(8,128)(2,1)}, u32[]{:S(2)}) copy-start(bf16[512,2048]{1,0:T(8,128)(2,1)} %refs_5_.1) | copy-start | bytes 6291460
  28.9 0.7 copy-start.14
  29.6 35.7 %copy-start.5 = (bf16[1,128,2048]{2,1,0:T(8,128)(2,1)S(1)}, bf16[1,128,2048]{2,1,0:T(8,128)(2,1)}, u32[]{:S(2)}) copy-start(bf16[1,128,2048]{2,1,0:T(8,128)(2,1)} %refs_0_.1) | copy-start | bytes 1572868
  29.6 35.7 %copy-start.10 = (f32[2048]{0:T(1024)S(1)}, f32[2048]{0:T(1024)}, u32[]{:S(2)}) copy-start(f32[2048]{0:T(1024)} %param.26) | copy-start | bytes 24580
  29.6 35.7 %copy-start.12 = (s32[1,128,10]{1,0,2:T(1,128)S(1)}, s32[1,128,10]{1,0,2:T(1,128)}, u32[]{:S(2)}) copy-start(s32[1,128,10]{1,0,2:T(1,128)} %param.27) | copy-start | bytes 15364
  29.6 35.7 %copy-start.13 = (f32[1,128,10]{1,0,2:T(1,128)S(1)}, f32[1,128,10]{1,0,2:T(1,128)}, u32[]{:S(2)}) copy-start(f32[1,128,10]{1,0,2:T(1,128)} %param.28) | copy-start | bytes 15364
  48.7 2.0 %collective-permute-start.4 = (bf16[128,2048]{1,0:T(8,128)(2,1)S(1)}, bf16[128,2048]{1,0:T(8,128)(2,1)S(1)}, u32[]{:S(2)}, u32[]{:S(2)}) collective-permute-start(bf16[128,2048]{1,0:T(8,128)(2,1)S(1)} %get-tuple-element.23), channel_id=1, source_target_pairs={{0,8},{8,0},{16,24},{24,16},{1,9},{9,1},{17,25},{25,17},{2,10},{10... | collective-permute-start | bytes 1572872 | tf_op jit(solution)/shard_map/projection_sum/ppermute | solution.py:352
  48.8 4.1 %collective-permute-start.3 = (bf16[128,2048]{1,0:T(8,128)(2,1)S(1)}, bf16[128,2048]{1,0:T(8,128)(2,1)S(1)}, u32[]{:S(2)}, u32[]{:S(2)}) collective-permute-start(bf16[128,2048]{1,0:T(8,128)(2,1)S(1)} %get-tuple-element.21), channel_id=1, source_target_pairs={{0,8},{8,0},{16,24},{24,16},{1,9},{9,1},{17,25},{25,17},{2,10},{10... | collective-permute-start | bytes 1572872 | tf_op jit(solution)/shard_map/projection_sum/ppermute | solution.py:354
  50.7 37.9 %copy-start.1 = (bf16[1,2048,512]{2,1,0:T(8,128)(2,1)S(1)}, bf16[1,2048,512]{2,1,0:T(8,128)(2,1)}, u32[]{:S(2)}) copy-start(bf16[1,2048,512]{2,1,0:T(8,128)(2,1)} %up_ref.1) | copy-start | bytes 6291460
  50.8 37.7 %copy-start = (bf16[1,2048,512]{2,1,0:T(8,128)(2,1)S(1)}, bf16[1,2048,512]{2,1,0:T(8,128)(2,1)}, u32[]{:S(2)}) copy-start(bf16[1,2048,512]{2,1,0:T(8,128)(2,1)} %gate_ref.1) | copy-start | bytes 6291460
  50.8 14.5 %collective-permute-start.5 = (bf16[128,2048]{1,0:T(8,128)(2,1)S(1)}, bf16[128,2048]{1,0:T(8,128)(2,1)S(1)}, u32[]{:S(2)}, u32[]{:S(2)}) collective-permute-start(bf16[128,2048]{1,0:T(8,128)(2,1)S(1)} %add_convert_fusion), channel_id=1, source_target_pairs={{0,16},{8,24},{16,0},{24,8},{1,17},{9,25},{17,1},{25,9},{2,18},{10... | collective-permute-start | bytes 1572872 | tf_op jit(solution)/shard_map/projection_sum/ppermute | solution.py:353
  88.6 21.7 %copy-start.11 = (f32[2048]{0:T(1024)S(1)}, f32[2048]{0:T(1024)}, u32[]{:S(2)}) copy-start(f32[2048]{0:T(1024)} %param.33) | copy-start | bytes 24580
  88.6 21.7 %copy-start.15 = (s32[1,128]{1,0:T(1,128)S(1)}, s32[1,128]{1,0:T(1,128)}, u32[]{:S(2)}) copy-start(s32[1,128]{1,0:T(1,128)} %mask_ref.1) | copy-start | bytes 1540
where the time goes:
time: 112 us
  blocking collectives  40.7 us (36%)
  waiting for transfers between devices  31.1 us (28%)
  Pallas kernels  25.2 us (22%)
  local copies, waits for them, and re-layouts  7.65 us (7%)
  starting transfers between devices  7.04 us (6%)
    all_to_all x1, blocking collectives, local_part(): came = lax.all_to_all(rows, ('ctx', 'exp'), 0, 0, tiled=True)  22.3 us
    pallas_call x1, Pallas kernels, local_part(): pl.pallas_call(functools.partial(mixer_kernel, n, heads, kw, vw), in_spec...  19.1 us
    all_to_all x1, blocking collectives, local_part(): back = lax.all_to_all(done, ('ctx', 'exp'), 0, 0, tiled=True)  18.4 us
    ppermute x3, waiting for transfers between devices, local_part(): lax.ppermute(packed[s], 'ctx', [(i, (i + s) % n) for i in range(n)])  17.3 us
    ppermute x1, waiting for transfers between devices, local_part(): lax.ppermute(pair.astype(bf16), 'ctx', [(i, (i + 2 * j) % n) for i in ran...  12.4 us
    unnamed x32, local copies, waits for them, and re-layouts  7.65 us
    ppermute x3, starting transfers between devices, local_part(): lax.ppermute(packed[s], 'ctx', [(i, (i + s) % n) for i in range(n)])  4.46 us
    pallas_call x1, Pallas kernels, local_part(): pl.pallas_call(expert_kernel, out_shape=shape((devices, CAP * chunks, LAN...  3.23 us
  transfers between devices with their start and end apart: 6, of which 5 were waited for; matrix products, arithmetic and copies ran while one was open for 0% of the time, Pallas kernels for 0%

commit v1 on v0

--- a/solution.py
+++ b/solution.py
@@ -49,90 +49,92 @@
     return lax.broadcasted_iota(jnp.int32, shape, dim)
 
 
+def in_hbm(*arrays):
+    return [pltpu.with_memory_space_constraint(a, pltpu.HBM) for a in arrays]
+
+
 def compiler_params(mib):
     return pltpu.CompilerParams(vmem_limit_bytes=mib * 1024 * 1024)
 
 
-def pack_kernel(n, kw, vw, k_ref, q_ref, v_ref, g_ref, w_ref, d_ref, *outs):
+def pack_kernel(n, kw, vw, k_ref, q_ref, v_ref, g_ref, w_ref, d_ref, *refs):
+    keyed, asked, gated = refs[:n], refs[n : 2 * n], refs[2 * n : 3 * n]
+    w_in, d_in, small_sems, sems = refs[3 * n :]
     me = lax.axis_index("ctx")
     tokens = k_ref.shape[1]
     heads = d_ref.shape[1]
-    ones = (iota((tokens, tokens), 0) <= iota((tokens, tokens), 1)).astype(bf16)
-    logs = jnp.log(d_ref[0])
-    sums = sum(mm(piece, ones) for piece in reversed(split3(logs)))
-    pieces = [*split3(sums), *split3(w_ref[0])]
-    aux = jnp.concatenate([p.astype(f32) for p in pieces], axis=0)
-    aux = jnp.concatenate([aux, jnp.zeros((LANES - 6 * heads, tokens), f32)], axis=0).astype(bf16)
-    for step, out in enumerate(outs):
+    small = [
+        pltpu.make_async_copy(d_ref.at[0], d_in, small_sems.at[0]),
+        pltpu.make_async_copy(w_ref.at[0], w_in, small_sems.at[1]),
+    ]
+    for copy in small:
+        copy.start()
+    copies = []
+    for step in range(n):
         to = lax.rem(me + step, n)
         kat = pl.ds(pl.multiple_of(to * kw, LANES), kw)
         vat = pl.ds(pl.multiple_of(to * vw, LANES), vw)
-        out[:, 0:kw] = k_ref[0, :, kat]
-        out[:, kw : 2 * kw] = q_ref[0, :, kat]
-        out[:, 2 * kw : 2 * kw + vw] = v_ref[0, :, vat]
-        out[:, 2 * kw + vw : 2 * kw + 2 * vw] = g_ref[0, :, vat]
-        out[:, 2 * kw + 2 * vw :] = aux
-
-
-def mixer_kernel(n, heads, kw, vw, *refs):
-    pieces = refs[:n]
-    gain_ref, proj_ref = refs[n : n + 2]
-    keeps = refs[n + 2 : n + 2 + n // 2]
-    gives = refs[n + 2 + n // 2 : n + 2 + n]
-    x_ref, inv_ref, score_ref, state_ref, mixed_ref, sems = refs[n + 2 + n :]
-    me = lax.axis_index("ctx")
-    tokens = pieces[0].shape[0]
-    local = vw // DK
-    group = vw // kw
-    copies = []
+        for i, (source, target) in enumerate(
+            (
+                (k_ref.at[0, :, kat], keyed[step].at[:, 0:kw]),
+                (q_ref.at[0, :, kat], asked[step].at[:, 0:kw]),
+                (v_ref.at[0, :, vat], asked[step].at[:, kw : kw + vw]),
+                (g_ref.at[0, :, vat], gated[step]),
+            )
+        ):
+            copy = pltpu.make_async_copy(source, target, sems.at[step, i])
+            copy.start()
+            copies.append(copy)
+    for copy in small:
+        copy.wait()
+    ones = (iota((tokens, tokens), 0) <= iota((tokens, tokens), 1)).astype(bf16)
+    logs = jnp.log(d_in[...])
+    sums = sum(mm(piece, ones) for piece in reversed(split3(logs)))
+    pieces = [*split3(sums), *split3(w_in[...])]
+    aux = jnp.concatenate([p.astype(f32) for p in pieces], axis=0)
+    aux = jnp.concatenate([aux, jnp.zeros((LANES - 6 * heads, tokens), f32)], axis=0).astype(bf16)
     for step in range(n):
-        came = lax.rem(me - step + n, n)
-        copy = pltpu.make_async_copy(pieces[step], x_ref.at[came], sems.at[step])
-        copy.start()
-        copies.append(copy)
+        keyed[step][:, kw:] = aux
     for copy in copies:
         copy.wait()
 
+
+def head_rates(heads, local, me, aux):
+    r, l = iota((LANES, LANES), 0), iota((LANES, LANES), 1)
+    wanted = me * local + lax.rem(l, local)
+    pick = ((lax.rem(r, heads) == wanted) & (l < 2 * local) & (r // heads // 3 == l // local)).astype(bf16)
+    return mm_tn(aux, pick), mm_tn(pick, aux)
+
+
+def inverse_scale(raw):
+    raw_f = raw.astype(f32)
+    return lax.rsqrt(jnp.sum(raw_f * raw_f, axis=1, keepdims=True) + EPS)
+
+
+def inverse_kernel(n, heads, kw, local, *refs):
+    keyed, inv_ref = refs[:n], refs[n]
+    me = lax.axis_index("ctx")
+    tokens = keyed[0].shape[0]
+    group = local * DK // kw
     row, col = iota((tokens, tokens), 0), iota((tokens, tokens), 1)
     apart = lax.bitwise_xor(row, col)
     eye = (row == col).astype(f32)
-    r, l = iota((LANES, LANES), 0), iota((LANES, LANES), 1)
-    kind = r // heads
-    wanted = me * local + lax.rem(l, local)
-    pick = (
-        (lax.rem(r, heads) == wanted)
-        & (l < 2 * local)
-        & (kind // 3 == l // local)
-    ).astype(bf16)
-
-    def rates(block):
-        aux = x_ref[block, :, 2 * kw + 2 * vw :]
-        return mm_tn(aux, pick), mm_tn(pick, aux)
-
-    def unit_scales(raw):
-        raw_f = raw.astype(f32)
-        return lax.rsqrt(jnp.sum(raw_f * raw_f, axis=1, keepdims=True) + EPS)
-
-    def prepare(block, carry):
-        as_cols, as_rows = rates(block)
-        systems, all_scores = [], []
+    for step in range(n):
+        block = lax.rem(me - step + n, n)
+        as_cols, as_rows = head_rates(heads, local, me, keyed[step][:, kw:])
+        systems = []
         for g in range(local // group):
-            k = x_ref[block, :, g * DK : (g + 1) * DK]
-            q = x_ref[block, :, kw + g * DK : kw + (g + 1) * DK]
+            k = keyed[step][:, g * DK : (g + 1) * DK]
             dots = mm_nt(k, k)
-            scores = mm_nt(q, k)
             diag = dots * eye
             k_row = lax.rsqrt(jnp.sum(diag, axis=0, keepdims=True) + EPS)
             k_col = lax.rsqrt(jnp.sum(diag, axis=1, keepdims=True) + EPS)
-            q_col = unit_scales(q) * DK ** (-0.5)
             dots = dots * k_row * k_col
-            scores = scores * k_row * q_col
             for h in range(g * group, (g + 1) * group):
                 gap = as_cols[:, h : h + 1] - as_rows[h : h + 1, :]
                 ratios = jnp.exp(jnp.minimum(gap, 0.0))
                 write = as_cols[:, local + h : local + h + 1]
                 systems.append(jnp.where(row > col, write * ratios * dots, 0.0))
-                all_scores.append(jnp.where(row >= col, ratios * scores, 0.0))
         near = [jnp.where(apart < 16, s, 0.0) for s in systems]
         inverse = [eye - s for s in near]
         power = [split2(s) for s in near]
@@ -150,59 +152,94 @@
             hi, lo = split2(inverse[h])
             inv_ref[block, h, 0] = hi
             inv_ref[block, h, 1] = lo
-            score_ref[block, h] = all_scores[h]
-        return carry
-
-    lax.fori_loop(0, n, prepare, 0)
-    state_ref[...] = jnp.zeros_like(state_ref)
+
+
+def state_kernel(n, heads, kw, vw, *refs):
+    keyed, asked = refs[:n], refs[n : 2 * n]
+    inv_ref, gain_ref, out_ref, kx_ref, qv_ref = refs[2 * n :]
+    me = lax.axis_index("ctx")
+    tokens = keyed[0].shape[0]
+    local = vw // DK
+    group = vw // kw
+    for step in range(n):
+        block = lax.rem(me - step + n, n)
+        kx_ref[block] = keyed[step][...]
+        qv_ref[block] = asked[step][...]
+    row, col = iota((tokens, tokens), 0), iota((tokens, tokens), 1)
     gain = gain_ref[...]
-
-    def advance(block, carry):
-        as_cols, as_rows = rates(block)
+    states = [jnp.zeros((DK, DK), f32) for _ in range(local)]
+    for block in range(n):
+        as_cols, as_rows = head_rates(heads, local, me, kx_ref[block, :, kw:])
         cumulative = jnp.exp(as_cols)
-        rows_at = pl.ds(pl.multiple_of(block * tokens, tokens), tokens)
         for g in range(local // group):
-            k = x_ref[block, :, g * DK : (g + 1) * DK]
-            q = x_ref[block, :, kw + g * DK : kw + (g + 1) * DK]
-            k_col = unit_scales(k)
-            q_col = unit_scales(q) * DK ** (-0.5)
+            k = kx_ref[block, :, g * DK : (g + 1) * DK]
+            q = qv_ref[block, :, g * DK : (g + 1) * DK]
+            k_col = inverse_scale(k)
+            q_col = inverse_scale(q) * DK ** (-0.5)
+            eye = (row == col).astype(f32)
+            k_row = jnp.sum(eye * k_col, axis=0, keepdims=True)
+            dots = mm_nt(q, k) * k_row * q_col
             both = jnp.concatenate([k, q], axis=0)
             for h in range(g * group, (g + 1) * group):
-                state = state_ref[h]
-                high, low = split2(state)
-                seen = mm(jnp.concatenate([both, both], axis=1), jnp.concatenate([high, low], axis=0))
-                v = x_ref[block, :, 2 * kw + h * DK : 2 * kw + (h + 1) * DK].astype(f32)
+                gap = as_cols[:, h : h + 1] - as_rows[h : h + 1, :]
+                scores = jnp.where(row >= col, jnp.exp(jnp.minimum(gap, 0.0)) * dots, 0.0)
+                v = qv_ref[block, :, kw + h * DK : kw + (h + 1) * DK].astype(f32)
                 cum = cumulative[:, h : h + 1]
                 write = as_cols[:, local + h : local + h + 1]
-                rhs = write * (v - (cum * k_col) * seen[:tokens])
+                rhs = write * v
+                if block > 0:
+                    high, low = split2(states[h])
+                    seen = mm(jnp.concatenate([both, both], axis=1), jnp.concatenate([high, low], axis=0))
+                    rhs = rhs - (write * cum * k_col) * seen[:tokens]
                 delta = mm3((inv_ref[block, h, 0], inv_ref[block, h, 1]), split2(rhs))
-                out = (cum * q_col) * seen[tokens:] + mm3(split2(score_ref[block, h]), split2(delta))
-                last = as_cols[tokens - 1 : tokens, h : h + 1]
-                kept = jnp.exp(last - as_cols[:, h : h + 1]) * k_col
-                dh, dl = split2(kept * delta)
-                state_ref[h] = jnp.exp(last) * state + mm_tn(
-                    jnp.concatenate([k, k], axis=0), jnp.concatenate([dh, dl], axis=0)
-                )
-                gate = x_ref[
-                    block, :, 2 * kw + vw + h * DK : 2 * kw + vw + (h + 1) * DK
-                ].astype(f32)
+                if block < n - 1:
+                    last = as_cols[tokens - 1 : tokens, h : h + 1]
+                    kept = jnp.exp(last - as_cols[:, h : h + 1]) * k_col
+                    dh, dl = split2(kept * delta)
+                    states[h] = jnp.exp(last) * states[h] + mm_tn(
+                        jnp.concatenate([k, k], axis=0), jnp.concatenate([dh, dl], axis=0)
+                    )
+                out = mm3(split2(scores), split2(delta))
+                if block > 0:
+                    out = out + (cum * q_col) * seen[tokens:]
                 mean = jnp.mean(out * out, axis=1, keepdims=True)
-                normed = out * lax.rsqrt(mean + EPS) * gain * (gate / (1.0 + jnp.exp(-gate)))
-                mixed_ref[rows_at, h * DK : (h + 1) * DK] = normed.astype(bf16)
-        return carry
-
-    lax.fori_loop(0, n, advance, 0)
-
+                out_ref[block, :, h * DK : (h + 1) * DK] = out * lax.rsqrt(mean + EPS) * gain
+
+
+def gate_kernel(n, *refs):
+    gated = refs[:n]
+    normed_ref, proj_hbm, mixed_ref = refs[n : n + 3]
+    chips = n // 2
+    keeps = refs[n + 3 : n + 2 + chips]
+    gives = refs[n + 2 + chips : n + 1 + 2 * chips]
+    proj_ref, sem = refs[n + 1 + 2 * chips :]
+    copy = pltpu.make_async_copy(proj_hbm, proj_ref, sem)
+    copy.start()
+    me = lax.axis_index("ctx")
+    for step in range(n):
+        block = lax.rem(me - step + n, n)
+        gate = gated[step][...].astype(f32)
+        mixed_ref[block] = (normed_ref[block] * (gate / (1.0 + jnp.exp(-gate)))).astype(bf16)
+    copy.wait()
     core = lax.rem(me, 2)
-    for j in range(n // 2):
-        chip = lax.rem(me // 2 + j, n // 2)
-        for refs_out, half in ((gives, 1 - core), (keeps, core)):
-            at = pl.multiple_of((chip * 2 + half) * tokens, tokens)
-            mine = mixed_ref[pl.ds(at, tokens), :]
-            width = 512
-            for c in range(0, proj_ref.shape[1], width):
-                part = mm(mine, proj_ref[:, c : c + width])
-                refs_out[j][:, c : c + width] = part.astype(refs_out[j].dtype)
+    for j in range(1, chips):
+        chip = lax.rem(me // 2 + j, chips)
+        project(mixed_ref, chip * 2 + 1 - core, proj_ref, gives[j - 1])
+        project(mixed_ref, chip * 2 + core, proj_ref, keeps[j - 1])
+
+
+def project(mixed_ref, block, proj_ref, out_ref):
+    mine = mixed_ref[block]
+    width = 512
+    for c in range(0, proj_ref.shape[1], width):
+        out_ref[:, c : c + width] = mm(mine, proj_ref[:, c : c + width]).astype(out_ref.dtype)
+
+
+def own_kernel(n, mixed_ref, proj_ref, keep_ref, give_ref):
+    me = lax.axis_index("ctx")
+    other = lax.bitwise_xor(me, 1)
+    project(mixed_ref, other, proj_ref, give_ref)
+    project(mixed_ref, me, proj_ref, keep_ref)
 
 
 def dispatch_kernel(parts, *refs):
@@ -311,47 +348,82 @@
     heads = write_rate.shape[2]
     width = residual.shape[2]
     kw, vw = keys.shape[2] // n, values.shape[2] // n
-    payload = 2 * kw + 2 * vw + LANES
     chips = n // 2
     slots = devices * CAP
     chunks = width // LANES
     shape = jax.ShapeDtypeStruct
 
+    hbm = pl.BlockSpec(memory_space=pltpu.HBM)
+    vmem = pl.BlockSpec(memory_space=pltpu.VMEM)
+    local = vw // DK
     with jax.named_scope("pack"):
         packed = pl.pallas_call(
             functools.partial(pack_kernel, n, kw, vw),
-            out_shape=[shape((tokens, payload), bf16)] * n,
+            in_specs=[hbm] * 6,
+            out_shape=[shape((tokens, kw + LANES), bf16)] * n
+            + [shape((tokens, kw + vw), bf16)] * n
+            + [shape((tokens, vw), bf16)] * n,
+            scratch_shapes=[
+                pltpu.VMEM((heads, tokens), f32),
+                pltpu.VMEM((heads, tokens), f32),
+                pltpu.SemaphoreType.DMA((2,)),
+                pltpu.SemaphoreType.DMA((n, 4)),
+            ],
             compiler_params=compiler_params(16),
-        )(keys, queries, values, out_gate, write_rate.transpose(0, 2, 1), decay.transpose(0, 2, 1))
+        )(*in_hbm(keys, queries, values, out_gate, write_rate.transpose(0, 2, 1), decay.transpose(0, 2, 1)))
     with jax.named_scope("heads_exchange"):
-        arrived = [packed[0]] + [
-            lax.ppermute(packed[s], "ctx", [(i, (i + s) % n) for i in range(n)]) for s in range(1, n)
-        ]
-    with jax.named_scope("mixer"):
-        vmem = pl.BlockSpec(memory_space=pltpu.VMEM)
-        local = vw // DK
+        far_first = sorted(range(1, n), key=lambda s: (s == 1, s))
+        came = {0: packed[:n][0], n: packed[n], 2 * n: packed[2 * n]}
+        for first in (0, n, 2 * n):
+            for s in far_first:
+                route = [(i, (i + s) % n) for i in range(n)]
+                came[first + s] = lax.ppermute(packed[first + s], "ctx", route)
+        keyed = [came[s] for s in range(n)]
+        asked = [came[n + s] for s in range(n)]
+        gated = [came[2 * n + s] for s in range(n)]
+    with jax.named_scope("block_inverses"):
+        inverses = pl.pallas_call(
+            functools.partial(inverse_kernel, n, heads, kw, local),
+            out_shape=shape((n, local, 2, tokens, tokens), bf16),
+            compiler_params=compiler_params(16),
+            cost_estimate=pl.CostEstimate(flops=8 * 10**9, bytes_accessed=10**6, transcendentals=0),
+        )(*keyed)
+    with jax.named_scope("states"):
+        normed = pl.pallas_call(
+            functools.partial(state_kernel, n, heads, kw, vw),
+            out_shape=shape((n, tokens, vw), f32),
+            scratch_shapes=[
+                pltpu.VMEM((n, tokens, kw + LANES), bf16),
+                pltpu.VMEM((n, tokens, kw + vw), bf16),
+            ],
+            compiler_params=compiler_params(24),
+            cost_estimate=pl.CostEstimate(flops=4 * 10**9, bytes_accessed=10**6, transcendentals=0),
+        )(*keyed, *asked, inverses, head_gain.reshape(1, -1))
+    with jax.named_scope("gates"):
         outs = pl.pallas_call(
-            functools.partial(mixer_kernel, n, heads, kw, vw),
-            in_specs=[pl.BlockSpec(memory_space=pl.ANY)] * n + [vmem] * 2,
-            out_shape=[shape((tokens, width), f32)] * chips + [shape((tokens, width), bf16)] * chips,
-            scratch_shapes=[
-                pltpu.VMEM((n, tokens, payload), bf16),
-                pltpu.VMEM((n, local, 2, tokens, tokens), bf16),
-                pltpu.VMEM((n, local, tokens, tokens), f32),
-                pltpu.VMEM((local, DK, DK), f32),
-                pltpu.VMEM((n * tokens, vw), bf16),
-                pltpu.SemaphoreType.DMA((n,)),
-            ],
-            compiler_params=compiler_params(40),
-        )(*arrived, head_gain.reshape(1, -1), out_proj)
-    keeps, gives = outs[:chips], outs[chips:]
+            functools.partial(gate_kernel, n),
+            in_specs=[vmem] * (n + 1) + [hbm],
+            out_shape=[shape((n, tokens, vw), bf16)]
+            + [shape((tokens, width), f32)] * (chips - 1)
+            + [shape((tokens, width), bf16)] * (chips - 1),
+            scratch_shapes=[pltpu.VMEM(out_proj.shape, bf16), pltpu.SemaphoreType.DMA],
+            compiler_params=compiler_params(24),
+        )(*gated, normed, *in_hbm(out_proj))
+    mixed, keeps, gives = outs[0], outs[1:chips], outs[chips:]
+    with jax.named_scope("own_projection"):
+        keep, give = pl.pallas_call(
+            functools.partial(own_kernel, n),
+            out_shape=[shape((tokens, width), f32), shape((tokens, width), bf16)],
+            compiler_params=compiler_params(24),
+            cost_estimate=pl.CostEstimate(flops=2 * 10**9, bytes_accessed=10**6, transcendentals=0),
+        )(mixed, out_proj)
     with jax.named_scope("projection_sum"):
         sibling = [(i, i ^ 1) for i in range(n)]
         parts = []
         for j in range(chips - 1, 0, -1):
-            pair = keeps[j] + lax.ppermute(gives[j], "ctx", sibling).astype(f32)
+            pair = keeps[j - 1] + lax.ppermute(gives[j - 1], "ctx", sibling).astype(f32)
             parts.append(lax.ppermute(pair.astype(bf16), "ctx", [(i, (i + 2 * j) % n) for i in range(n)]))
-        parts = [keeps[0], lax.ppermute(gives[0], "ctx", sibling)] + parts
+        parts = [keep, lax.ppermute(give, "ctx", sibling)] + parts
     with jax.named_scope("dispatch"):
         hidden, rows, table = pl.pallas_call(
             functools.partial(dispatch_kernel, len(parts)),

time: 112 us -> 94.6 us (0.84)
  waiting for transfers between devices: 31.1 us -> 13.5 us
  local copies, waits for them, and re-layouts: 7.65 us -> 0.05 us
  starting transfers between devices: 7.04 us -> 14.1 us
    ppermute x5 -> x11, waiting for transfers between devices: 18.7 us -> 1.07 us  [the longest x1 0.67 us: local_part(): pair = keeps[j - 1] + lax.ppermute(gives[j - 1], 'ctx', sibling).astype(f32)]
    unnamed x32 -> x20, local copies, waits for them, and re-layouts: 7.65 us -> 0.05 us
    ppermute x5 -> x11, starting transfers between devices: 5.03 us -> 11.8 us  [the longest x9 10.7 us: local_part(): came[first + s] = lax.ppermute(packed[first + s], 'ctx', route)]
    pallas_call x2 -> x5, Pallas kernels: 19.3 us -> 19.8 us  [the longest x1 8.39 us: local_part(): pl.pallas_call(functools.partial(inverse_kernel, n, heads, kw, local), ou...]
  transfers between devices with their start and end apart: 6 -> 12, of which waited for: 5 -> 3; matrix products, arithmetic and copies ran while one was open for 0% -> 0% of each run, Pallas kernels for 0% -> 17%
where the time goes in v1:
time: 94.6 us; the launch traced here: 94.4 us
  blocking collectives  40.7 us (43%)
  Pallas kernels  25.7 us (27%)
  starting transfers between devices  14.1 us (15%)
  waiting for transfers between devices  13.5 us (14%)
    all_to_all x1, blocking collectives, local_part(): came = lax.all_to_all(rows, ('ctx', 'exp'), 0, 0, tiled=True)  22.3 us
    all_to_all x1, blocking collectives, local_part(): back = lax.all_to_all(done, ('ctx', 'exp'), 0, 0, tiled=True)  18.4 us
    ppermute x1, waiting for transfers between devices, local_part(): lax.ppermute(pair.astype(bf16), 'ctx', [(i, (i + 2 * j) % n) for i in ran...  12.4 us
    ppermute x9, starting transfers between devices, local_part(): came[first + s] = lax.ppermute(packed[first + s], 'ctx', route)  10.7 us
    pallas_call x1, Pallas kernels, local_part(): pl.pallas_call(functools.partial(inverse_kernel, n, heads, kw, local), ou...  8.39 us
    pallas_call x1, Pallas kernels, local_part(): pl.pallas_call(functools.partial(state_kernel, n, heads, kw, vw), out_sha...  6.49 us
    pallas_call x1, Pallas kernels, local_part(): pl.pallas_call(expert_kernel, out_shape=shape((devices, CAP * chunks, LAN...  3.23 us
    pallas_call x1, Pallas kernels, local_part(): pl.pallas_call(functools.partial(gate_kernel, n), in_specs=[vmem] * (n +...  2.59 us
  transfers between devices with their start and end apart: 12, of which 3 were waited for; matrix products, arithmetic and copies ran while one was open for 0% of the time, Pallas kernels for 17%

profile of v1, /device:TPU:0, one launch (start us, length us, event | category | flops | bytes accessed | tf_op | source)
XLA Modules:
  0.0 94.4 jit_solution(17788136883969852890)
XLA Ops:
  0.0 1.6 %pack.1 = (bf16[128,384]{1,0:T(8,128)(2,1)S(1)}, bf16[128,384]{1,0:T(8,128)(2,1)S(1)}, bf16[128,384]{1,0:T(8,128)(2,1)S(1)}, bf16[128,384]{1,0:T(8,128)(2,1)S(1)...) custom-call(bf16[1,128,1024]{2,1,0:T(8,128)(2,1)} %k_ref.1, ...), custom_call_target="tpu_custom_call" | custom-call | tf_op jit(solution)/shard_map/pack/pallas_call | solution.py:360
  1.6 0.5 collective-permute-start.3
  2.1 2.6 %collective-permute-start.4 = (bf16[128,384]{1,0:T(8,128)(2,1)S(1)}, bf16[128,384]{1,0:T(8,128)(2,1)S(1)}, u32[]{:S(2)}, u32[]{:S(2)}) collective-permute-start(bf16[128,384]{1,0:T(8,128)(2,1)S(1)} %get-tuple-element.31), channel_id=1, source_target_pairs={{0,16},{8,24},{16,0},{24,8},{1,17},{9,25},{17,1},{25,9},{2,18},{10... | collective-permute-start | bytes 294920 | tf_op jit(solution)/shard_map/heads_exchange/ppermute | solution.py:380
  4.7 1.4 %collective-permute-start.5 = (bf16[128,384]{1,0:T(8,128)(2,1)S(1)}, bf16[128,384]{1,0:T(8,128)(2,1)S(1)}, u32[]{:S(2)}, u32[]{:S(2)}) collective-permute-start(bf16[128,384]{1,0:T(8,128)(2,1)S(1)} %get-tuple-element.32), channel_id=1, source_target_pairs={{0,24},{8,0},{16,8},{24,16},{1,25},{9,1},{17,9},{25,17},{2,26},{10... | collective-permute-start | bytes 294920 | tf_op jit(solution)/shard_map/heads_exchange/ppermute | solution.py:380
  6.1 0.0 collective-permute-start
  6.1 0.4 collective-permute-start.1
  6.5 0.0 collective-permute-done.3.refs_1_
  6.5 1.5 %collective-permute-start.6 = (bf16[128,768]{1,0:T(8,128)(2,1)S(1)}, bf16[128,768]{1,0:T(8,128)(2,1)S(1)}, u32[]{:S(2)}, u32[]{:S(2)}) collective-permute-start(bf16[128,768]{1,0:T(8,128)(2,1)S(1)} %get-tuple-element.34), channel_id=1, source_target_pairs={{0,8},{8,16},{16,24},{24,0},{1,9},{9,17},{17,25},{25,1},{2,10},{10... | collective-permute-start | bytes 589832 | tf_op jit(solution)/shard_map/heads_exchange/ppermute | solution.py:380
  8.0 0.0 collective-permute-done.4.refs_2_
  8.0 2.4 %collective-permute-start.7 = (bf16[128,768]{1,0:T(8,128)(2,1)S(1)}, bf16[128,768]{1,0:T(8,128)(2,1)S(1)}, u32[]{:S(2)}, u32[]{:S(2)}) collective-permute-start(bf16[128,768]{1,0:T(8,128)(2,1)S(1)} %get-tuple-element.35), channel_id=1, source_target_pairs={{0,16},{8,24},{16,0},{24,8},{1,17},{9,25},{17,1},{25,9},{2,18},{10... | collective-permute-start | bytes 589832 | tf_op jit(solution)/shard_map/heads_exchange/ppermute | solution.py:380
  10.3 0.0 collective-permute-done.5.refs_3_
  10.3 1.8 %collective-permute-start.8 = (bf16[128,768]{1,0:T(8,128)(2,1)S(1)}, bf16[128,768]{1,0:T(8,128)(2,1)S(1)}, u32[]{:S(2)}, u32[]{:S(2)}) collective-permute-start(bf16[128,768]{1,0:T(8,128)(2,1)S(1)} %get-tuple-element.36), channel_id=1, source_target_pairs={{0,24},{8,0},{16,8},{24,16},{1,25},{9,1},{17,9},{25,17},{2,26},{10... | collective-permute-start | bytes 589832 | tf_op jit(solution)/shard_map/heads_exchange/ppermute | solution.py:380
  12.1 0.0 copy-start.9
  12.2 8.4 %block_inverses.1.refs_8_ = bf16[4,4,2,128,128]{4,3,2,1,0:T(8,128)(2,1)S(1)} custom-call(bf16[128,384]{1,0:T(8,128)(2,1)S(1)} %get-tuple-element.29.refs_0_, bf16[128,384]{1,0:T(8,128)(2,1)S(1)} %collective-permute-done.3.refs_1_, bf16[128,384]{1,0:T(8,128)(2,1)S(1)} %collective-permute-done.4.refs_2_, bf16[128,384]{1,0:T(8,128)(2,1)S(1)} %collective-permute-done.5.refs_3_), custom_call_target="tpu_custom_call" | custom-call | flops 8000000000 | bytes 1000000 | tf_op jit(solution)/shard_map/block_inverses/pallas_call | solution.py:385
  20.5 0.0 collective-permute-done.6.refs_5_
  20.6 0.2 collective-permute-start.2
  20.8 0.0 collective-permute-done.7.refs_6_
  20.8 0.4 collective-permute-done.8.refs_7_
  21.2 0.0 copy-done.9
  21.2 6.5 %states.1.refs_4_ = f32[4,128,512]{2,1,0:T(8,128)S(1)} custom-call(bf16[128,384]{1,0:T(8,128)(2,1)S(1)} %get-tuple-element.29.refs_0_, bf16[128,384]{1,0:T(8,128)(2,1)S(1)} %collective-permute-done.3.refs_1_, bf16[128,384]{1,0:T(8,128)(2,1)S(1)} %collective-permute-done.4.refs_2_, bf16[128,384]{1,0:T(8,128)(2,1)S(1)} %collective-permute-done.5.refs_3_, ...), custom_call_target="tpu_custom_call" | custom-call | flops 4000000000 | bytes 1000000 | tf_op jit(solution)/shard_map/states/pallas_call | solution.py:392
  27.7 0.0 copy-start.2
  27.7 0.0 collective-permute-done.refs_1_
  27.7 0.0 collective-permute-done.1.refs_2_
  27.7 0.0 collective-permute-done.2.refs_3_
  27.7 2.6 %gates.1 = (bf16[4,128,512]{2,1,0:T(8,128)(2,1)S(1)}, f32[128,2048]{1,0:T(8,128)S(1)}, bf16[128,2048]{1,0:T(8,128)(2,1)S(1)}) custom-call(bf16[128,512]{1,0:T(8,128)(2,1)S(1)} %get-tuple-element.25.refs_0_, bf16[128,512]{1,0:T(8,128)(2,1)S(1)} %collective-permute-done.refs_1_, bf16[128,512]{1,0:T(8,128)(2,1)S(1)} %collective-permute-done.1.refs_2_, ...), custom_call_target="tpu_custom_call" | custom-call | tf_op jit(solution)/shard_map/gates/pallas_call | solution.py:403
  30.3 1.0 %collective-permute-start.10 = (bf16[128,2048]{1,0:T(8,128)(2,1)S(1)}, bf16[128,2048]{1,0:T(8,128)(2,1)S(1)}, u32[]{:S(2)}, u32[]{:S(2)}) collective-permute-start(bf16[128,2048]{1,0:T(8,128)(2,1)S(1)} %get-tuple-element.41), channel_id=1, source_target_pairs={{0,8},{8,0},{16,24},{24,16},{1,9},{9,1},{17,25},{25,17},{2,10},{10... | collective-permute-start | bytes 1572872 | tf_op jit(solution)/shard_map/projection_sum/ppermute | solution.py:424
  31.3 0.0 copy-done.2
  31.3 0.7 own_projection.1
  32.0 0.0 copy-start.3
  32.1 0.0 copy-start.4
  32.1 0.0 copy-start.6
  32.1 0.0 copy-start.7
  32.1 0.1 collective-permute-start.9
  32.2 0.7 collective-permute-done.10
  32.9 0.0 copy-start.1
  32.9 0.1 add_convert_fusion
  33.0 0.0 copy-start
  33.0 2.3 %collective-permute-start.11 = (bf16[128,2048]{1,0:T(8,128)(2,1)S(1)}, bf16[128,2048]{1,0:T(8,128)(2,1)S(1)}, u32[]{:S(2)}, u32[]{:S(2)}) collective-permute-start(bf16[128,2048]{1,0:T(8,128)(2,1)S(1)} %add_convert_fusion), channel_id=1, source_target_pairs={{0,16},{8,24},{16,0},{24,8},{1,17},{9,25},{17,1},{25,9},{2,18},{10... | collective-permute-start | bytes 1572872 | tf_op jit(solution)/shard_map/projection_sum/ppermute | solution.py:425
  35.3 0.0 collective-permute-done.9.refs_5_
  35.3 12.4 %collective-permute-done.11.refs_6_ = bf16[128,2048]{1,0:T(8,128)(2,1)S(1)} collective-permute-done((bf16[128,2048]{1,0:T(8,128)(2,1)S(1)}, bf16[128,2048]{1,0:T(8,128)(2,1)S(1)}, u32[]{:S(2)}, u32[]{:S(2)}) %collective-permute-start.11) | collective-permute-done | bytes 524320 | tf_op jit(solution)/shard_map/projection_sum/ppermute | solution.py:425
  47.7 0.0 copy-done.3
  47.7 0.0 copy-done.4
  47.7 0.0 copy-done.6
  47.7 0.0 copy-done.7
  47.7 1.0 %dispatch.1 = (f32[128,2048]{1,0:T(8,128)S(1)}, bf16[32,64,128]{2,1,0:T(8,128)(2,1)S(1)}, f32[128,128]{1,0:T(8,128)S(1)}) custom-call(bf16[1,128,2048]{2,1,0:T(8,128)(2,1)S(1)} %copy-done.3, f32[1,2048]{1,0:T(1,128)S(1)} %bitcast.7, s32[10,1,128]{2,1,0:T(1,128)S(1)} %bitcast.9, f32[10,1,128]{2,1,0:T(1,128)S(1)} %bitcast.10, ...), custom_call_target="tpu_custom_call" | custom-call | tf_op jit(solution)/shard_map/dispatch/pallas_call | solution.py:428
  48.7 22.3 %all_to_all.10.rows_ref = bf16[32,64,128]{2,1,0:T(8,128)(2,1)S(1)} all-to-all(bf16[32,64,128]{2,1,0:T(8,128)(2,1)S(1)} %get-tuple-element.44), channel_id=1, replica_groups=mesh['ctx'=4,'exp'=8] {'ctx','exp'}, dimensions={0} | all-to-all | bytes 1048576 | tf_op jit(solution)/shard_map/to_experts/all_to_all | solution.py:445
  71.0 0.0 copy-done.1
  71.0 0.0 copy-done
  71.0 0.0 copy-start.5
  71.0 0.0 copy-start.8
  71.0 3.2 %experts.1 = bf16[32,64,128]{2,1,0:T(8,128)(2,1)S(1)} custom-call(bf16[32,64,128]{2,1,0:T(8,128)(2,1)S(1)} %all_to_all.10.rows_ref, bf16[1,2048,512]{2,1,0:T(8,128)(2,1)S(1)} %copy-done, bf16[1,2048,512]{2,1,0:T(8,128)(2,1)S(1)} %copy-done.1, bf16[1,512,2048]{2,1,0:T(8,128)(2,1)} %down_ref.1), custom_call_target="tpu_custom_call" | custom-call | tf_op jit(solution)/shard_map/experts/pallas_call | solution.py:447
  74.2 18.4 %all_to_all.11.back_ref = bf16[32,64,128]{2,1,0:T(8,128)(2,1)S(1)} all-to-all(bf16[32,64,128]{2,1,0:T(8,128)(2,1)S(1)} %experts.1), channel_id=1, replica_groups=mesh['ctx'=4,'exp'=8] {'ctx','exp'}, dimensions={0} | all-to-all | bytes 1048576 | tf_op jit(solution)/shard_map/from_experts/all_to_all | solution.py:454
  92.6 0.0 copy-done.5
  92.6 0.0 copy-done.8
  92.6 1.7 %combine.1 = bf16[1,128,2048]{2,1,0:T(8,128)(2,1)} custom-call(f32[128,2048]{1,0:T(8,128)S(1)} %get-tuple-element.42.hidden_ref, f32[128,128]{1,0:T(8,128)S(1)} %get-tuple-element.43.table_ref, bf16[32,64,128]{2,1,0:T(8,128)(2,1)S(1)} %all_to_all.11.back_ref, s32[1,128]{1,0:T(1,128)S(1)} %copy-done.8, f32[1,2048]{1,0:T(1,128)S(1)} %bitcast.8), custom_call_target="tpu_custom_call" | custom-call | tf_op jit(solution)/shard_map/combine/pallas_call | solution.py:456
Async XLA Ops:
  1.6 4.9 %collective-permute-start.3 = (bf16[128,384]{1,0:T(8,128)(2,1)S(1)}, bf16[128,384]{1,0:T(8,128)(2,1)S(1)}, u32[]{:S(2)}, u32[]{:S(2)}) collective-permute-start(bf16[128,384]{1,0:T(8,128)(2,1)S(1)} %get-tuple-element.30), channel_id=1, source_target_pairs={{0,8},{8,16},{16,24},{24,0},{1,9},{9,17},{17,25},{25,1},{2,10},{10... | collective-permute-start | bytes 294920 | tf_op jit(solution)/shard_map/heads_exchange/ppermute | solution.py:380
  2.1 5.8 %collective-permute-start.4 = (bf16[128,384]{1,0:T(8,128)(2,1)S(1)}, bf16[128,384]{1,0:T(8,128)(2,1)S(1)}, u32[]{:S(2)}, u32[]{:S(2)}) collective-permute-start(bf16[128,384]{1,0:T(8,128)(2,1)S(1)} %get-tuple-element.31), channel_id=1, source_target_pairs={{0,16},{8,24},{16,0},{24,8},{1,17},{9,25},{17,1},{25,9},{2,18},{10... | collective-permute-start | bytes 294920 | tf_op jit(solution)/shard_map/heads_exchange/ppermute | solution.py:380
  4.7 5.6 %collective-permute-start.5 = (bf16[128,384]{1,0:T(8,128)(2,1)S(1)}, bf16[128,384]{1,0:T(8,128)(2,1)S(1)}, u32[]{:S(2)}, u32[]{:S(2)}) collective-permute-start(bf16[128,384]{1,0:T(8,128)(2,1)S(1)} %get-tuple-element.32), channel_id=1, source_target_pairs={{0,24},{8,0},{16,8},{24,16},{1,25},{9,1},{17,9},{25,17},{2,26},{10... | collective-permute-start | bytes 294920 | tf_op jit(solution)/shard_map/heads_exchange/ppermute | solution.py:380
  6.1 21.6 %collective-permute-start = (bf16[128,512]{1,0:T(8,128)(2,1)S(1)}, bf16[128,512]{1,0:T(8,128)(2,1)S(1)}, u32[]{:S(2)}, u32[]{:S(2)}) collective-permute-start(bf16[128,512]{1,0:T(8,128)(2,1)S(1)} %get-tuple-element.26), channel_id=1, source_target_pairs={{0,8},{8,16},{16,24},{24,0},{1,9},{9,17},{17,25},{25,1},{2,10},{10... | collective-permute-start | bytes 393224 | tf_op jit(solution)/shard_map/heads_exchange/ppermute | solution.py:380
  6.1 21.6 %collective-permute-start.1 = (bf16[128,512]{1,0:T(8,128)(2,1)S(1)}, bf16[128,512]{1,0:T(8,128)(2,1)S(1)}, u32[]{:S(2)}, u32[]{:S(2)}) collective-permute-start(bf16[128,512]{1,0:T(8,128)(2,1)S(1)} %get-tuple-element.27), channel_id=1, source_target_pairs={{0,16},{8,24},{16,0},{24,8},{1,17},{9,25},{17,1},{25,9},{2,18},{10... | collective-permute-start | bytes 393224 | tf_op jit(solution)/shard_map/heads_exchange/ppermute | solution.py:380
  6.5 14.1 %collective-permute-start.6 = (bf16[128,768]{1,0:T(8,128)(2,1)S(1)}, bf16[128,768]{1,0:T(8,128)(2,1)S(1)}, u32[]{:S(2)}, u32[]{:S(2)}) collective-permute-start(bf16[128,768]{1,0:T(8,128)(2,1)S(1)} %get-tuple-element.34), channel_id=1, source_target_pairs={{0,8},{8,16},{16,24},{24,0},{1,9},{9,17},{17,25},{25,1},{2,10},{10... | collective-permute-start | bytes 589832 | tf_op jit(solution)/shard_map/heads_exchange/ppermute | solution.py:380
  8.0 12.8 %collective-permute-start.7 = (bf16[128,768]{1,0:T(8,128)(2,1)S(1)}, bf16[128,768]{1,0:T(8,128)(2,1)S(1)}, u32[]{:S(2)}, u32[]{:S(2)}) collective-permute-start(bf16[128,768]{1,0:T(8,128)(2,1)S(1)} %get-tuple-element.35), channel_id=1, source_target_pairs={{0,16},{8,24},{16,0},{24,8},{1,17},{9,25},{17,1},{25,9},{2,18},{10... | collective-permute-start | bytes 589832 | tf_op jit(solution)/shard_map/heads_exchange/ppermute | solution.py:380
  10.3 10.9 %collective-permute-start.8 = (bf16[128,768]{1,0:T(8,128)(2,1)S(1)}, bf16[128,768]{1,0:T(8,128)(2,1)S(1)}, u32[]{:S(2)}, u32[]{:S(2)}) collective-permute-start(bf16[128,768]{1,0:T(8,128)(2,1)S(1)} %get-tuple-element.36), channel_id=1, source_target_pairs={{0,24},{8,0},{16,8},{24,16},{1,25},{9,1},{17,9},{25,17},{2,26},{10... | collective-permute-start | bytes 589832 | tf_op jit(solution)/shard_map/heads_exchange/ppermute | solution.py:380
  12.1 9.0 %copy-start.9 = (f32[128]{0:T(128)S(1)}, f32[128]{0:T(128)}, u32[]{:S(2)}) copy-start(f32[128]{0:T(128)} %param.23) | copy-start | bytes 1540
  20.6 7.2 %collective-permute-start.2 = (bf16[128,512]{1,0:T(8,128)(2,1)S(1)}, bf16[128,512]{1,0:T(8,128)(2,1)S(1)}, u32[]{:S(2)}, u32[]{:S(2)}) collective-permute-start(bf16[128,512]{1,0:T(8,128)(2,1)S(1)} %get-tuple-element.28), channel_id=1, source_target_pairs={{0,24},{8,0},{16,8},{24,16},{1,25},{9,1},{17,9},{25,17},{2,26},{10... | collective-permute-start | bytes 393224 | tf_op jit(solution)/shard_map/heads_exchange/ppermute | solution.py:380
  27.7 3.6 %copy-start.2 = (bf16[512,2048]{1,0:T(8,128)(2,1)S(1)}, bf16[512,2048]{1,0:T(8,128)(2,1)}, u32[]{:S(2)}) copy-start(bf16[512,2048]{1,0:T(8,128)(2,1)} %proj_ref.1) | copy-start | bytes 6291460
  30.3 2.5 %collective-permute-start.10 = (bf16[128,2048]{1,0:T(8,128)(2,1)S(1)}, bf16[128,2048]{1,0:T(8,128)(2,1)S(1)}, u32[]{:S(2)}, u32[]{:S(2)}) collective-permute-start(bf16[128,2048]{1,0:T(8,128)(2,1)S(1)} %get-tuple-element.41), channel_id=1, source_target_pairs={{0,8},{8,0},{16,24},{24,16},{1,9},{9,1},{17,25},{25,17},{2,10},{10... | collective-permute-start | bytes 1572872 | tf_op jit(solution)/shard_map/projection_sum/ppermute | solution.py:424
  32.0 15.7 %copy-start.3 = (bf16[1,128,2048]{2,1,0:T(8,128)(2,1)S(1)}, bf16[1,128,2048]{2,1,0:T(8,128)(2,1)}, u32[]{:S(2)}) copy-start(bf16[1,128,2048]{2,1,0:T(8,128)(2,1)} %refs_0_.1) | copy-start | bytes 1572868
  32.1 15.7 %copy-start.4 = (f32[2048]{0:T(1024)S(1)}, f32[2048]{0:T(1024)}, u32[]{:S(2)}) copy-start(f32[2048]{0:T(1024)} %param.26) | copy-start | bytes 24580
  32.1 15.7 %copy-start.6 = (s32[1,128,10]{1,0,2:T(1,128)S(1)}, s32[1,128,10]{1,0,2:T(1,128)}, u32[]{:S(2)}) copy-start(s32[1,128,10]{1,0,2:T(1,128)} %param.27) | copy-start | bytes 15364
  32.1 15.7 %copy-start.7 = (f32[1,128,10]{1,0,2:T(1,128)S(1)}, f32[1,128,10]{1,0,2:T(1,128)}, u32[]{:S(2)}) copy-start(f32[1,128,10]{1,0,2:T(1,128)} %param.28) | copy-start | bytes 15364
  32.1 3.2 %collective-permute-start.9 = (bf16[128,2048]{1,0:T(8,128)(2,1)S(1)}, bf16[128,2048]{1,0:T(8,128)(2,1)S(1)}, u32[]{:S(2)}, u32[]{:S(2)}) collective-permute-start(bf16[128,2048]{1,0:T(8,128)(2,1)S(1)} %get-tuple-element.39), channel_id=1, source_target_pairs={{0,8},{8,0},{16,24},{24,16},{1,9},{9,1},{17,25},{25,17},{2,10},{10... | collective-permute-start | bytes 1572872 | tf_op jit(solution)/shard_map/projection_sum/ppermute | solution.py:426
  32.9 38.1 %copy-start.1 = (bf16[1,2048,512]{2,1,0:T(8,128)(2,1)S(1)}, bf16[1,2048,512]{2,1,0:T(8,128)(2,1)}, u32[]{:S(2)}) copy-start(bf16[1,2048,512]{2,1,0:T(8,128)(2,1)} %up_ref.1) | copy-start | bytes 6291460
  33.0 38.0 %copy-start = (bf16[1,2048,512]{2,1,0:T(8,128)(2,1)S(1)}, bf16[1,2048,512]{2,1,0:T(8,128)(2,1)}, u32[]{:S(2)}) copy-start(bf16[1,2048,512]{2,1,0:T(8,128)(2,1)} %gate_ref.1) | copy-start | bytes 6291460
  33.0 14.7 %collective-permute-start.11 = (bf16[128,2048]{1,0:T(8,128)(2,1)S(1)}, bf16[128,2048]{1,0:T(8,128)(2,1)S(1)}, u32[]{:S(2)}, u32[]{:S(2)}) collective-permute-start(bf16[128,2048]{1,0:T(8,128)(2,1)S(1)} %add_convert_fusion), channel_id=1, source_target_pairs={{0,16},{8,24},{16,0},{24,8},{1,17},{9,25},{17,1},{25,9},{2,18},{10... | collective-permute-start | bytes 1572872 | tf_op jit(solution)/shard_map/projection_sum/ppermute | solution.py:425
  71.0 21.7 %copy-start.5 = (f32[2048]{0:T(1024)S(1)}, f32[2048]{0:T(1024)}, u32[]{:S(2)}) copy-start(f32[2048]{0:T(1024)} %param.33) | copy-start | bytes 24580
  71.0 21.7 %copy-start.8 = (s32[1,128]{1,0:T(1,128)S(1)}, s32[1,128]{1,0:T(1,128)}, u32[]{:S(2)}) copy-start(s32[1,128]{1,0:T(1,128)} %mask_ref.1) | copy-start | bytes 1540

commit v2 on v1

v2 whole, which is shorter than its diff:
```python
import functools

import jax
import jax.numpy as jnp
from jax import lax
from jax.experimental import pallas as pl
from jax.experimental.pallas import tpu as pltpu
from jax.sharding import PartitionSpec as P

DK = 128
CAP = 4
EPS = 1e-06
AUX = 16
LANES = 128

bf16 = jnp.bfloat16
f32 = jnp.float32


def mm(a, b):
    return jnp.dot(a, b, preferred_element_type=f32)


def mm_nt(a, b):
    return lax.dot_general(a, b, (((1,), (1,)), ((), ())), preferred_element_type=f32)


def mm_tn(a, b):
    return lax.dot_general(a, b, (((0,), (0,)), ((), ())), preferred_element_type=f32)


def split2(x):
    hi = x.astype(bf16)
    return hi, (x - hi.astype(f32)).astype(bf16)


def split3(x):
    hi = x.astype(bf16)
    rest = x - hi.astype(f32)
    mid = rest.astype(bf16)
    return hi, mid, (rest - mid.astype(f32)).astype(bf16)


def mm3(a, b):
    (ah, al), (bh, bl) = a, b
    return mm(jnp.concatenate([ah, al, ah], axis=1), jnp.concatenate([bh, bh, bl], axis=0))


def iota(shape, dim):
    return lax.broadcasted_iota(jnp.int32, shape, dim)


def in_hbm(*arrays):
    return [pltpu.with_memory_space_constraint(a, pltpu.HBM) for a in arrays]


def compiler_params(mib):
    return pltpu.CompilerParams(vmem_limit_bytes=mib * 1024 * 1024)


def routes(n):
    return [(chips, flip) for chips in range(n // 2) for flip in (0, 1)]


def moved(index, route, n, back=False):
    chips, flip = route
    chip = lax.rem(index // 2 + (n // 2 - chips if back else chips), n // 2)
    return chip * 2 + lax.rem(lax.rem(index, 2) + flip, 2)


def send(x, route, n):
    chips, flip = route
    pairs = [(i, (i // 2 + chips) % (n // 2) * 2 + (i % 2 + flip) % 2) for i in range(n)]
    return lax.ppermute(x, "ctx", pairs)


def pack_kernel(n, kw, vw, k_ref, q_ref, v_ref, g_ref, w_ref, d_ref, *outs):
    me = lax.axis_index("ctx")
    tokens = k_ref.shape[1]
    heads = d_ref.shape[1]
    local = vw // DK
    ones = (iota((tokens, tokens), 0) <= iota((tokens, tokens), 1)).astype(bf16)
    logs = jnp.log(d_ref[0])
    sums = sum(mm(piece, ones) for piece in reversed(split3(logs)))
    pieces = [p.astype(f32) for p in (*split3(sums), *split3(w_ref[0]))]
    rates = jnp.concatenate(pieces, axis=0).astype(bf16)
    rows = AUX * kw // LANES
    row, entry = iota((rows, 6 * heads), 0), iota((rows, 6 * heads), 1)
    outs = list(outs)
    for route in routes(n):
        to = moved(me, route, n)
        kat = pl.ds(pl.multiple_of(to * kw, LANES), kw)
        vat = pl.ds(pl.multiple_of(to * vw, LANES), vw)
        keyed = outs.pop(0)
        keyed[0:tokens] = k_ref[0, :, kat]
        wanted = row // local * heads + to * local + lax.rem(row, local)
        aux = mm(((row < 6 * local) & (entry == wanted)).astype(bf16), rates)
        for i in range(kw // LANES):
            keyed[tokens:, i * LANES : (i + 1) * LANES] = aux[i * AUX : (i + 1) * AUX].astype(bf16)
        asked = outs.pop(0)
        asked[:, 0:kw] = q_ref[0, :, kat]
        asked[:, kw : kw + vw] = v_ref[0, :, vat]
        if route[0] == 0:
            asked[:, kw + vw :] = g_ref[0, :, vat]
        else:
            outs.pop(0)[...] = g_ref[0, :, vat]


def head_rates(local, keyed, tokens):
    aux = jnp.concatenate(
        [keyed[tokens:, i * LANES : (i + 1) * LANES] for i in range(keyed.shape[1] // LANES)], axis=0
    )
    row, col = iota((aux.shape[0], LANES), 0), iota((aux.shape[0], LANES), 1)
    total = (
        (row < 6 * local) & (col < 2 * local) & (lax.rem(row, local) == lax.rem(col, local)) & (row // (3 * local) == col // local)
    ).astype(bf16)
    return mm_tn(aux, total), mm_tn(total, aux)


def inverse_scale(raw):
    raw_f = raw.astype(f32)
    return lax.rsqrt(jnp.sum(raw_f * raw_f, axis=1, keepdims=True) + EPS)


def inverse_kernel(n, local, *refs):
    keyed, inv_ref = refs[:n], refs[n]
    me = lax.axis_index("ctx")
    tokens = inv_ref.shape[-1]
    group = local * DK // keyed[0].shape[1]
    row, col = iota((tokens, tokens), 0), iota((tokens, tokens), 1)
    apart = lax.bitwise_xor(row, col)
    eye = (row == col).astype(f32)
    systems = []
    for piece in keyed:
        as_cols, as_rows = head_rates(local, piece, tokens)
        for g in range(local // group):
            k = piece[0:tokens, g * DK : (g + 1) * DK]
            dots = mm_nt(k, k)
            diag = dots * eye
            k_row = lax.rsqrt(jnp.sum(diag, axis=0, keepdims=True) + EPS)
            k_col = lax.rsqrt(jnp.sum(diag, axis=1, keepdims=True) + EPS)
            dots = jnp.where(row > col, dots * k_row * k_col, 0.0)
            for h in range(g * group, (g + 1) * group):
                gap = as_cols[:, h : h + 1] - as_rows[h : h + 1, :]
                write = as_cols[:, local + h : local + h + 1]
                systems.append(write * jnp.exp(jnp.minimum(gap, 0.0)) * dots)
    near = [jnp.where(apart < 16, s, 0.0) for s in systems]
    power = [split2(s) for s in near]
    inverse = [eye - s for s in near]
    power = [mm3(p, p) for p in power]
    for _ in range(2):
        halves = [split2(p) for p in power]
        both = [mm3(split2(jnp.concatenate([p, x], axis=0)), ps) for p, x, ps in zip(power, inverse, halves)]
        power = [b[:tokens] for b in both]
        inverse = [x + b[tokens:] for x, b in zip(inverse, both)]
    inverse = [x + mm3(split2(x), split2(p)) for x, p in zip(inverse, power)]
    size = 16
    while size < tokens:
        odd = [slice(at, at + size) for at in range(size, tokens, 2 * size)]
        beside = (apart >= size) & (apart < 2 * size)
        below = [jnp.where(beside, s, 0.0) for s in systems]
        below = [split2(jnp.concatenate([b[o] for o in odd], axis=0)) for b in below]
        halves = [split2(x) for x in inverse]
        first = [mm3(b, x) for b, x in zip(below, halves)]
        first = [split2(widen(f, size)) for f in first]
        lower = [tuple(jnp.concatenate([part[o] for o in odd], axis=0) for part in x) for x in halves]
        inverse = [x - widen(mm3(a, b), size) for x, a, b in zip(inverse, lower, first)]
        size *= 2
    for i, route in enumerate(routes(n)):
        block = moved(me, route, n, back=True)
        for h in range(local):
            hi, lo = split2(inverse[i * local + h])
            inv_ref[block, h, 0] = hi
            inv_ref[block, h, 1] = lo


def widen(x, size):
    none = jnp.zeros((size, x.shape[1]), x.dtype)
    return jnp.concatenate(
        [part for at in range(0, x.shape[0], size) for part in (none, x[at : at + size])], axis=0
    )


def state_kernel(n, kw, vw, *refs):
    keyed, asked = refs[:n], refs[n : 2 * n]
    inv_ref, gain_ref, out_ref, kx_ref, qv_ref = refs[2 * n :]
    me = lax.axis_index("ctx")
    tokens = inv_ref.shape[-1]
    local = vw // DK
    group = vw // kw
    all_heads = range(local)
    for i, route in enumerate(routes(n)):
        block = moved(me, route, n, back=True)
        kx_ref[block] = keyed[i][...]
        qv_ref[block] = asked[i][:, 0 : kw + vw]
    row, col = iota((tokens, tokens), 0), iota((tokens, tokens), 1)
    eye = (row == col).astype(f32)
    gain = gain_ref[...]

    def prepare(block):
        as_cols, as_rows = head_rates(local, kx_ref.at[block], tokens)
        cumulative = jnp.exp(as_cols)
        last = as_cols[tokens - 1 : tokens]
        ends = jnp.exp(last)
        kept = jnp.exp(last - as_cols)
        made = []
        for g in range(local // group):
            k = kx_ref[block, 0:tokens, g * DK : (g + 1) * DK]
            q = qv_ref[block, :, g * DK : (g + 1) * DK]
            k_col = inverse_scale(k)
            q_col = inverse_scale(q) * DK ** (-0.5)
            k_row = jnp.sum(eye * k_col, axis=0, keepdims=True)
            dots = jnp.where(row >= col, mm_nt(q, k) * k_row * q_col, 0.0)
            for h in range(g * group, (g + 1) * group):
                gap = as_cols[:, h : h + 1] - as_rows[h : h + 1, :]
                scores = split2(jnp.exp(jnp.minimum(gap, 0.0)) * dots)
                write = as_cols[:, local + h : local + h + 1]
                cum = cumulative[:, h : h + 1]
                made.append(
                    dict(
                        k=k,
                        q=q,
                        scores=scores,
                        write=write,
                        erase=write * cum * k_col,
                        ask=cum * q_col,
                        kept=kept[:, h : h + 1] * k_col,
                        end=ends[:, h : h + 1],
                    )
                )
        return made

    def finish(block, made, seen, delta):
        for h in all_heads:
            out = mm3(made[h]["scores"], delta[h])
            if block > 0:
                out = out + made[h]["ask"] * seen[h][tokens:]
            mean = jnp.mean(out * out, axis=1, keepdims=True)
            out_ref[block, :, h * DK : (h + 1) * DK] = out * lax.rsqrt(mean + EPS) * gain

    states, before, made = None, None, prepare(0)
    for block in range(n):
        rhs = [
            m["write"] * qv_ref[block, :, kw + h * DK : kw + (h + 1) * DK].astype(f32) for h, m in enumerate(made)
        ]
        seen = None
        if block > 0:
            both = [jnp.concatenate([m["k"], m["q"]], axis=0) for m in made]
            seen = [
                mm(jnp.concatenate([b, b], axis=1), jnp.concatenate(split2(s), axis=0)) for b, s in zip(both, states)
            ]
        if before is not None:
            finish(*before)
        if block > 0:
            rhs = [r - m["erase"] * s[:tokens] for r, m, s in zip(rhs, made, seen)]
        delta = [mm3((inv_ref[block, h, 0], inv_ref[block, h, 1]), split2(rhs[h])) for h in all_heads]
        later = prepare(block + 1) if block < n - 1 else None
        if block < n - 1:
            grown = [
                mm_tn(jnp.concatenate([m["k"], m["k"]], axis=0), jnp.concatenate(split2(m["kept"] * d), axis=0))
                for m, d in zip(made, delta)
            ]
            states = grown if block == 0 else [m["end"] * s + g for m, s, g in zip(made, states, grown)]
        before = (block, made, seen, [split2(d) for d in delta])
        made = later
    finish(*before)


def gate_kernel(n, *refs):
    gated = refs[:n]
    normed_ref, proj_ref, mixed_ref = refs[n : n + 3]
    chips = n // 2
    keeps = refs[n + 3 : n + 2 + chips]
    gives = refs[n + 2 + chips :]
    me = lax.axis_index("ctx")
    vw = mixed_ref.shape[2]
    for i, route in enumerate(routes(n)):
        block = moved(me, route, n, back=True)
        gate = gated[i][:, gated[i].shape[1] - vw :].astype(f32)
        mixed_ref[block] = (normed_ref[block] * (gate / (1.0 + jnp.exp(-gate)))).astype(bf16)
    for j in range(1, chips):
        project(mixed_ref, moved(me, (j, 1), n), proj_ref, gives[j - 1])
        project(mixed_ref, moved(me, (j, 0), n), proj_ref, keeps[j - 1])


def project(mixed_ref, block, proj_ref, out_ref):
    mine = mixed_ref[block]
    width = 512
    for c in range(0, proj_ref.shape[1], width):
        out_ref[:, c : c + width] = mm(mine, proj_ref[:, c : c + width]).astype(out_ref.dtype)


def own_kernel(n, mixed_ref, proj_ref, keep_ref, give_ref):
    me = lax.axis_index("ctx")
    project(mixed_ref, moved(me, (0, 1), n), proj_ref, give_ref)
    project(mixed_ref, me, proj_ref, keep_ref)


def dispatch_kernel(parts, *refs):
    residual_ref, gain_ref, ids_ref, weight_ref = refs[:4]
    part_refs = refs[4 : 4 + parts]
    hidden_ref, rows_ref, table_ref, flat_ref = refs[4 + parts :]
    tokens, width = hidden_ref.shape
    slots = table_ref.shape[0]
    chunks = width // LANES
    hidden = residual_ref[0].astype(f32)
    for part in part_refs:
        hidden = hidden + part[...].astype(f32)
    hidden_ref[...] = hidden
    mean = jnp.mean(hidden * hidden, axis=1, keepdims=True)
    normed = (hidden * lax.rsqrt(mean + EPS) * gain_ref[...]).astype(bf16)
    slot = iota((slots, tokens), 0)
    expert = slot // CAP
    named = jnp.zeros((slots, tokens), f32)
    weight = jnp.zeros((slots, tokens), f32)
    for j in range(ids_ref.shape[0]):
        hit = ids_ref[j] == expert
        named = named + hit.astype(f32)
        weight = weight + jnp.where(hit, weight_ref[j], 0.0)
    before = (iota((tokens, tokens), 0) < iota((tokens, tokens), 1)).astype(bf16)
    rank = mm(named.astype(bf16), before)
    chosen = jnp.where(rank == lax.rem(slot, CAP).astype(f32), named, 0.0)
    table_ref[...] = chosen * weight
    picker = chosen.astype(bf16)
    step = 512
    for c in range(0, width, step):
        rows = mm(picker, normed[:, c : c + step])
        for i in range(step // LANES):
            flat_ref[pl.ds(c // LANES + i, slots, stride=chunks), :] = rows[:, i * LANES : (i + 1) * LANES]
    rows_ref[...] = flat_ref[...].astype(bf16).reshape(rows_ref.shape)


def expert_kernel(rows_ref, gate_ref, up_ref, down_ref, out_ref, flat_ref, x_ref):
    slots = flat_ref.shape[0] * LANES // x_ref.shape[1]
    width = x_ref.shape[1]
    chunks = width // LANES
    flat_ref[...] = rows_ref[...].reshape(flat_ref.shape).astype(f32)
    for c in range(chunks):
        x_ref[:, c * LANES : (c + 1) * LANES] = flat_ref[pl.ds(c, slots, stride=chunks), :].astype(bf16)
    tile = 128

    def one(t, carry):
        x = x_ref[pl.ds(pl.multiple_of(t * tile, tile), tile), :]
        gate = mm(x, gate_ref[0])
        up = mm(x, up_ref[0])
        act = (gate / (1.0 + jnp.exp(-gate)) * up).astype(bf16)
        step = 512
        for c in range(0, width, step):
            y = mm(act, down_ref[0, :, c : c + step])
            for i in range(step // LANES):
                flat_ref[pl.ds(t * tile * chunks + c // LANES + i, tile, stride=chunks), :] = y[
                    :, i * LANES : (i + 1) * LANES
                ]
        return carry

    lax.fori_loop(0, slots // tile, one, 0)
    out_ref[...] = flat_ref[...].astype(bf16).reshape(out_ref.shape)


def combine_kernel(hidden_ref, table_ref, back_ref, mask_ref, dir_ref, out_ref, flat_ref, ret_ref):
    tokens, width = hidden_ref.shape
    slots = table_ref.shape[0]
    chunks = width // LANES
    flat_ref[...] = back_ref[...].reshape(flat_ref.shape).astype(f32)
    for c in range(chunks):
        got = flat_ref[pl.ds(c, slots, stride=chunks), :].astype(bf16)
        ret_ref[0:slots, c * LANES : (c + 1) * LANES] = got
        ret_ref[slots : 2 * slots, c * LANES : (c + 1) * LANES] = got
    high, low = split2(table_ref[...])
    moe = mm_tn(jnp.concatenate([high, low], axis=0), ret_ref[...])
    combined = hidden_ref[...] + moe
    direction = dir_ref[...]
    unit = direction / jnp.sqrt(jnp.sum(direction * direction, axis=1, keepdims=True) + EPS)
    along = jnp.sum(combined * unit, axis=1, keepdims=True)
    eye = iota((tokens, tokens), 0) == iota((tokens, tokens), 1)
    mask = jnp.sum(jnp.where(eye, mask_ref[...].astype(f32), 0.0), axis=1, keepdims=True)
    out_ref[0] = (combined - (mask * along) * unit).astype(bf16)


def local_part(
    n,
    devices,
    queries,
    keys,
    values,
    out_gate,
    write_rate,
    decay,
    head_gain,
    residual,
    out_proj,
    ffn_gain,
    expert_ids,
    route_weight,
    w_gate,
    w_up,
    w_down,
    ablate_mask,
    direction,
):
    tokens = queries.shape[1]
    width = residual.shape[2]
    kw, vw = keys.shape[2] // n, values.shape[2] // n
    chips = n // 2
    slots = devices * CAP
    chunks = width // LANES
    shape = jax.ShapeDtypeStruct

    local = vw // DK
    ways = routes(n)
    keyed_shape = shape((tokens + AUX, kw), bf16)
    with jax.named_scope("pack"):
        packed = pl.pallas_call(
            functools.partial(pack_kernel, n, kw, vw),
            out_shape=[
                out
                for route in ways
                for out in (
                    [keyed_shape, shape((tokens, kw + 2 * vw), bf16)]
                    if route[0] == 0
                    else [keyed_shape, shape((tokens, kw + vw), bf16), shape((tokens, vw), bf16)]
                )
            ],
            compiler_params=compiler_params(16),
        )(*in_hbm(keys, queries, values, out_gate, write_rate.transpose(0, 2, 1), decay.transpose(0, 2, 1)))
    with jax.named_scope("heads_exchange"):
        packed = list(packed)
        keyed, asked, gated = [], [], []
        for route in ways:
            keyed.append(packed.pop(0))
            asked.append(packed.pop(0))
            gated.append(packed.pop(0) if route[0] else None)
        order = [i for i, route in enumerate(ways) if route[0]] + [1]
        for i in order:
            keyed[i] = send(keyed[i], ways[i], n)
        for i in order[:-1]:
            asked[i] = send(asked[i], ways[i], n)
        keyed, late = lax.optimization_barrier((keyed, [asked[1]] + [gated[i] for i in order[:-1]]))
        asked[1] = send(late[0], ways[1], n)
        for i, gate in zip(order[:-1], late[1:]):
            gated[i] = send(gate, ways[i], n)
        gated[:2] = asked[:2]
    with jax.named_scope("block_inverses"):
        inverses = pl.pallas_call(
            functools.partial(inverse_kernel, n, local),
            out_shape=shape((n, local, 2, tokens, tokens), bf16),
            compiler_params=compiler_params(16),
            cost_estimate=pl.CostEstimate(flops=6 * 10**9, bytes_accessed=10**6, transcendentals=0),
        )(*keyed)
    with jax.named_scope("states"):
        normed = pl.pallas_call(
            functools.partial(state_kernel, n, kw, vw),
            out_shape=shape((n, tokens, vw), f32),
            scratch_shapes=[
                pltpu.VMEM((n, tokens + AUX, kw), bf16),
                pltpu.VMEM((n, tokens, kw + vw), bf16),
            ],
            compiler_params=compiler_params(16),
            cost_estimate=pl.CostEstimate(flops=4 * 10**9, bytes_accessed=10**6, transcendentals=0),
        )(*keyed, *asked, inverses, head_gain.reshape(1, -1))
    with jax.named_scope("gates"):
        outs = pl.pallas_call(
            functools.partial(gate_kernel, n),
            out_shape=[shape((n, tokens, vw), bf16)]
            + [shape((tokens, width), f32)] * (chips - 1)
            + [shape((tokens, width), bf16)] * (chips - 1),
            compiler_params=compiler_params(16),
        )(*gated, normed, out_proj)
    mixed, keeps, gives = outs[0], outs[1:chips], outs[chips:]
    with jax.named_scope("own_projection"):
        keep, give = pl.pallas_call(
            functools.partial(own_kernel, n),
            out_shape=[shape((tokens, width), f32), shape((tokens, width), bf16)],
            compiler_params=compiler_params(16),
            cost_estimate=pl.CostEstimate(flops=2 * 10**9, bytes_accessed=10**6, transcendentals=0),
        )(mixed, out_proj)
    with jax.named_scope("projection_sum"):
        parts = []
        for j in range(chips - 1, 0, -1):
            pair = keeps[j - 1] + send(gives[j - 1], (0, 1), n).astype(f32)
            parts.append(send(pair.astype(bf16), (j, 0), n))
        parts = [keep, send(give, (0, 1), n)] + parts
    with jax.named_scope("dispatch"):
        hidden, rows, table = pl.pallas_call(
            functools.partial(dispatch_kernel, len(parts)),
            out_shape=[
                shape((tokens, width), f32),
                shape((devices, CAP * chunks, LANES), bf16),
                shape((slots, tokens), f32),
            ],
            scratch_shapes=[pltpu.VMEM((slots * chunks, LANES), f32)],
            compiler_params=compiler_params(24),
        )(
            residual,
            ffn_gain.reshape(1, -1),
            expert_ids.transpose(2, 0, 1),
            route_weight.transpose(2, 0, 1),
            *parts,
        )
    with jax.named_scope("to_experts"):
        came = lax.all_to_all(rows, ("ctx", "exp"), 0, 0, tiled=True)
    with jax.named_scope("experts"):
        done = pl.pallas_call(
            expert_kernel,
            out_shape=shape((devices, CAP * chunks, LANES), bf16),
            scratch_shapes=[pltpu.VMEM((slots * chunks, LANES), f32), pltpu.VMEM((slots, width), bf16)],
            compiler_params=compiler_params(24),
        )(came, w_gate, w_up, w_down)
    with jax.named_scope("from_experts"):
        back = lax.all_to_all(done, ("ctx", "exp"), 0, 0, tiled=True)
    with jax.named_scope("combine"):
        return pl.pallas_call(
            combine_kernel,
            out_shape=shape((1, tokens, width), bf16),
            scratch_shapes=[
                pltpu.VMEM((slots * chunks, LANES), f32),
                pltpu.VMEM((2 * slots, width), bf16),
            ],
            compiler_params=compiler_params(24),
        )(hidden, table, back, ablate_mask, direction.reshape(1, -1))


def solution(mesh):
    seq = P("exp", "ctx", None)
    owned = P(("ctx", "exp"), None, None)
    placed = (
        (seq,) * 6 + (P(), seq, P("ctx", None), P(), seq, seq) + (owned,) * 3 + (P("exp", "ctx"), P())
    )
    n = mesh.shape["ctx"]
    return jax.shard_map(
        functools.partial(local_part, n, n * mesh.shape["exp"]),
        mesh=mesh,
        in_specs=placed,
        out_specs=seq,
        check_vma=False,
    )
```

time: 94.6 us -> 85.5 us (0.904)
  Pallas kernels: 25.7 us -> 17.9 us
  starting transfers between devices: 14.1 us -> 9.27 us
  waiting for transfers between devices: 13.5 us -> 17.1 us
    pallas_call x4, Pallas kernels: 19.1 us -> 12.9 us  [the longest x1 5.39 us: local_part(): pl.pallas_call(functools.partial(inverse_kernel, n, local), out_shape=sha...]
    ppermute x12 -> x11, starting transfers between devices: 14.1 us -> 9.27 us  [send(): return lax.ppermute(x, 'ctx', pairs)]
    ppermute x12 -> x11, waiting for transfers between devices: 13.5 us -> 17.1 us  [send(): return lax.ppermute(x, 'ctx', pairs)]
    pallas_call x1, Pallas kernels: 3.23 us -> 1.6 us  [local_part(): pl.pallas_call(expert_kernel, out_shape=shape((devices, CAP * chunks, LAN...]
  transfers between devices with their start and end apart: 12 -> 11, of which waited for: 3 -> 6; matrix products, arithmetic and copies ran while one was open for 0% -> 0% of each run, Pallas kernels for 17% -> 13%
where the time goes in v2:
time: 85.5 us; the launch traced here: 85.3 us
  blocking collectives  40.6 us (47%)
  Pallas kernels  17.9 us (21%)
  waiting for transfers between devices  17.1 us (20%)
  starting transfers between devices  9.27 us (11%)
    all_to_all x1, blocking collectives, local_part(): came = lax.all_to_all(rows, ('ctx', 'exp'), 0, 0, tiled=True)  22.2 us
    all_to_all x1, blocking collectives, local_part(): back = lax.all_to_all(done, ('ctx', 'exp'), 0, 0, tiled=True)  18.4 us
    ppermute x11, waiting for transfers between devices, send(): return lax.ppermute(x, 'ctx', pairs)  17.1 us
    ppermute x11, starting transfers between devices, send(): return lax.ppermute(x, 'ctx', pairs)  9.27 us
    pallas_call x1, Pallas kernels, local_part(): pl.pallas_call(functools.partial(inverse_kernel, n, local), out_shape=sha...  5.39 us
    pallas_call x1, Pallas kernels, local_part(): pl.pallas_call(functools.partial(state_kernel, n, kw, vw), out_shape=shap...  4.82 us
    pallas_call x1, Pallas kernels, local_part(): pl.pallas_call(combine_kernel, out_shape=shape((1, tokens, width), bf16),...  1.73 us
  transfers between devices with their start and end apart: 11, of which 6 were waited for; matrix products, arithmetic and copies ran while one was open for 0% of the time, Pallas kernels for 13%

profile of v2, /device:TPU:0, one launch (start us, length us, event | category | flops | bytes accessed | tf_op | source)
XLA Modules:
  0.0 85.3 jit_solution(3633195368862436755)
XLA Ops:
  0.0 1.7 %pack.1 = (bf16[144,256]{1,0:T(8,128)(2,1)S(1)}, bf16[128,1280]{1,0:T(8,128)(2,1)S(1)}, bf16[144,256]{1,0:T(8,128)(2,1)S(1)}, bf16[128,1280]{1,0:T(8,128)(2,1)S(...) custom-call(bf16[1,128,1024]{2,1,0:T(8,128)(2,1)} %k_ref.1, ...), custom_call_target="tpu_custom_call" | custom-call | tf_op jit(solution)/shard_map/pack/pallas_call | solution.py:413
  1.7 0.5 collective-permute-start
  2.2 2.6 %collective-permute-start.1 = (bf16[144,256]{1,0:T(8,128)(2,1)S(1)}, bf16[144,256]{1,0:T(8,128)(2,1)S(1)}, u32[]{:S(2)}, u32[]{:S(2)}) collective-permute-start(bf16[144,256]{1,0:T(8,128)(2,1)S(1)} %get-tuple-element.33), channel_id=1, source_target_pairs={{0,16},{8,24},{16,0},{24,8},{1,17},{9,25},{17,1},{25,9},{2,18},{10... | collective-permute-start | bytes 221192 | tf_op jit(solution)/shard_map/heads_exchange/ppermute | solution.py:74
  4.8 0.1 collective-permute-start.2
  4.8 1.7 %collective-permute-start.6 = (bf16[128,768]{1,0:T(8,128)(2,1)S(1)}, bf16[128,768]{1,0:T(8,128)(2,1)S(1)}, u32[]{:S(2)}, u32[]{:S(2)}) collective-permute-start(bf16[128,768]{1,0:T(8,128)(2,1)S(1)} %get-tuple-element.45), channel_id=1, source_target_pairs={{0,16},{8,24},{16,0},{24,8},{1,17},{9,25},{17,1},{25,9},{2,18},{10... | collective-permute-start | bytes 589832 | tf_op jit(solution)/shard_map/heads_exchange/ppermute | solution.py:74
  6.6 0.0 collective-permute-start.7
  6.6 0.0 collective-permute-done.refs_1_
  6.6 1.0 %collective-permute-done.1.refs_2_ = bf16[144,256]{1,0:T(8,128)(2,1)S(1)} collective-permute-done((bf16[144,256]{1,0:T(8,128)(2,1)S(1)}, bf16[144,256]{1,0:T(8,128)(2,1)S(1)}, u32[]{:S(2)}, u32[]{:S(2)}) %collective-permute-start.1) | collective-permute-done | bytes 73760 | tf_op jit(solution)/shard_map/heads_exchange/ppermute | solution.py:74
  7.6 1.4 %collective-permute-done.2.refs_3_ = bf16[144,256]{1,0:T(8,128)(2,1)S(1)} collective-permute-done((bf16[144,256]{1,0:T(8,128)(2,1)S(1)}, bf16[144,256]{1,0:T(8,128)(2,1)S(1)}, u32[]{:S(2)}, u32[]{:S(2)}) %collective-permute-start.2) | collective-permute-done | bytes 73760 | tf_op jit(solution)/shard_map/heads_exchange/ppermute | solution.py:74
  9.0 0.0 copy-start.10
  9.0 1.5 %collective-permute-start.4 = (bf16[128,512]{1,0:T(8,128)(2,1)S(1)}, bf16[128,512]{1,0:T(8,128)(2,1)S(1)}, u32[]{:S(2)}, u32[]{:S(2)}) collective-permute-start(bf16[128,512]{1,0:T(8,128)(2,1)S(1)} %get-tuple-element.39), channel_id=1, source_target_pairs={{0,16},{8,24},{16,0},{24,8},{1,17},{9,25},{17,1},{25,9},{2,18},{10... | collective-permute-start | bytes 393224 | tf_op jit(solution)/shard_map/heads_exchange/ppermute | solution.py:74
  10.5 0.4 collective-permute-start.5
  10.9 0.3 collective-permute-start.3
  11.1 5.4 %block_inverses.1.refs_8_ = bf16[4,4,2,128,128]{4,3,2,1,0:T(8,128)(2,1)S(1)} custom-call(bf16[144,256]{1,0:T(8,128)(2,1)S(1)} %get-tuple-element.41.refs_0_, bf16[144,256]{1,0:T(8,128)(2,1)S(1)} %collective-permute-done.refs_1_, bf16[144,256]{1,0:T(8,128)(2,1)S(1)} %collective-permute-done.1.refs_2_, bf16[144,256]{1,0:T(8,128)(2,1)S(1)} %collective-permute-done.2.refs_3_), custom_call_target="tpu_custom_call" | custom-call | flops 6000000000 | bytes 1000000 | tf_op jit(solution)/shard_map/block_inverses/pallas_call | solution.py:444
  16.5 0.0 collective-permute-done.6.refs_6_
  16.6 0.9 %collective-permute-done.7.refs_7_ = bf16[128,768]{1,0:T(8,128)(2,1)S(1)} collective-permute-done((bf16[128,768]{1,0:T(8,128)(2,1)S(1)}, bf16[128,768]{1,0:T(8,128)(2,1)S(1)}, u32[]{:S(2)}, u32[]{:S(2)}) %collective-permute-start.7) | collective-permute-done | bytes 196640 | tf_op jit(solution)/shard_map/heads_exchange/ppermute | solution.py:74
  17.4 0.0 collective-permute-done.3.refs_5_.refs_1_
  17.4 0.0 copy-done.10
  17.4 0.0 copy-start.3
  17.4 4.8 %states.1.refs_4_ = f32[4,128,512]{2,1,0:T(8,128)S(1)} custom-call(bf16[144,256]{1,0:T(8,128)(2,1)S(1)} %get-tuple-element.41.refs_0_, bf16[144,256]{1,0:T(8,128)(2,1)S(1)} %collective-permute-done.refs_1_, bf16[144,256]{1,0:T(8,128)(2,1)S(1)} %collective-permute-done.1.refs_2_, bf16[144,256]{1,0:T(8,128)(2,1)S(1)} %collective-permute-done.2.refs_3_, ...), custom_call_target="tpu_custom_call" | custom-call | flops 4000000000 | bytes 1000000 | tf_op jit(solution)/shard_map/states/pallas_call | solution.py:451
  22.3 0.0 collective-permute-done.4.refs_2_
  22.3 0.8 collective-permute-done.5.refs_3_
  23.0 0.0 copy-done.3
  23.1 1.0 %gates.1 = (bf16[4,128,512]{2,1,0:T(8,128)(2,1)S(1)}, f32[128,2048]{1,0:T(8,128)S(1)}, bf16[128,2048]{1,0:T(8,128)(2,1)S(1)}) custom-call(bf16[128,1280]{1,0:T(8,128)(2,1)S(1)} %get-tuple-element.30.refs_4_.refs_0_, bf16[128,1280]{1,0:T(8,128)(2,1)S(1)} %collective-permute-done.3.refs_5_.refs_1_, bf16[128,512]{1,0:T(8,128)(2,1)S(1)} %collective-permute-done.4.refs_2_, ...), custom_call_target="tpu_custom_call" | custom-call | tf_op jit(solution)/shard_map/gates/pallas_call | solution.py:462
  24.0 0.2 collective-permute-start.9
  24.3 0.0 copy-start.2
  24.3 0.7 own_projection.1
  25.0 0.0 copy-start.4
  25.0 0.0 copy-start.5
  25.0 0.0 copy-start.7
  25.0 0.0 copy-start.8
  25.0 0.4 collective-permute-start.8
  25.4 0.6 collective-permute-done.9
  26.0 0.0 copy-start.1
  26.0 0.1 add_convert_fusion
  26.1 0.0 copy-start
  26.1 1.6 %collective-permute-start.10 = (bf16[128,2048]{1,0:T(8,128)(2,1)S(1)}, bf16[128,2048]{1,0:T(8,128)(2,1)S(1)}, u32[]{:S(2)}, u32[]{:S(2)}) collective-permute-start(bf16[128,2048]{1,0:T(8,128)(2,1)S(1)} %add_convert_fusion), channel_id=1, source_target_pairs={{0,16},{8,24},{16,0},{24,8},{1,17},{9,25},{17,1},{25,9},{2,18},{10... | collective-permute-start | bytes 1572872 | tf_op jit(solution)/shard_map/projection_sum/ppermute | solution.py:74
  27.7 0.0 collective-permute-done.8.refs_5_
  27.7 12.5 %collective-permute-done.10.refs_6_ = bf16[128,2048]{1,0:T(8,128)(2,1)S(1)} collective-permute-done((bf16[128,2048]{1,0:T(8,128)(2,1)S(1)}, bf16[128,2048]{1,0:T(8,128)(2,1)S(1)}, u32[]{:S(2)}, u32[]{:S(2)}) %collective-permute-start.10) | collective-permute-done | bytes 524320 | tf_op jit(solution)/shard_map/projection_sum/ppermute | solution.py:74
  40.2 0.0 copy-done.4
  40.2 0.0 copy-done.5
  40.2 0.0 copy-done.7
  40.4 0.0 copy-done.8
  40.4 1.0 %dispatch.1 = (f32[128,2048]{1,0:T(8,128)S(1)}, bf16[32,64,128]{2,1,0:T(8,128)(2,1)S(1)}, f32[128,128]{1,0:T(8,128)S(1)}) custom-call(bf16[1,128,2048]{2,1,0:T(8,128)(2,1)S(1)} %copy-done.4, f32[1,2048]{1,0:T(1,128)S(1)} %bitcast.7, s32[10,1,128]{2,1,0:T(1,128)S(1)} %bitcast.9, f32[10,1,128]{2,1,0:T(1,128)S(1)} %bitcast.10, ...), custom_call_target="tpu_custom_call" | custom-call | tf_op jit(solution)/shard_map/dispatch/pallas_call | solution.py:484
  41.4 22.2 %all_to_all.10.rows_ref = bf16[32,64,128]{2,1,0:T(8,128)(2,1)S(1)} all-to-all(bf16[32,64,128]{2,1,0:T(8,128)(2,1)S(1)} %get-tuple-element.54), channel_id=1, replica_groups=mesh['ctx'=4,'exp'=8] {'ctx','exp'}, dimensions={0} | all-to-all | bytes 1048576 | tf_op jit(solution)/shard_map/to_experts/all_to_all | solution.py:501
  63.5 0.0 copy-done.2
  63.5 0.0 copy-done.1
  63.5 0.0 copy-done
  63.5 0.0 copy-start.6
  63.5 0.0 copy-start.9
  63.5 1.6 %experts.1 = bf16[32,64,128]{2,1,0:T(8,128)(2,1)S(1)} custom-call(bf16[32,64,128]{2,1,0:T(8,128)(2,1)S(1)} %all_to_all.10.rows_ref, bf16[1,2048,512]{2,1,0:T(8,128)(2,1)S(1)} %copy-done, bf16[1,2048,512]{2,1,0:T(8,128)(2,1)S(1)} %copy-done.1, bf16[1,512,2048]{2,1,0:T(8,128)(2,1)S(1)} %copy-done.2), custom_call_target="tpu_custom_call" | custom-call | tf_op jit(solution)/shard_map/experts/pallas_call | solution.py:503
  65.1 18.4 %all_to_all.11.back_ref = bf16[32,64,128]{2,1,0:T(8,128)(2,1)S(1)} all-to-all(bf16[32,64,128]{2,1,0:T(8,128)(2,1)S(1)} %experts.1), channel_id=1, replica_groups=mesh['ctx'=4,'exp'=8] {'ctx','exp'}, dimensions={0} | all-to-all | bytes 1048576 | tf_op jit(solution)/shard_map/from_experts/all_to_all | solution.py:510
  83.6 0.0 copy-done.6
  83.6 0.0 copy-done.9
  83.6 1.7 %combine.1 = bf16[1,128,2048]{2,1,0:T(8,128)(2,1)} custom-call(f32[128,2048]{1,0:T(8,128)S(1)} %get-tuple-element.52.hidden_ref, f32[128,128]{1,0:T(8,128)S(1)} %get-tuple-element.53.table_ref, bf16[32,64,128]{2,1,0:T(8,128)(2,1)S(1)} %all_to_all.11.back_ref, s32[1,128]{1,0:T(1,128)S(1)} %copy-done.9, f32[1,2048]{1,0:T(1,128)S(1)} %bitcast.8), custom_call_target="tpu_custom_call" | custom-call | tf_op jit(solution)/shard_map/combine/pallas_call | solution.py:512
Async XLA Ops:
  1.7 4.9 %collective-permute-start = (bf16[144,256]{1,0:T(8,128)(2,1)S(1)}, bf16[144,256]{1,0:T(8,128)(2,1)S(1)}, u32[]{:S(2)}, u32[]{:S(2)}) collective-permute-start(bf16[144,256]{1,0:T(8,128)(2,1)S(1)} %get-tuple-element.32), channel_id=1, source_target_pairs={{0,8},{8,0},{16,24},{24,16},{1,9},{9,1},{17,25},{25,17},{2,10},{10... | collective-permute-start | bytes 221192 | tf_op jit(solution)/shard_map/heads_exchange/ppermute | solution.py:74
  2.2 5.4 %collective-permute-start.1 = (bf16[144,256]{1,0:T(8,128)(2,1)S(1)}, bf16[144,256]{1,0:T(8,128)(2,1)S(1)}, u32[]{:S(2)}, u32[]{:S(2)}) collective-permute-start(bf16[144,256]{1,0:T(8,128)(2,1)S(1)} %get-tuple-element.33), channel_id=1, source_target_pairs={{0,16},{8,24},{16,0},{24,8},{1,17},{9,25},{17,1},{25,9},{2,18},{10... | collective-permute-start | bytes 221192 | tf_op jit(solution)/shard_map/heads_exchange/ppermute | solution.py:74
  4.8 4.2 %collective-permute-start.2 = (bf16[144,256]{1,0:T(8,128)(2,1)S(1)}, bf16[144,256]{1,0:T(8,128)(2,1)S(1)}, u32[]{:S(2)}, u32[]{:S(2)}) collective-permute-start(bf16[144,256]{1,0:T(8,128)(2,1)S(1)} %get-tuple-element.34), channel_id=1, source_target_pairs={{0,24},{8,16},{16,8},{24,0},{1,25},{9,17},{17,9},{25,1},{2,26},{10... | collective-permute-start | bytes 221192 | tf_op jit(solution)/shard_map/heads_exchange/ppermute | solution.py:74
  4.8 11.7 %collective-permute-start.6 = (bf16[128,768]{1,0:T(8,128)(2,1)S(1)}, bf16[128,768]{1,0:T(8,128)(2,1)S(1)}, u32[]{:S(2)}, u32[]{:S(2)}) collective-permute-start(bf16[128,768]{1,0:T(8,128)(2,1)S(1)} %get-tuple-element.45), channel_id=1, source_target_pairs={{0,16},{8,24},{16,0},{24,8},{1,17},{9,25},{17,1},{25,9},{2,18},{10... | collective-permute-start | bytes 589832 | tf_op jit(solution)/shard_map/heads_exchange/ppermute | solution.py:74
  6.6 10.8 %collective-permute-start.7 = (bf16[128,768]{1,0:T(8,128)(2,1)S(1)}, bf16[128,768]{1,0:T(8,128)(2,1)S(1)}, u32[]{:S(2)}, u32[]{:S(2)}) collective-permute-start(bf16[128,768]{1,0:T(8,128)(2,1)S(1)} %get-tuple-element.46), channel_id=1, source_target_pairs={{0,24},{8,16},{16,8},{24,0},{1,25},{9,17},{17,9},{25,1},{2,26},{10... | collective-permute-start | bytes 589832 | tf_op jit(solution)/shard_map/heads_exchange/ppermute | solution.py:74
  9.0 8.4 %copy-start.10 = (f32[128]{0:T(128)S(1)}, f32[128]{0:T(128)}, u32[]{:S(2)}) copy-start(f32[128]{0:T(128)} %param.23) | copy-start | bytes 1540
  9.0 13.3 %collective-permute-start.4 = (bf16[128,512]{1,0:T(8,128)(2,1)S(1)}, bf16[128,512]{1,0:T(8,128)(2,1)S(1)}, u32[]{:S(2)}, u32[]{:S(2)}) collective-permute-start(bf16[128,512]{1,0:T(8,128)(2,1)S(1)} %get-tuple-element.39), channel_id=1, source_target_pairs={{0,16},{8,24},{16,0},{24,8},{1,17},{9,25},{17,1},{25,9},{2,18},{10... | collective-permute-start | bytes 393224 | tf_op jit(solution)/shard_map/heads_exchange/ppermute | solution.py:74
  10.5 12.5 %collective-permute-start.5 = (bf16[128,512]{1,0:T(8,128)(2,1)S(1)}, bf16[128,512]{1,0:T(8,128)(2,1)S(1)}, u32[]{:S(2)}, u32[]{:S(2)}) collective-permute-start(bf16[128,512]{1,0:T(8,128)(2,1)S(1)} %get-tuple-element.40), channel_id=1, source_target_pairs={{0,24},{8,16},{16,8},{24,0},{1,25},{9,17},{17,9},{25,1},{2,26},{10... | collective-permute-start | bytes 393224 | tf_op jit(solution)/shard_map/heads_exchange/ppermute | solution.py:74
  10.9 6.5 %collective-permute-start.3 = (bf16[128,1280]{1,0:T(8,128)(2,1)S(1)}, bf16[128,1280]{1,0:T(8,128)(2,1)S(1)}, u32[]{:S(2)}, u32[]{:S(2)}) collective-permute-start(bf16[128,1280]{1,0:T(8,128)(2,1)S(1)} %get-tuple-element.38), channel_id=1, source_target_pairs={{0,8},{8,0},{16,24},{24,16},{1,9},{9,1},{17,25},{25,17},{2,10},{10... | collective-permute-start | bytes 983048 | tf_op jit(solution)/shard_map/heads_exchange/ppermute | solution.py:74
  17.4 5.6 %copy-start.3 = (bf16[512,2048]{1,0:T(8,128)(2,1)S(1)}, bf16[512,2048]{1,0:T(8,128)(2,1)}, u32[]{:S(2)}) copy-start(bf16[512,2048]{1,0:T(8,128)(2,1)} %proj_ref.1) | copy-start | bytes 6291460
  24.0 2.0 %collective-permute-start.9 = (bf16[128,2048]{1,0:T(8,128)(2,1)S(1)}, bf16[128,2048]{1,0:T(8,128)(2,1)S(1)}, u32[]{:S(2)}, u32[]{:S(2)}) collective-permute-start(bf16[128,2048]{1,0:T(8,128)(2,1)S(1)} %get-tuple-element.51), channel_id=1, source_target_pairs={{0,8},{8,0},{16,24},{24,16},{1,9},{9,1},{17,25},{25,17},{2,10},{10... | collective-permute-start | bytes 1572872 | tf_op jit(solution)/shard_map/projection_sum/ppermute | solution.py:74
  24.3 39.2 %copy-start.2 = (bf16[1,512,2048]{2,1,0:T(8,128)(2,1)S(1)}, bf16[1,512,2048]{2,1,0:T(8,128)(2,1)}, u32[]{:S(2)}) copy-start(bf16[1,512,2048]{2,1,0:T(8,128)(2,1)} %down_ref.1) | copy-start | bytes 6291460
  25.0 15.2 %copy-start.4 = (bf16[1,128,2048]{2,1,0:T(8,128)(2,1)S(1)}, bf16[1,128,2048]{2,1,0:T(8,128)(2,1)}, u32[]{:S(2)}) copy-start(bf16[1,128,2048]{2,1,0:T(8,128)(2,1)} %refs_0_.1) | copy-start | bytes 1572868
  25.0 15.2 %copy-start.5 = (f32[2048]{0:T(1024)S(1)}, f32[2048]{0:T(1024)}, u32[]{:S(2)}) copy-start(f32[2048]{0:T(1024)} %param.26) | copy-start | bytes 24580
  25.0 15.2 %copy-start.7 = (s32[1,128,10]{1,0,2:T(1,128)S(1)}, s32[1,128,10]{1,0,2:T(1,128)}, u32[]{:S(2)}) copy-start(s32[1,128,10]{1,0,2:T(1,128)} %param.27) | copy-start | bytes 15364
  25.0 15.4 %copy-start.8 = (f32[1,128,10]{1,0,2:T(1,128)S(1)}, f32[1,128,10]{1,0,2:T(1,128)}, u32[]{:S(2)}) copy-start(f32[1,128,10]{1,0,2:T(1,128)} %param.28) | copy-start | bytes 15364
  25.0 2.7 %collective-permute-start.8 = (bf16[128,2048]{1,0:T(8,128)(2,1)S(1)}, bf16[128,2048]{1,0:T(8,128)(2,1)S(1)}, u32[]{:S(2)}, u32[]{:S(2)}) collective-permute-start(bf16[128,2048]{1,0:T(8,128)(2,1)S(1)} %get-tuple-element.49), channel_id=1, source_target_pairs={{0,8},{8,0},{16,24},{24,16},{1,9},{9,1},{17,25},{25,17},{2,10},{10... | collective-permute-start | bytes 1572872 | tf_op jit(solution)/shard_map/projection_sum/ppermute | solution.py:74
  26.0 37.5 %copy-start.1 = (bf16[1,2048,512]{2,1,0:T(8,128)(2,1)S(1)}, bf16[1,2048,512]{2,1,0:T(8,128)(2,1)}, u32[]{:S(2)}) copy-start(bf16[1,2048,512]{2,1,0:T(8,128)(2,1)} %up_ref.1) | copy-start | bytes 6291460
  26.1 37.4 %copy-start = (bf16[1,2048,512]{2,1,0:T(8,128)(2,1)S(1)}, bf16[1,2048,512]{2,1,0:T(8,128)(2,1)}, u32[]{:S(2)}) copy-start(bf16[1,2048,512]{2,1,0:T(8,128)(2,1)} %gate_ref.1) | copy-start | bytes 6291460
  26.1 14.1 %collective-permute-start.10 = (bf16[128,2048]{1,0:T(8,128)(2,1)S(1)}, bf16[128,2048]{1,0:T(8,128)(2,1)S(1)}, u32[]{:S(2)}, u32[]{:S(2)}) collective-permute-start(bf16[128,2048]{1,0:T(8,128)(2,1)S(1)} %add_convert_fusion), channel_id=1, source_target_pairs={{0,16},{8,24},{16,0},{24,8},{1,17},{9,25},{17,1},{25,9},{2,18},{10... | collective-permute-start | bytes 1572872 | tf_op jit(solution)/shard_map/projection_sum/ppermute | solution.py:74
  63.5 20.1 %copy-start.6 = (f32[2048]{0:T(1024)S(1)}, f32[2048]{0:T(1024)}, u32[]{:S(2)}) copy-start(f32[2048]{0:T(1024)} %param.33) | copy-start | bytes 24580
  63.5 20.1 %copy-start.9 = (s32[1,128]{1,0:T(1,128)S(1)}, s32[1,128]{1,0:T(1,128)}, u32[]{:S(2)}) copy-start(s32[1,128]{1,0:T(1,128)} %mask_ref.1) | copy-start | bytes 1540

commit v3 on v2

--- a/solution.py
+++ b/solution.py
@@ -74,11 +74,12 @@
     return lax.ppermute(x, "ctx", pairs)
 
 
-def pack_kernel(n, kw, vw, k_ref, q_ref, v_ref, g_ref, w_ref, d_ref, *outs):
+def pack_kernel(n, kw, vw, k_ref, w_ref, d_ref, q_ref, v_ref, g_ref, *outs):
+    local = vw // DK
+    keyed, asked, gated = outs[:n], outs[n : 2 * n], outs[2 * n :]
     me = lax.axis_index("ctx")
     tokens = k_ref.shape[1]
     heads = d_ref.shape[1]
-    local = vw // DK
     ones = (iota((tokens, tokens), 0) <= iota((tokens, tokens), 1)).astype(bf16)
     logs = jnp.log(d_ref[0])
     sums = sum(mm(piece, ones) for piece in reversed(split3(logs)))
@@ -86,24 +87,19 @@
     rates = jnp.concatenate(pieces, axis=0).astype(bf16)
     rows = AUX * kw // LANES
     row, entry = iota((rows, 6 * heads), 0), iota((rows, 6 * heads), 1)
-    outs = list(outs)
-    for route in routes(n):
+    for i, route in enumerate(routes(n)):
         to = moved(me, route, n)
         kat = pl.ds(pl.multiple_of(to * kw, LANES), kw)
-        vat = pl.ds(pl.multiple_of(to * vw, LANES), vw)
-        keyed = outs.pop(0)
-        keyed[0:tokens] = k_ref[0, :, kat]
+        keyed[i][0:tokens] = k_ref[0, :, kat]
         wanted = row // local * heads + to * local + lax.rem(row, local)
         aux = mm(((row < 6 * local) & (entry == wanted)).astype(bf16), rates)
-        for i in range(kw // LANES):
-            keyed[tokens:, i * LANES : (i + 1) * LANES] = aux[i * AUX : (i + 1) * AUX].astype(bf16)
-        asked = outs.pop(0)
-        asked[:, 0:kw] = q_ref[0, :, kat]
-        asked[:, kw : kw + vw] = v_ref[0, :, vat]
-        if route[0] == 0:
-            asked[:, kw + vw :] = g_ref[0, :, vat]
-        else:
-            outs.pop(0)[...] = g_ref[0, :, vat]
+        for at in range(kw // LANES):
+            keyed[i][tokens:, at * LANES : (at + 1) * LANES] = aux[at * AUX : (at + 1) * AUX].astype(bf16)
+        asked[i][:, 0:kw] = q_ref[0, :, kat]
+        asked[i][:, kw:] = v_ref[0, :, pl.ds(pl.multiple_of(to * vw, LANES), vw)]
+    for j, out in enumerate(gated):
+        chip = lax.rem(me // 2 + j + 1, n // 2)
+        out[...] = g_ref[0, :, pl.ds(pl.multiple_of(chip * 2 * vw, LANES), 2 * vw)]
 
 
 def head_rates(local, keyed, tokens):
@@ -183,7 +179,7 @@
 
 def state_kernel(n, kw, vw, *refs):
     keyed, asked = refs[:n], refs[n : 2 * n]
-    inv_ref, gain_ref, out_ref, kx_ref, qv_ref = refs[2 * n :]
+    inv_ref, gain_ref, keep_ref, give_ref, out_ref, kx_ref, qv_ref = refs[2 * n :]
     me = lax.axis_index("ctx")
     tokens = inv_ref.shape[-1]
     local = vw // DK
@@ -192,7 +188,7 @@
     for i, route in enumerate(routes(n)):
         block = moved(me, route, n, back=True)
         kx_ref[block] = keyed[i][...]
-        qv_ref[block] = asked[i][:, 0 : kw + vw]
+        qv_ref[block] = asked[i][...]
     row, col = iota((tokens, tokens), 0), iota((tokens, tokens), 1)
     eye = (row == col).astype(f32)
     gain = gain_ref[...]
@@ -264,51 +260,50 @@
         before = (block, made, seen, [split2(d) for d in delta])
         made = later
     finish(*before)
-
-
-def gate_kernel(n, *refs):
-    gated = refs[:n]
-    normed_ref, proj_ref, mixed_ref = refs[n : n + 3]
-    chips = n // 2
-    keeps = refs[n + 3 : n + 2 + chips]
-    gives = refs[n + 2 + chips :]
+    for j in range(n // 2):
+        keep_ref[j] = out_ref[moved(me, (j, 0), n)]
+        give_ref[j] = out_ref[moved(me, (j, 1), n)].astype(bf16)
+
+
+def chip_projection(me, keep, other, gate_ref, start, proj_ref, proj_other_ref, columns):
+    vw = keep.shape[1]
+    mixed = []
+    for heads, core in ((keep, lax.rem(me, 2)), (other, 1 - lax.rem(me, 2))):
+        gate = gate_ref[:, pl.ds(pl.multiple_of(start + core * vw, LANES), vw)].astype(f32)
+        mixed.append((heads.astype(f32) * (gate / (1.0 + jnp.exp(-gate)))).astype(bf16))
+    for at in range(0, proj_ref.shape[1], columns):
+        here = slice(at, at + columns)
+        yield here, mm(mixed[0], proj_ref[:, here]) + mm(mixed[1], proj_other_ref[:, here])
+
+
+def far_kernel(n, *refs):
+    gated = refs[: n // 2 - 1]
+    keep_ref, other_ref, proj_ref, proj_other_ref, *sums = refs[n // 2 - 1 :]
     me = lax.axis_index("ctx")
-    vw = mixed_ref.shape[2]
-    for i, route in enumerate(routes(n)):
-        block = moved(me, route, n, back=True)
-        gate = gated[i][:, gated[i].shape[1] - vw :].astype(f32)
-        mixed_ref[block] = (normed_ref[block] * (gate / (1.0 + jnp.exp(-gate)))).astype(bf16)
-    for j in range(1, chips):
-        project(mixed_ref, moved(me, (j, 1), n), proj_ref, gives[j - 1])
-        project(mixed_ref, moved(me, (j, 0), n), proj_ref, keeps[j - 1])
-
-
-def project(mixed_ref, block, proj_ref, out_ref):
-    mine = mixed_ref[block]
-    width = 512
-    for c in range(0, proj_ref.shape[1], width):
-        out_ref[:, c : c + width] = mm(mine, proj_ref[:, c : c + width]).astype(out_ref.dtype)
-
-
-def own_kernel(n, mixed_ref, proj_ref, keep_ref, give_ref):
+    for j, (gate_ref, out) in enumerate(zip(gated, sums), 1):
+        for here, part in chip_projection(me, keep_ref[j], other_ref[j], gate_ref, 0, proj_ref, proj_other_ref, 512):
+            out[:, here] = part.astype(bf16)
+
+
+def home_kernel(
+    residual_ref,
+    gate_ref,
+    keep_ref,
+    other_ref,
+    proj_ref,
+    proj_other_ref,
+    ids_ref,
+    weight_ref,
+    base_ref,
+    picker_ref,
+    table_ref,
+):
     me = lax.axis_index("ctx")
-    project(mixed_ref, moved(me, (0, 1), n), proj_ref, give_ref)
-    project(mixed_ref, me, proj_ref, keep_ref)
-
-
-def dispatch_kernel(parts, *refs):
-    residual_ref, gain_ref, ids_ref, weight_ref = refs[:4]
-    part_refs = refs[4 : 4 + parts]
-    hidden_ref, rows_ref, table_ref, flat_ref = refs[4 + parts :]
-    tokens, width = hidden_ref.shape
-    slots = table_ref.shape[0]
-    chunks = width // LANES
-    hidden = residual_ref[0].astype(f32)
-    for part in part_refs:
-        hidden = hidden + part[...].astype(f32)
-    hidden_ref[...] = hidden
-    mean = jnp.mean(hidden * hidden, axis=1, keepdims=True)
-    normed = (hidden * lax.rsqrt(mean + EPS) * gain_ref[...]).astype(bf16)
+    start = me // 2 * 2 * keep_ref.shape[2]
+    gate_ref = gate_ref.at[0]
+    for here, part in chip_projection(me, keep_ref[0], other_ref[0], gate_ref, start, proj_ref, proj_other_ref, 512):
+        base_ref[:, here] = residual_ref[0, :, here].astype(f32) + part
+    slots, tokens = table_ref.shape
     slot = iota((slots, tokens), 0)
     expert = slot // CAP
     named = jnp.zeros((slots, tokens), f32)
@@ -321,10 +316,28 @@
     rank = mm(named.astype(bf16), before)
     chosen = jnp.where(rank == lax.rem(slot, CAP).astype(f32), named, 0.0)
     table_ref[...] = chosen * weight
-    picker = chosen.astype(bf16)
+    picker_ref[...] = chosen.astype(bf16)
+
+
+def dispatch_kernel(base_ref, gain_ref, picker_ref, *refs):
+    part_refs = refs[:-3]
+    hidden_ref, rows_ref, flat_ref = refs[-3:]
+    width = hidden_ref.shape[1]
+    slots = picker_ref.shape[0]
+    chunks = width // LANES
+    squares = 0.0
     step = 512
     for c in range(0, width, step):
-        rows = mm(picker, normed[:, c : c + step])
+        total = base_ref[:, c : c + step]
+        for part in part_refs:
+            total = total + part[:, c : c + step].astype(f32)
+        hidden_ref[:, c : c + step] = total
+        squares = squares + jnp.sum(total * total, axis=1, keepdims=True)
+    scale = lax.rsqrt(squares * (1.0 / width) + EPS)
+    picker = picker_ref[...]
+    for c in range(0, width, step):
+        normed = (hidden_ref[:, c : c + step] * scale * gain_ref[:, c : c + step]).astype(bf16)
+        rows = mm(picker, normed)
         for i in range(step // LANES):
             flat_ref[pl.ds(c // LANES + i, slots, stride=chunks), :] = rows[:, i * LANES : (i + 1) * LANES]
     rows_ref[...] = flat_ref[...].astype(bf16).reshape(rows_ref.shape)
@@ -357,24 +370,26 @@
     out_ref[...] = flat_ref[...].astype(bf16).reshape(out_ref.shape)
 
 
-def combine_kernel(hidden_ref, table_ref, back_ref, mask_ref, dir_ref, out_ref, flat_ref, ret_ref):
+def combine_kernel(hidden_ref, table_ref, back_ref, mask_ref, dir_ref, out_ref, flat_ref, sum_ref):
     tokens, width = hidden_ref.shape
     slots = table_ref.shape[0]
     chunks = width // LANES
     flat_ref[...] = back_ref[...].reshape(flat_ref.shape).astype(f32)
-    for c in range(chunks):
-        got = flat_ref[pl.ds(c, slots, stride=chunks), :].astype(bf16)
-        ret_ref[0:slots, c * LANES : (c + 1) * LANES] = got
-        ret_ref[slots : 2 * slots, c * LANES : (c + 1) * LANES] = got
-    high, low = split2(table_ref[...])
-    moe = mm_tn(jnp.concatenate([high, low], axis=0), ret_ref[...])
-    combined = hidden_ref[...] + moe
+    table = jnp.concatenate(split2(table_ref[...]), axis=0)
     direction = dir_ref[...]
     unit = direction / jnp.sqrt(jnp.sum(direction * direction, axis=1, keepdims=True) + EPS)
-    along = jnp.sum(combined * unit, axis=1, keepdims=True)
     eye = iota((tokens, tokens), 0) == iota((tokens, tokens), 1)
     mask = jnp.sum(jnp.where(eye, mask_ref[...].astype(f32), 0.0), axis=1, keepdims=True)
-    out_ref[0] = (combined - (mask * along) * unit).astype(bf16)
+    along = 0.0
+    step = 256
+    for c in range(0, width, step):
+        back = jnp.concatenate(
+            [flat_ref[pl.ds(c // LANES + i, slots, stride=chunks), :].astype(bf16) for i in range(step // LANES)], axis=1
+        )
+        total = hidden_ref[:, c : c + step] + mm_tn(table, jnp.concatenate([back, back], axis=0))
+        sum_ref[:, c : c + step] = total
+        along = along + jnp.sum(total * unit[:, c : c + step], axis=1, keepdims=True)
+    out_ref[0] = (sum_ref[...] - (mask * along) * unit).astype(bf16)
 
 
 def local_part(
@@ -412,34 +427,18 @@
     with jax.named_scope("pack"):
         packed = pl.pallas_call(
             functools.partial(pack_kernel, n, kw, vw),
-            out_shape=[
-                out
-                for route in ways
-                for out in (
-                    [keyed_shape, shape((tokens, kw + 2 * vw), bf16)]
-                    if route[0] == 0
-                    else [keyed_shape, shape((tokens, kw + vw), bf16), shape((tokens, vw), bf16)]
-                )
-            ],
+            out_shape=[keyed_shape] * n
+            + [shape((tokens, kw + vw), bf16)] * n
+            + [shape((tokens, 2 * vw), bf16)] * (chips - 1),
             compiler_params=compiler_params(16),
-        )(*in_hbm(keys, queries, values, out_gate, write_rate.transpose(0, 2, 1), decay.transpose(0, 2, 1)))
+        )(*in_hbm(keys, write_rate.transpose(0, 2, 1), decay.transpose(0, 2, 1), queries, values, out_gate))
+        keyed, asked, gated = list(packed[:n]), list(packed[n : 2 * n]), packed[2 * n :]
     with jax.named_scope("heads_exchange"):
-        packed = list(packed)
-        keyed, asked, gated = [], [], []
-        for route in ways:
-            keyed.append(packed.pop(0))
-            asked.append(packed.pop(0))
-            gated.append(packed.pop(0) if route[0] else None)
         order = [i for i, route in enumerate(ways) if route[0]] + [1]
         for i in order:
             keyed[i] = send(keyed[i], ways[i], n)
         for i in order[:-1]:
             asked[i] = send(asked[i], ways[i], n)
-        keyed, late = lax.optimization_barrier((keyed, [asked[1]] + [gated[i] for i in order[:-1]]))
-        asked[1] = send(late[0], ways[1], n)
-        for i, gate in zip(order[:-1], late[1:]):
-            gated[i] = send(gate, ways[i], n)
-        gated[:2] = asked[:2]
     with jax.named_scope("block_inverses"):
         inverses = pl.pallas_call(
             functools.partial(inverse_kernel, n, local),
@@ -447,56 +446,56 @@
             compiler_params=compiler_params(16),
             cost_estimate=pl.CostEstimate(flops=6 * 10**9, bytes_accessed=10**6, transcendentals=0),
         )(*keyed)
+    with jax.named_scope("late_exchange"):
+        proj = out_proj
+        inverses, asked[1], gated = lax.optimization_barrier((inverses, asked[1], gated))
+        asked[1] = send(asked[1], ways[1], n)
+        gated = [send(gate, (j, 0), n) for j, gate in enumerate(gated, 1)]
+        proj_other = send(proj, (0, 1), n)
     with jax.named_scope("states"):
-        normed = pl.pallas_call(
+        keep, give = pl.pallas_call(
             functools.partial(state_kernel, n, kw, vw),
-            out_shape=shape((n, tokens, vw), f32),
+            out_shape=[shape((chips, tokens, vw), f32), shape((chips, tokens, vw), bf16)],
             scratch_shapes=[
+                pltpu.VMEM((n, tokens, vw), f32),
                 pltpu.VMEM((n, tokens + AUX, kw), bf16),
                 pltpu.VMEM((n, tokens, kw + vw), bf16),
             ],
             compiler_params=compiler_params(16),
             cost_estimate=pl.CostEstimate(flops=4 * 10**9, bytes_accessed=10**6, transcendentals=0),
         )(*keyed, *asked, inverses, head_gain.reshape(1, -1))
-    with jax.named_scope("gates"):
-        outs = pl.pallas_call(
-            functools.partial(gate_kernel, n),
-            out_shape=[shape((n, tokens, vw), bf16)]
-            + [shape((tokens, width), f32)] * (chips - 1)
-            + [shape((tokens, width), bf16)] * (chips - 1),
+    with jax.named_scope("far_projection"):
+        other = send(give, (0, 1), n)
+        sums = pl.pallas_call(
+            functools.partial(far_kernel, n),
+            out_shape=[shape((tokens, width), bf16)] * (chips - 1),
             compiler_params=compiler_params(16),
-        )(*gated, normed, out_proj)
-    mixed, keeps, gives = outs[0], outs[1:chips], outs[chips:]
-    with jax.named_scope("own_projection"):
-        keep, give = pl.pallas_call(
-            functools.partial(own_kernel, n),
-            out_shape=[shape((tokens, width), f32), shape((tokens, width), bf16)],
+        )(*gated, keep, other, out_proj, proj_other)
+    with jax.named_scope("projection_sum"):
+        parts = [send(part, (j, 0), n) for j, part in enumerate(sums, 1)]
+    with jax.named_scope("home"):
+        base, picker, table = pl.pallas_call(
+            home_kernel,
+            out_shape=[shape((tokens, width), f32), shape((slots, tokens), bf16), shape((slots, tokens), f32)],
             compiler_params=compiler_params(16),
-            cost_estimate=pl.CostEstimate(flops=2 * 10**9, bytes_accessed=10**6, transcendentals=0),
-        )(mixed, out_proj)
-    with jax.named_scope("projection_sum"):
-        parts = []
-        for j in range(chips - 1, 0, -1):
-            pair = keeps[j - 1] + send(gives[j - 1], (0, 1), n).astype(f32)
-            parts.append(send(pair.astype(bf16), (j, 0), n))
-        parts = [keep, send(give, (0, 1), n)] + parts
+            cost_estimate=pl.CostEstimate(flops=1000, bytes_accessed=1000, transcendentals=0),
+        )(
+            residual,
+            out_gate,
+            keep,
+            other,
+            out_proj,
+            proj_other,
+            expert_ids.transpose(2, 0, 1),
+            route_weight.transpose(2, 0, 1),
+        )
     with jax.named_scope("dispatch"):
-        hidden, rows, table = pl.pallas_call(
-            functools.partial(dispatch_kernel, len(parts)),
-            out_shape=[
-                shape((tokens, width), f32),
-                shape((devices, CAP * chunks, LANES), bf16),
-                shape((slots, tokens), f32),
-            ],
+        hidden, rows = pl.pallas_call(
+            dispatch_kernel,
+            out_shape=[shape((tokens, width), f32), shape((devices, CAP * chunks, LANES), bf16)],
             scratch_shapes=[pltpu.VMEM((slots * chunks, LANES), f32)],
             compiler_params=compiler_params(24),
-        )(
-            residual,
-            ffn_gain.reshape(1, -1),
-            expert_ids.transpose(2, 0, 1),
-            route_weight.transpose(2, 0, 1),
-            *parts,
-        )
+        )(base, ffn_gain.reshape(1, -1), picker, *parts)
     with jax.named_scope("to_experts"):
         came = lax.all_to_all(rows, ("ctx", "exp"), 0, 0, tiled=True)
     with jax.named_scope("experts"):
@@ -514,7 +513,7 @@
             out_shape=shape((1, tokens, width), bf16),
             scratch_shapes=[
                 pltpu.VMEM((slots * chunks, LANES), f32),
-                pltpu.VMEM((2 * slots, width), bf16),
+                pltpu.VMEM((tokens, width), f32),
             ],
             compiler_params=compiler_params(24),
         )(hidden, table, back, ablate_mask, direction.reshape(1, -1))

time: 85.5 us -> 83.9 us (0.981)
  starting transfers between devices: 9.27 us -> 8.35 us
    ppermute x11 -> x10, starting transfers between devices: 9.27 us -> 8.35 us  [send(): return lax.ppermute(x, 'ctx', pairs)]
    ppermute x11 -> x10, waiting for transfers between devices: 17.1 us -> 17.4 us  [send(): return lax.ppermute(x, 'ctx', pairs)]
  transfers between devices with their start and end apart: 11 -> 10, of which waited for: 6 -> 6; matrix products, arithmetic and copies ran while one was open for 0% -> 0% of each run, Pallas kernels for 13% -> 15%
where the time goes in v3:
time: 83.9 us; the launch traced here: 83.7 us
  blocking collectives  40 us (48%)
  Pallas kernels  17.7 us (21%)
  waiting for transfers between devices  17.4 us (21%)
  starting transfers between devices  8.35 us (10%)
    all_to_all x1, blocking collectives, local_part(): came = lax.all_to_all(rows, ('ctx', 'exp'), 0, 0, tiled=True)  21.6 us
    all_to_all x1, blocking collectives, local_part(): back = lax.all_to_all(done, ('ctx', 'exp'), 0, 0, tiled=True)  18.4 us
    ppermute x10, waiting for transfers between devices, send(): return lax.ppermute(x, 'ctx', pairs)  17.4 us
    ppermute x10, starting transfers between devices, send(): return lax.ppermute(x, 'ctx', pairs)  8.35 us
    pallas_call x1, Pallas kernels, local_part(): pl.pallas_call(functools.partial(inverse_kernel, n, local), out_shape=sha...  5.4 us
    pallas_call x1, Pallas kernels, local_part(): pl.pallas_call(functools.partial(state_kernel, n, kw, vw), out_shape=[sha...  4.89 us
    pallas_call x1, Pallas kernels, local_part(): pl.pallas_call(functools.partial(pack_kernel, n, kw, vw), out_shape=[keye...  1.71 us
  transfers between devices with their start and end apart: 10, of which 6 were waited for; matrix products, arithmetic and copies ran while one was open for 0% of the time, Pallas kernels for 15%

profile of v3, /device:TPU:0, one launch (start us, length us, event | category | flops | bytes accessed | tf_op | source)
XLA Modules:
  0.0 83.7 jit_solution(9490170052907694636)
XLA Ops:
  0.0 0.5 collective-permute-start.7
  0.5 1.7 %pack.1 = (bf16[144,256]{1,0:T(8,128)(2,1)S(1)}, bf16[144,256]{1,0:T(8,128)(2,1)S(1)}, bf16[144,256]{1,0:T(8,128)(2,1)S(1)}, bf16[144,256]{1,0:T(8,128)(2,1)S(1)...) custom-call(bf16[1,128,1024]{2,1,0:T(8,128)(2,1)} %k_ref.1, ...), custom_call_target="tpu_custom_call" | custom-call | tf_op jit(solution)/shard_map/pack/pallas_call | solution.py:428
  2.2 0.1 collective-permute-start
  2.3 2.9 %collective-permute-start.1 = (bf16[144,256]{1,0:T(8,128)(2,1)S(1)}, bf16[144,256]{1,0:T(8,128)(2,1)S(1)}, u32[]{:S(2)}, u32[]{:S(2)}) collective-permute-start(bf16[144,256]{1,0:T(8,128)(2,1)S(1)} %get-tuple-element.26), channel_id=1, source_target_pairs={{0,16},{8,24},{16,0},{24,8},{1,17},{9,25},{17,1},{25,9},{2,18},{10... | collective-permute-start | bytes 221192 | tf_op jit(solution)/shard_map/heads_exchange/ppermute | solution.py:74
  5.2 0.0 collective-permute-start.2
  5.2 1.4 %collective-permute-start.4 = (bf16[128,768]{1,0:T(8,128)(2,1)S(1)}, bf16[128,768]{1,0:T(8,128)(2,1)S(1)}, u32[]{:S(2)}, u32[]{:S(2)}) collective-permute-start(bf16[128,768]{1,0:T(8,128)(2,1)S(1)} %get-tuple-element.32), channel_id=1, source_target_pairs={{0,16},{8,24},{16,0},{24,8},{1,17},{9,25},{17,1},{25,9},{2,18},{10... | collective-permute-start | bytes 589832 | tf_op jit(solution)/shard_map/heads_exchange/ppermute | solution.py:74
  6.7 0.0 collective-permute-done.refs_1_
  6.7 0.3 collective-permute-start.5
  7.0 0.9 %collective-permute-done.1.refs_2_ = bf16[144,256]{1,0:T(8,128)(2,1)S(1)} collective-permute-done((bf16[144,256]{1,0:T(8,128)(2,1)S(1)}, bf16[144,256]{1,0:T(8,128)(2,1)S(1)}, u32[]{:S(2)}, u32[]{:S(2)}) %collective-permute-start.1) | collective-permute-done | bytes 73760 | tf_op jit(solution)/shard_map/heads_exchange/ppermute | solution.py:74
  7.9 1.9 %collective-permute-done.2.refs_3_ = bf16[144,256]{1,0:T(8,128)(2,1)S(1)} collective-permute-done((bf16[144,256]{1,0:T(8,128)(2,1)S(1)}, bf16[144,256]{1,0:T(8,128)(2,1)S(1)}, u32[]{:S(2)}, u32[]{:S(2)}) %collective-permute-start.2) | collective-permute-done | bytes 73760 | tf_op jit(solution)/shard_map/heads_exchange/ppermute | solution.py:74
  9.8 0.0 copy-start.11
  9.8 5.4 %block_inverses.1.refs_8_ = bf16[4,4,2,128,128]{4,3,2,1,0:T(8,128)(2,1)S(1)} custom-call(bf16[144,256]{1,0:T(8,128)(2,1)S(1)} %get-tuple-element.24.refs_0_, bf16[144,256]{1,0:T(8,128)(2,1)S(1)} %collective-permute-done.refs_1_, bf16[144,256]{1,0:T(8,128)(2,1)S(1)} %collective-permute-done.1.refs_2_, bf16[144,256]{1,0:T(8,128)(2,1)S(1)} %collective-permute-done.2.refs_3_), custom_call_target="tpu_custom_call" | custom-call | flops 6000000000 | bytes 1000000 | tf_op jit(solution)/shard_map/block_inverses/pallas_call | solution.py:443
  15.2 0.1 collective-permute-start.3
  15.3 1.9 %collective-permute-start.8 = (bf16[128,1024]{1,0:T(8,128)(2,1)S(1)}, bf16[128,1024]{1,0:T(8,128)(2,1)S(1)}, u32[]{:S(2)}, u32[]{:S(2)}) collective-permute-start(bf16[128,1024]{1,0:T(8,128)(2,1)S(1)} %get-tuple-element.39), channel_id=1, source_target_pairs={{0,16},{8,24},{16,0},{24,8},{1,17},{9,25},{17,1},{25,9},{2,18},{10... | collective-permute-start | bytes 786440 | tf_op jit(solution)/shard_map/late_exchange/ppermute | solution.py:74
  17.2 0.0 collective-permute-done.4.refs_6_
  17.2 1.0 %collective-permute-done.5.refs_7_ = bf16[128,768]{1,0:T(8,128)(2,1)S(1)} collective-permute-done((bf16[128,768]{1,0:T(8,128)(2,1)S(1)}, bf16[128,768]{1,0:T(8,128)(2,1)S(1)}, u32[]{:S(2)}, u32[]{:S(2)}) %collective-permute-start.5) | collective-permute-done | bytes 196640 | tf_op jit(solution)/shard_map/heads_exchange/ppermute | solution.py:74
  18.2 0.0 collective-permute-done.3.refs_5_
  18.2 0.0 copy-done.11
  18.2 0.0 copy-start
  18.2 4.9 %states.1 = (f32[2,128,512]{2,1,0:T(8,128)S(1)}, bf16[2,128,512]{2,1,0:T(8,128)(2,1)S(1)}) custom-call(bf16[144,256]{1,0:T(8,128)(2,1)S(1)} %get-tuple-element.24.refs_0_, bf16[144,256]{1,0:T(8,128)(2,1)S(1)} %collective-permute-done.refs_1_, bf16[144,256]{1,0:T(8,128)(2,1)S(1)} %collective-permute-done.1.refs_2_, ...), custom_call_target="tpu_custom_call" | custom-call | flops 4000000000 | bytes 1000000 | tf_op jit(solution)/shard_map/states/pallas_call | solution.py:456
  23.1 0.1 collective-permute-start.6
  23.3 0.8 collective-permute-done.8.refs_0_
  24.0 0.7 collective-permute-done.6.other_ref.refs_2_
  24.7 0.0 collective-permute-done.7.proj_other_ref.refs_4_
  24.7 0.0 copy-done
  24.7 0.0 copy-start.4
  24.7 0.0 copy-start.5
  24.7 0.0 copy-start.8
  24.7 0.0 copy-start.9
  24.8 0.8 far_projection.1
  25.6 0.9 %collective-permute-start.9 = (bf16[128,2048]{1,0:T(8,128)(2,1)S(1)}, bf16[128,2048]{1,0:T(8,128)(2,1)S(1)}, u32[]{:S(2)}, u32[]{:S(2)}) collective-permute-start(bf16[128,2048]{1,0:T(8,128)(2,1)S(1)} %far_projection.1), channel_id=1, source_target_pairs={{0,16},{8,24},{16,0},{24,8},{1,17},{9,25},{17,1},{25,9},{2,18},{10... | collective-permute-start | bytes 1572872 | tf_op jit(solution)/shard_map/projection_sum/ppermute | solution.py:74
  26.5 0.0 copy-done.4
  26.5 0.0 copy-done.5
  26.5 0.0 copy-done.8
  26.5 0.0 copy-done.9
  26.5 0.0 copy-start.6
  26.5 0.0 copy-start.2
  26.5 0.0 copy-start.3
  26.5 0.9 %home.1 = (f32[128,2048]{1,0:T(8,128)S(1)}, bf16[128,128]{1,0:T(8,128)(2,1)S(1)}, f32[128,128]{1,0:T(8,128)S(1)}) custom-call(bf16[1,128,2048]{2,1,0:T(8,128)(2,1)S(1)} %copy-done.5, bf16[1,128,2048]{2,1,0:T(8,128)(2,1)S(1)} %copy-done.4, f32[2,128,512]{2,1,0:T(8,128)S(1)} %get-tuple-element.35.keep_ref.refs_1_, ...), custom_call_target="tpu_custom_call" | custom-call | flops 1000 | bytes 1000 | tf_op jit(solution)/shard_map/home/pallas_call | solution.py:477
  27.4 0.0 copy-start.1
  27.4 12.2 %collective-permute-done.9.refs_0_ = bf16[128,2048]{1,0:T(8,128)(2,1)S(1)} collective-permute-done((bf16[128,2048]{1,0:T(8,128)(2,1)S(1)}, bf16[128,2048]{1,0:T(8,128)(2,1)S(1)}, u32[]{:S(2)}, u32[]{:S(2)}) %collective-permute-start.9) | collective-permute-done | bytes 524320 | tf_op jit(solution)/shard_map/projection_sum/ppermute | solution.py:74
  39.6 0.0 copy-done.6
  39.6 0.9 %dispatch.1 = (f32[128,2048]{1,0:T(8,128)S(1)}, bf16[32,64,128]{2,1,0:T(8,128)(2,1)S(1)}) custom-call(f32[128,2048]{1,0:T(8,128)S(1)} %get-tuple-element.37.base_ref, f32[1,2048]{1,0:T(1,128)S(1)} %bitcast.7, bf16[128,128]{1,0:T(8,128)(2,1)S(1)} %get-tuple-element.38.picker_ref, bf16[128,2048]{1,0:T(8,128)(2,1)S(1)} %collective-permute-done.9.refs_0_), custom_call_target="tpu_custom_call" | custom-call | tf_op jit(solution)/shard_map/dispatch/pallas_call | solution.py:493
  40.5 21.6 %all_to_all.10.rows_ref = bf16[32,64,128]{2,1,0:T(8,128)(2,1)S(1)} all-to-all(bf16[32,64,128]{2,1,0:T(8,128)(2,1)S(1)} %get-tuple-element.42), channel_id=1, replica_groups=mesh['ctx'=4,'exp'=8] {'ctx','exp'}, dimensions={0} | all-to-all | bytes 1048576 | tf_op jit(solution)/shard_map/to_experts/all_to_all | solution.py:500
  62.1 0.0 copy-done.2
  62.1 0.0 copy-done.3
  62.1 0.0 copy-done.1
  62.1 0.0 copy-start.7
  62.1 0.0 copy-start.10
  62.1 1.6 %experts.1 = bf16[32,64,128]{2,1,0:T(8,128)(2,1)S(1)} custom-call(bf16[32,64,128]{2,1,0:T(8,128)(2,1)S(1)} %all_to_all.10.rows_ref, bf16[1,2048,512]{2,1,0:T(8,128)(2,1)S(1)} %copy-done.1, bf16[1,2048,512]{2,1,0:T(8,128)(2,1)S(1)} %copy-done.2, bf16[1,512,2048]{2,1,0:T(8,128)(2,1)S(1)} %copy-done.3), custom_call_target="tpu_custom_call" | custom-call | tf_op jit(solution)/shard_map/experts/pallas_call | solution.py:502
  63.7 18.4 %all_to_all.11.back_ref = bf16[32,64,128]{2,1,0:T(8,128)(2,1)S(1)} all-to-all(bf16[32,64,128]{2,1,0:T(8,128)(2,1)S(1)} %experts.1), channel_id=1, replica_groups=mesh['ctx'=4,'exp'=8] {'ctx','exp'}, dimensions={0} | all-to-all | bytes 1048576 | tf_op jit(solution)/shard_map/from_experts/all_to_all | solution.py:509
  82.1 0.0 copy-done.7
  82.1 0.0 copy-done.10
  82.1 1.5 %combine.1 = bf16[1,128,2048]{2,1,0:T(8,128)(2,1)} custom-call(f32[128,2048]{1,0:T(8,128)S(1)} %get-tuple-element.40.hidden_ref, f32[128,128]{1,0:T(8,128)S(1)} %get-tuple-element.41.table_ref, bf16[32,64,128]{2,1,0:T(8,128)(2,1)S(1)} %all_to_all.11.back_ref, s32[1,128]{1,0:T(1,128)S(1)} %copy-done.10, f32[1,2048]{1,0:T(1,128)S(1)} %bitcast.8), custom_call_target="tpu_custom_call" | custom-call | tf_op jit(solution)/shard_map/combine/pallas_call | solution.py:511
Async XLA Ops:
  0.0 24.7 %collective-permute-start.7 = (bf16[512,2048]{1,0:T(8,128)(2,1)}, bf16[512,2048]{1,0:T(8,128)(2,1)S(1)}, u32[]{:S(2)}, u32[]{:S(2)}) collective-permute-start(bf16[512,2048]{1,0:T(8,128)(2,1)} %refs_3_.1), channel_id=1, source_target_pairs={{0,8},{8,0},{16,24},{24,16},{1,9},{9,1},{17,25},{25,17},{2,10},{10... | collective-permute-start | bytes 6291464 | tf_op jit(solution)/shard_map/late_exchange/ppermute | solution.py:74
  2.2 4.5 %collective-permute-start = (bf16[144,256]{1,0:T(8,128)(2,1)S(1)}, bf16[144,256]{1,0:T(8,128)(2,1)S(1)}, u32[]{:S(2)}, u32[]{:S(2)}) collective-permute-start(bf16[144,256]{1,0:T(8,128)(2,1)S(1)} %get-tuple-element.25), channel_id=1, source_target_pairs={{0,8},{8,0},{16,24},{24,16},{1,9},{9,1},{17,25},{25,17},{2,10},{10... | collective-permute-start | bytes 221192 | tf_op jit(solution)/shard_map/heads_exchange/ppermute | solution.py:74
  2.3 5.6 %collective-permute-start.1 = (bf16[144,256]{1,0:T(8,128)(2,1)S(1)}, bf16[144,256]{1,0:T(8,128)(2,1)S(1)}, u32[]{:S(2)}, u32[]{:S(2)}) collective-permute-start(bf16[144,256]{1,0:T(8,128)(2,1)S(1)} %get-tuple-element.26), channel_id=1, source_target_pairs={{0,16},{8,24},{16,0},{24,8},{1,17},{9,25},{17,1},{25,9},{2,18},{10... | collective-permute-start | bytes 221192 | tf_op jit(solution)/shard_map/heads_exchange/ppermute | solution.py:74
  5.2 4.6 %collective-permute-start.2 = (bf16[144,256]{1,0:T(8,128)(2,1)S(1)}, bf16[144,256]{1,0:T(8,128)(2,1)S(1)}, u32[]{:S(2)}, u32[]{:S(2)}) collective-permute-start(bf16[144,256]{1,0:T(8,128)(2,1)S(1)} %get-tuple-element.27), channel_id=1, source_target_pairs={{0,24},{8,16},{16,8},{24,0},{1,25},{9,17},{17,9},{25,1},{2,26},{10... | collective-permute-start | bytes 221192 | tf_op jit(solution)/shard_map/heads_exchange/ppermute | solution.py:74
  5.2 12.0 %collective-permute-start.4 = (bf16[128,768]{1,0:T(8,128)(2,1)S(1)}, bf16[128,768]{1,0:T(8,128)(2,1)S(1)}, u32[]{:S(2)}, u32[]{:S(2)}) collective-permute-start(bf16[128,768]{1,0:T(8,128)(2,1)S(1)} %get-tuple-element.32), channel_id=1, source_target_pairs={{0,16},{8,24},{16,0},{24,8},{1,17},{9,25},{17,1},{25,9},{2,18},{10... | collective-permute-start | bytes 589832 | tf_op jit(solution)/shard_map/heads_exchange/ppermute | solution.py:74
  6.7 11.5 %collective-permute-start.5 = (bf16[128,768]{1,0:T(8,128)(2,1)S(1)}, bf16[128,768]{1,0:T(8,128)(2,1)S(1)}, u32[]{:S(2)}, u32[]{:S(2)}) collective-permute-start(bf16[128,768]{1,0:T(8,128)(2,1)S(1)} %get-tuple-element.33), channel_id=1, source_target_pairs={{0,24},{8,16},{16,8},{24,0},{1,25},{9,17},{17,9},{25,1},{2,26},{10... | collective-permute-start | bytes 589832 | tf_op jit(solution)/shard_map/heads_exchange/ppermute | solution.py:74
  9.8 8.4 %copy-start.11 = (f32[128]{0:T(128)S(1)}, f32[128]{0:T(128)}, u32[]{:S(2)}) copy-start(f32[128]{0:T(128)} %param.23) | copy-start | bytes 1540
  15.2 3.0 %collective-permute-start.3 = (bf16[128,768]{1,0:T(8,128)(2,1)S(1)}, bf16[128,768]{1,0:T(8,128)(2,1)S(1)}, u32[]{:S(2)}, u32[]{:S(2)}) collective-permute-start(bf16[128,768]{1,0:T(8,128)(2,1)S(1)} %get-tuple-element.31), channel_id=1, source_target_pairs={{0,8},{8,0},{16,24},{24,16},{1,9},{9,1},{17,25},{25,17},{2,10},{10... | collective-permute-start | bytes 589832 | tf_op jit(solution)/shard_map/late_exchange/ppermute | solution.py:74
  15.3 8.7 %collective-permute-start.8 = (bf16[128,1024]{1,0:T(8,128)(2,1)S(1)}, bf16[128,1024]{1,0:T(8,128)(2,1)S(1)}, u32[]{:S(2)}, u32[]{:S(2)}) collective-permute-start(bf16[128,1024]{1,0:T(8,128)(2,1)S(1)} %get-tuple-element.39), channel_id=1, source_target_pairs={{0,16},{8,24},{16,0},{24,8},{1,17},{9,25},{17,1},{25,9},{2,18},{10... | collective-permute-start | bytes 786440 | tf_op jit(solution)/shard_map/late_exchange/ppermute | solution.py:74
  18.2 6.5 %copy-start = (bf16[512,2048]{1,0:T(8,128)(2,1)S(1)}, bf16[512,2048]{1,0:T(8,128)(2,1)}, u32[]{:S(2)}) copy-start(bf16[512,2048]{1,0:T(8,128)(2,1)} %refs_3_.1) | copy-start | bytes 6291460
  23.1 1.6 %collective-permute-start.6 = (bf16[2,128,512]{2,1,0:T(8,128)(2,1)S(1)}, bf16[2,128,512]{2,1,0:T(8,128)(2,1)S(1)}, u32[]{:S(2)}, u32[]{:S(2)}) collective-permute-start(bf16[2,128,512]{2,1,0:T(8,128)(2,1)S(1)} %get-tuple-element.36), channel_id=1, source_target_pairs={{0,8},{8,0},{16,24},{24,16},{1,9},{9,1},{17,25},{25,17},{2,10},{10... | collective-permute-start | bytes 786440 | tf_op jit(solution)/shard_map/far_projection/ppermute | solution.py:74
  24.7 1.7 %copy-start.4 = (bf16[1,128,2048]{2,1,0:T(8,128)(2,1)S(1)}, bf16[1,128,2048]{2,1,0:T(8,128)(2,1)}, u32[]{:S(2)}) copy-start(bf16[1,128,2048]{2,1,0:T(8,128)(2,1)} %gate_ref.2) | copy-start | bytes 1572868
  24.7 1.7 %copy-start.5 = (bf16[1,128,2048]{2,1,0:T(8,128)(2,1)S(1)}, bf16[1,128,2048]{2,1,0:T(8,128)(2,1)}, u32[]{:S(2)}) copy-start(bf16[1,128,2048]{2,1,0:T(8,128)(2,1)} %residual_ref.1) | copy-start | bytes 1572868
  24.7 1.7 %copy-start.8 = (s32[1,128,10]{1,0,2:T(1,128)S(1)}, s32[1,128,10]{1,0,2:T(1,128)}, u32[]{:S(2)}) copy-start(s32[1,128,10]{1,0,2:T(1,128)} %param.27) | copy-start | bytes 15364
  24.7 1.7 %copy-start.9 = (f32[1,128,10]{1,0,2:T(1,128)S(1)}, f32[1,128,10]{1,0,2:T(1,128)}, u32[]{:S(2)}) copy-start(f32[1,128,10]{1,0,2:T(1,128)} %param.28) | copy-start | bytes 15364
  25.6 14.0 %collective-permute-start.9 = (bf16[128,2048]{1,0:T(8,128)(2,1)S(1)}, bf16[128,2048]{1,0:T(8,128)(2,1)S(1)}, u32[]{:S(2)}, u32[]{:S(2)}) collective-permute-start(bf16[128,2048]{1,0:T(8,128)(2,1)S(1)} %far_projection.1), channel_id=1, source_target_pairs={{0,16},{8,24},{16,0},{24,8},{1,17},{9,25},{17,1},{25,9},{2,18},{10... | collective-permute-start | bytes 1572872 | tf_op jit(solution)/shard_map/projection_sum/ppermute | solution.py:74
  26.5 13.1 %copy-start.6 = (f32[2048]{0:T(1024)S(1)}, f32[2048]{0:T(1024)}, u32[]{:S(2)}) copy-start(f32[2048]{0:T(1024)} %param.26) | copy-start | bytes 24580
  26.5 35.6 %copy-start.2 = (bf16[1,2048,512]{2,1,0:T(8,128)(2,1)S(1)}, bf16[1,2048,512]{2,1,0:T(8,128)(2,1)}, u32[]{:S(2)}) copy-start(bf16[1,2048,512]{2,1,0:T(8,128)(2,1)} %up_ref.1) | copy-start | bytes 6291460
  26.5 35.6 %copy-start.3 = (bf16[1,512,2048]{2,1,0:T(8,128)(2,1)S(1)}, bf16[1,512,2048]{2,1,0:T(8,128)(2,1)}, u32[]{:S(2)}) copy-start(bf16[1,512,2048]{2,1,0:T(8,128)(2,1)} %down_ref.1) | copy-start | bytes 6291460
  27.4 34.7 %copy-start.1 = (bf16[1,2048,512]{2,1,0:T(8,128)(2,1)S(1)}, bf16[1,2048,512]{2,1,0:T(8,128)(2,1)}, u32[]{:S(2)}) copy-start(bf16[1,2048,512]{2,1,0:T(8,128)(2,1)} %gate_ref.3) | copy-start | bytes 6291460
  62.1 20.1 %copy-start.7 = (f32[2048]{0:T(1024)S(1)}, f32[2048]{0:T(1024)}, u32[]{:S(2)}) copy-start(f32[2048]{0:T(1024)} %param.33) | copy-start | bytes 24580
  62.1 20.1 %copy-start.10 = (s32[1,128]{1,0:T(1,128)S(1)}, s32[1,128]{1,0:T(1,128)}, u32[]{:S(2)}) copy-start(s32[1,128]{1,0:T(1,128)} %mask_ref.1) | copy-start | bytes 1540

commit v4 on v3

--- a/solution.py
+++ b/solution.py
@@ -107,10 +107,21 @@
         [keyed[tokens:, i * LANES : (i + 1) * LANES] for i in range(keyed.shape[1] // LANES)], axis=0
     )
     row, col = iota((aux.shape[0], LANES), 0), iota((aux.shape[0], LANES), 1)
-    total = (
-        (row < 6 * local) & (col < 2 * local) & (lax.rem(row, local) == lax.rem(col, local)) & (row // (3 * local) == col // local)
-    ).astype(bf16)
-    return mm_tn(aux, total), mm_tn(total, aux)
+    same = (row < 6 * local) & (lax.rem(row, local) == lax.rem(col, local)) & (row // (3 * local) == col // local)
+    return aux, (same & (col < 2 * local)).astype(bf16)
+
+
+def both_halves(x):
+    return jnp.concatenate(split2(x), axis=1)
+
+
+def mm3_held(held, b):
+    return mm(jnp.concatenate([held, held[:, : held.shape[1] // 2]], axis=1), b)
+
+
+def stacked(x):
+    high, low = split2(x)
+    return jnp.concatenate([high, high, low], axis=0)
 
 
 def inverse_scale(raw):
@@ -119,27 +130,38 @@
 
 
 def inverse_kernel(n, local, *refs):
-    keyed, inv_ref = refs[:n], refs[n]
+    keyed = refs[:n]
+    value_ref, erase_ref, key_ref, row_ref = refs[n:]
     me = lax.axis_index("ctx")
-    tokens = inv_ref.shape[-1]
+    tokens = value_ref.shape[2]
     group = local * DK // keyed[0].shape[1]
     row, col = iota((tokens, tokens), 0), iota((tokens, tokens), 1)
     apart = lax.bitwise_xor(row, col)
     eye = (row == col).astype(f32)
-    systems = []
-    for piece in keyed:
-        as_cols, as_rows = head_rates(local, piece, tokens)
+    systems, scales = [], []
+    for i, route in enumerate(routes(n)):
+        block = moved(me, route, n, back=True)
+        aux, total = head_rates(local, keyed[i], tokens)
+        as_cols, as_rows = mm_tn(aux, total), mm_tn(total, aux)
+        down, up = jnp.exp(as_rows), jnp.exp(-as_rows)
+        left = jnp.exp(as_rows[:, tokens - 1 :] - as_rows)
+        down_cols = jnp.exp(as_cols)
         for g in range(local // group):
-            k = piece[0:tokens, g * DK : (g + 1) * DK]
+            k = keyed[i][0:tokens, g * DK : (g + 1) * DK]
+            k_t = k.astype(f32).T
             dots = mm_nt(k, k)
             diag = dots * eye
             k_row = lax.rsqrt(jnp.sum(diag, axis=0, keepdims=True) + EPS)
             k_col = lax.rsqrt(jnp.sum(diag, axis=1, keepdims=True) + EPS)
-            dots = jnp.where(row > col, dots * k_row * k_col, 0.0)
+            dots = jnp.where(row > col, dots * k_row, 0.0)
             for h in range(g * group, (g + 1) * group):
-                gap = as_cols[:, h : h + 1] - as_rows[h : h + 1, :]
-                write = as_cols[:, local + h : local + h + 1]
-                systems.append(write * jnp.exp(jnp.minimum(gap, 0.0)) * dots)
+                write = as_rows[local + h : local + h + 1]
+                scale = as_cols[:, local + h : local + h + 1] * down_cols[:, h : h + 1] * k_col
+                systems.append(scale * (up[h : h + 1] * dots))
+                scales.append((write, write * down[h : h + 1] * k_row))
+                key_ref[block, h] = both_halves(k_t * (left[h : h + 1] * k_row))
+                row_ref[block, h, 0:1] = up[h : h + 1] * k_row
+                row_ref[block, h, 1:2] = jnp.broadcast_to(down[h : h + 1, tokens - 1 :], (1, tokens))
     near = [jnp.where(apart < 16, s, 0.0) for s in systems]
     power = [split2(s) for s in near]
     inverse = [eye - s for s in near]
@@ -165,9 +187,9 @@
     for i, route in enumerate(routes(n)):
         block = moved(me, route, n, back=True)
         for h in range(local):
-            hi, lo = split2(inverse[i * local + h])
-            inv_ref[block, h, 0] = hi
-            inv_ref[block, h, 1] = lo
+            for_values, for_state = scales[i * local + h]
+            value_ref[block, h] = both_halves(inverse[i * local + h] * for_values)
+            erase_ref[block, h] = both_halves(inverse[i * local + h] * for_state)
 
 
 def widen(x, size):
@@ -179,9 +201,9 @@
 
 def state_kernel(n, kw, vw, *refs):
     keyed, asked = refs[:n], refs[n : 2 * n]
-    inv_ref, gain_ref, keep_ref, give_ref, out_ref, kx_ref, qv_ref = refs[2 * n :]
+    value_ref, erase_ref, key_ref, row_ref, gain_ref, keep_ref, give_ref, out_ref, kx_ref, qv_ref = refs[2 * n :]
     me = lax.axis_index("ctx")
-    tokens = inv_ref.shape[-1]
+    tokens = value_ref.shape[2]
     local = vw // DK
     group = vw // kw
     all_heads = range(local)
@@ -190,74 +212,57 @@
         kx_ref[block] = keyed[i][...]
         qv_ref[block] = asked[i][...]
     row, col = iota((tokens, tokens), 0), iota((tokens, tokens), 1)
-    eye = (row == col).astype(f32)
     gain = gain_ref[...]
 
     def prepare(block):
-        as_cols, as_rows = head_rates(local, kx_ref.at[block], tokens)
-        cumulative = jnp.exp(as_cols)
-        last = as_cols[tokens - 1 : tokens]
-        ends = jnp.exp(last)
-        kept = jnp.exp(last - as_cols)
+        aux, total = head_rates(local, kx_ref.at[block], tokens)
+        down_cols = jnp.exp(mm_tn(aux, total))
         made = []
         for g in range(local // group):
             k = kx_ref[block, 0:tokens, g * DK : (g + 1) * DK]
             q = qv_ref[block, :, g * DK : (g + 1) * DK]
-            k_col = inverse_scale(k)
             q_col = inverse_scale(q) * DK ** (-0.5)
-            k_row = jnp.sum(eye * k_col, axis=0, keepdims=True)
-            dots = jnp.where(row >= col, mm_nt(q, k) * k_row * q_col, 0.0)
+            dots = jnp.where(row >= col, mm_nt(q, k), 0.0)
             for h in range(g * group, (g + 1) * group):
-                gap = as_cols[:, h : h + 1] - as_rows[h : h + 1, :]
-                scores = split2(jnp.exp(jnp.minimum(gap, 0.0)) * dots)
-                write = as_cols[:, local + h : local + h + 1]
-                cum = cumulative[:, h : h + 1]
+                v = qv_ref[block, :, kw + h * DK : kw + (h + 1) * DK]
                 made.append(
                     dict(
-                        k=k,
-                        q=q,
-                        scores=scores,
-                        write=write,
-                        erase=write * cum * k_col,
-                        ask=cum * q_col,
-                        kept=kept[:, h : h + 1] * k_col,
-                        end=ends[:, h : h + 1],
+                        k=jnp.concatenate([k, k], axis=1),
+                        q=jnp.concatenate([q, q], axis=1),
+                        scores=both_halves(dots * row_ref[block, h, 0:1]),
+                        scale=down_cols[:, h : h + 1] * q_col,
+                        written=mm(value_ref[block, h], jnp.concatenate([v, v], axis=0)),
                     )
                 )
         return made
 
-    def finish(block, made, seen, delta):
+    def finish(block, made, held, delta):
         for h in all_heads:
-            out = mm3(made[h]["scores"], delta[h])
-            if block > 0:
-                out = out + made[h]["ask"] * seen[h][tokens:]
+            out = mm3_held(made[h]["scores"], delta[h])
+            if held is not None:
+                out = out + mm(made[h]["q"], held[h])
+            out = made[h]["scale"] * out
             mean = jnp.mean(out * out, axis=1, keepdims=True)
             out_ref[block, :, h * DK : (h + 1) * DK] = out * lax.rsqrt(mean + EPS) * gain
 
     states, before, made = None, None, prepare(0)
     for block in range(n):
-        rhs = [
-            m["write"] * qv_ref[block, :, kw + h * DK : kw + (h + 1) * DK].astype(f32) for h, m in enumerate(made)
-        ]
-        seen = None
+        held = None
+        delta = [m["written"] for m in made]
         if block > 0:
-            both = [jnp.concatenate([m["k"], m["q"]], axis=0) for m in made]
-            seen = [
-                mm(jnp.concatenate([b, b], axis=1), jnp.concatenate(split2(s), axis=0)) for b, s in zip(both, states)
-            ]
-        if before is not None:
+            held = [jnp.concatenate(split2(s), axis=0) for s in states]
+            seen = [mm(m["k"], s) for m, s in zip(made, held)]
             finish(*before)
-        if block > 0:
-            rhs = [r - m["erase"] * s[:tokens] for r, m, s in zip(rhs, made, seen)]
-        delta = [mm3((inv_ref[block, h, 0], inv_ref[block, h, 1]), split2(rhs[h])) for h in all_heads]
+            delta = [d - mm3_held(erase_ref[block, h], stacked(seen[h])) for h, d in enumerate(delta)]
         later = prepare(block + 1) if block < n - 1 else None
+        delta = [stacked(d) for d in delta]
         if block < n - 1:
-            grown = [
-                mm_tn(jnp.concatenate([m["k"], m["k"]], axis=0), jnp.concatenate(split2(m["kept"] * d), axis=0))
-                for m, d in zip(made, delta)
-            ]
-            states = grown if block == 0 else [m["end"] * s + g for m, s, g in zip(made, states, grown)]
-        before = (block, made, seen, [split2(d) for d in delta])
+            grown = [mm3_held(key_ref[block, h], delta[h]) for h in all_heads]
+            if block == 0:
+                states = grown
+            else:
+                states = [row_ref[block, h, 1:2] * states[h] + grown[h] for h in all_heads]
+        before = (block, made, held, delta)
         made = later
     finish(*before)
     for j in range(n // 2):
@@ -440,15 +445,16 @@
         for i in order[:-1]:
             asked[i] = send(asked[i], ways[i], n)
     with jax.named_scope("block_inverses"):
+        wide = shape((n, local, tokens, 2 * tokens), bf16)
         inverses = pl.pallas_call(
             functools.partial(inverse_kernel, n, local),
-            out_shape=shape((n, local, 2, tokens, tokens), bf16),
+            out_shape=[wide, wide, shape((n, local, DK, 2 * tokens), bf16), shape((n, local, 8, tokens), f32)],
             compiler_params=compiler_params(16),
             cost_estimate=pl.CostEstimate(flops=6 * 10**9, bytes_accessed=10**6, transcendentals=0),
         )(*keyed)
     with jax.named_scope("late_exchange"):
         proj = out_proj
-        inverses, asked[1], gated = lax.optimization_barrier((inverses, asked[1], gated))
+        keyed, asked[1], gated = lax.optimization_barrier((keyed, asked[1], gated))
         asked[1] = send(asked[1], ways[1], n)
         gated = [send(gate, (j, 0), n) for j, gate in enumerate(gated, 1)]
         proj_other = send(proj, (0, 1), n)
@@ -463,7 +469,7 @@
             ],
             compiler_params=compiler_params(16),
             cost_estimate=pl.CostEstimate(flops=4 * 10**9, bytes_accessed=10**6, transcendentals=0),
-        )(*keyed, *asked, inverses, head_gain.reshape(1, -1))
+        )(*keyed, *asked, *inverses, head_gain.reshape(1, -1))
     with jax.named_scope("far_projection"):
         other = send(give, (0, 1), n)
         sums = pl.pallas_call(

time: 83.9 us -> 82.4 us (0.982)
  Pallas kernels: 17.7 us -> 15.5 us
    pallas_call x1, Pallas kernels: 4.89 us -> 2.78 us  [local_part(): pl.pallas_call(functools.partial(state_kernel, n, kw, vw), out_shape=[sha...]
  transfers between devices with their start and end apart: 10 -> 10, of which waited for: 6 -> 5; matrix products, arithmetic and copies ran while one was open for 0% -> 0% of each run, Pallas kernels for 15% -> 13%
where the time goes in v4:
time: 82.4 us; the launch traced here: 82.2 us
  blocking collectives  39.6 us (48%)
  waiting for transfers between devices  18.1 us (22%)
  Pallas kernels  15.5 us (19%)
  starting transfers between devices  8.77 us (11%)
    all_to_all x1, blocking collectives, local_part(): came = lax.all_to_all(rows, ('ctx', 'exp'), 0, 0, tiled=True)  21.2 us
    all_to_all x1, blocking collectives, local_part(): back = lax.all_to_all(done, ('ctx', 'exp'), 0, 0, tiled=True)  18.4 us
    ppermute x10, waiting for transfers between devices, send(): return lax.ppermute(x, 'ctx', pairs)  18.1 us
    ppermute x10, starting transfers between devices, send(): return lax.ppermute(x, 'ctx', pairs)  8.77 us
    pallas_call x1, Pallas kernels, local_part(): pl.pallas_call(functools.partial(inverse_kernel, n, local), out_shape=[wi...  5.48 us
    pallas_call x1, Pallas kernels, local_part(): pl.pallas_call(functools.partial(state_kernel, n, kw, vw), out_shape=[sha...  2.78 us
    pallas_call x1, Pallas kernels, local_part(): pl.pallas_call(functools.partial(pack_kernel, n, kw, vw), out_shape=[keye...  1.71 us
  transfers between devices with their start and end apart: 10, of which 5 were waited for; matrix products, arithmetic and copies ran while one was open for 0% of the time, Pallas kernels for 13%

profile of v4, /device:TPU:0, one launch (start us, length us, event | category | flops | bytes accessed | tf_op | source)
XLA Modules:
  0.0 82.2 jit_solution(957490175436305153)
XLA Ops:
  0.0 0.5 collective-permute-start.7
  0.5 1.7 %pack.1 = (bf16[144,256]{1,0:T(8,128)(2,1)S(1)}, bf16[144,256]{1,0:T(8,128)(2,1)S(1)}, bf16[144,256]{1,0:T(8,128)(2,1)S(1)}, bf16[144,256]{1,0:T(8,128)(2,1)S(1)...) custom-call(bf16[1,128,1024]{2,1,0:T(8,128)(2,1)} %k_ref.1, ...), custom_call_target="tpu_custom_call" | custom-call | tf_op jit(solution)/shard_map/pack/pallas_call | solution.py:433
  2.2 0.1 collective-permute-start
  2.3 2.9 %collective-permute-start.1 = (bf16[144,256]{1,0:T(8,128)(2,1)S(1)}, bf16[144,256]{1,0:T(8,128)(2,1)S(1)}, u32[]{:S(2)}, u32[]{:S(2)}) collective-permute-start(bf16[144,256]{1,0:T(8,128)(2,1)S(1)} %get-tuple-element.33), channel_id=1, source_target_pairs={{0,16},{8,24},{16,0},{24,8},{1,17},{9,25},{17,1},{25,9},{2,18},{10... | collective-permute-start | bytes 221192 | tf_op jit(solution)/shard_map/heads_exchange/ppermute | solution.py:74
  5.2 0.0 collective-permute-start.2
  5.2 1.4 %collective-permute-start.4 = (bf16[128,768]{1,0:T(8,128)(2,1)S(1)}, bf16[128,768]{1,0:T(8,128)(2,1)S(1)}, u32[]{:S(2)}, u32[]{:S(2)}) collective-permute-start(bf16[128,768]{1,0:T(8,128)(2,1)S(1)} %get-tuple-element.43), channel_id=1, source_target_pairs={{0,16},{8,24},{16,0},{24,8},{1,17},{9,25},{17,1},{25,9},{2,18},{10... | collective-permute-start | bytes 589832 | tf_op jit(solution)/shard_map/heads_exchange/ppermute | solution.py:74
  6.7 0.0 collective-permute-done.refs_1_
  6.7 0.3 collective-permute-start.5
  7.0 0.9 %collective-permute-done.1.refs_2_ = bf16[144,256]{1,0:T(8,128)(2,1)S(1)} collective-permute-done((bf16[144,256]{1,0:T(8,128)(2,1)S(1)}, bf16[144,256]{1,0:T(8,128)(2,1)S(1)}, u32[]{:S(2)}, u32[]{:S(2)}) %collective-permute-start.1) | collective-permute-done | bytes 73760 | tf_op jit(solution)/shard_map/heads_exchange/ppermute | solution.py:74
  7.9 1.9 %collective-permute-done.2.refs_3_ = bf16[144,256]{1,0:T(8,128)(2,1)S(1)} collective-permute-done((bf16[144,256]{1,0:T(8,128)(2,1)S(1)}, bf16[144,256]{1,0:T(8,128)(2,1)S(1)}, u32[]{:S(2)}, u32[]{:S(2)}) %collective-permute-start.2) | collective-permute-done | bytes 73760 | tf_op jit(solution)/shard_map/heads_exchange/ppermute | solution.py:74
  9.8 0.0 copy-start.11
  9.8 0.1 collective-permute-start.3
  9.9 1.9 %collective-permute-start.8 = (bf16[128,1024]{1,0:T(8,128)(2,1)S(1)}, bf16[128,1024]{1,0:T(8,128)(2,1)S(1)}, u32[]{:S(2)}, u32[]{:S(2)}) collective-permute-start(bf16[128,1024]{1,0:T(8,128)(2,1)S(1)} %get-tuple-element.53), channel_id=1, source_target_pairs={{0,16},{8,24},{16,0},{24,8},{1,17},{9,25},{17,1},{25,9},{2,18},{10... | collective-permute-start | bytes 786440 | tf_op jit(solution)/shard_map/late_exchange/ppermute | solution.py:74
  11.8 5.5 %block_inverses.1 = (bf16[4,4,128,256]{3,2,1,0:T(8,128)(2,1)S(1)}, bf16[4,4,128,256]{3,2,1,0:T(8,128)(2,1)S(1)}, bf16[4,4,128,256]{3,2,1,0:T(8,128)(2,1)S(1)}, f32[4,4,8,128]{3,2,1,0:T(8,128)S(1)}) custom-call(bf16[144,256]{1,0:T(8,128)(2,1)S(1)} %get-tuple-element.37.refs_0_, bf16[144,256]{1,0:T(8,128)(2,1)S(1)} %collective-permute-done.refs_1_, ...), custom_call_target="tpu_custom_call" | custom-call | flops 6000000000 | bytes 1000000 | tf_op jit(solution)/shard_map/block_inverses/pallas_call | solution.py:449
  17.3 0.0 collective-permute-done.4.refs_6_
  17.3 1.0 %collective-permute-done.5.refs_7_ = bf16[128,768]{1,0:T(8,128)(2,1)S(1)} collective-permute-done((bf16[128,768]{1,0:T(8,128)(2,1)S(1)}, bf16[128,768]{1,0:T(8,128)(2,1)S(1)}, u32[]{:S(2)}, u32[]{:S(2)}) %collective-permute-start.5) | collective-permute-done | bytes 196640 | tf_op jit(solution)/shard_map/heads_exchange/ppermute | solution.py:74
  18.2 0.0 collective-permute-done.3.refs_5_
  18.2 0.0 copy-done.11
  18.2 0.0 copy-start
  18.2 2.8 %states.1 = (f32[2,128,512]{2,1,0:T(8,128)S(1)}, bf16[2,128,512]{2,1,0:T(8,128)(2,1)S(1)}) custom-call(bf16[144,256]{1,0:T(8,128)(2,1)S(1)} %get-tuple-element.37.refs_0_, bf16[144,256]{1,0:T(8,128)(2,1)S(1)} %collective-permute-done.refs_1_, bf16[144,256]{1,0:T(8,128)(2,1)S(1)} %collective-permute-done.1.refs_2_, ...), custom_call_target="tpu_custom_call" | custom-call | flops 4000000000 | bytes 1000000 | tf_op jit(solution)/shard_map/states/pallas_call | solution.py:462
  21.0 0.1 collective-permute-start.6
  21.2 2.6 %collective-permute-done.8.refs_0_ = bf16[128,1024]{1,0:T(8,128)(2,1)S(1)} collective-permute-done((bf16[128,1024]{1,0:T(8,128)(2,1)S(1)}, bf16[128,1024]{1,0:T(8,128)(2,1)S(1)}, u32[]{:S(2)}, u32[]{:S(2)}) %collective-permute-start.8) | collective-permute-done | bytes 262176 | tf_op jit(solution)/shard_map/late_exchange/ppermute | solution.py:74
  23.8 0.0 collective-permute-done.6.other_ref.refs_2_
  23.8 0.0 collective-permute-done.7.proj_other_ref.refs_4_
  23.8 0.0 copy-done
  23.8 0.0 copy-start.4
  23.8 0.0 copy-start.5
  23.8 0.0 copy-start.8
  23.8 0.0 copy-start.9
  23.9 0.8 far_projection.1
  24.7 1.4 %collective-permute-start.9 = (bf16[128,2048]{1,0:T(8,128)(2,1)S(1)}, bf16[128,2048]{1,0:T(8,128)(2,1)S(1)}, u32[]{:S(2)}, u32[]{:S(2)}) collective-permute-start(bf16[128,2048]{1,0:T(8,128)(2,1)S(1)} %far_projection.1), channel_id=1, source_target_pairs={{0,16},{8,24},{16,0},{24,8},{1,17},{9,25},{17,1},{25,9},{2,18},{10... | collective-permute-start | bytes 1572872 | tf_op jit(solution)/shard_map/projection_sum/ppermute | solution.py:74
  26.0 0.0 copy-done.4
  26.0 0.0 copy-done.5
  26.0 0.0 copy-done.8
  26.0 0.0 copy-done.9
  26.0 0.0 copy-start.6
  26.1 0.0 copy-start.2
  26.1 0.0 copy-start.3
  26.1 0.9 %home.1 = (f32[128,2048]{1,0:T(8,128)S(1)}, bf16[128,128]{1,0:T(8,128)(2,1)S(1)}, f32[128,128]{1,0:T(8,128)S(1)}) custom-call(bf16[1,128,2048]{2,1,0:T(8,128)(2,1)S(1)} %copy-done.5, bf16[1,128,2048]{2,1,0:T(8,128)(2,1)S(1)} %copy-done.4, f32[2,128,512]{2,1,0:T(8,128)S(1)} %get-tuple-element.49.keep_ref.refs_1_, ...), custom_call_target="tpu_custom_call" | custom-call | flops 1000 | bytes 1000 | tf_op jit(solution)/shard_map/home/pallas_call | solution.py:483
  26.9 0.0 copy-start.1
  27.0 11.7 %collective-permute-done.9.refs_0_ = bf16[128,2048]{1,0:T(8,128)(2,1)S(1)} collective-permute-done((bf16[128,2048]{1,0:T(8,128)(2,1)S(1)}, bf16[128,2048]{1,0:T(8,128)(2,1)S(1)}, u32[]{:S(2)}, u32[]{:S(2)}) %collective-permute-start.9) | collective-permute-done | bytes 524320 | tf_op jit(solution)/shard_map/projection_sum/ppermute | solution.py:74
  38.7 0.0 copy-done.6
  38.7 0.7 dispatch.1
  39.4 21.2 %all_to_all.10.rows_ref = bf16[32,64,128]{2,1,0:T(8,128)(2,1)S(1)} all-to-all(bf16[32,64,128]{2,1,0:T(8,128)(2,1)S(1)} %get-tuple-element.56), channel_id=1, replica_groups=mesh['ctx'=4,'exp'=8] {'ctx','exp'}, dimensions={0} | all-to-all | bytes 1048576 | tf_op jit(solution)/shard_map/to_experts/all_to_all | solution.py:506
  60.6 0.0 copy-done.2
  60.6 0.0 copy-done.3
  60.6 0.0 copy-done.1
  60.6 0.0 copy-start.7
  60.6 0.0 copy-start.10
  60.7 1.6 %experts.1 = bf16[32,64,128]{2,1,0:T(8,128)(2,1)S(1)} custom-call(bf16[32,64,128]{2,1,0:T(8,128)(2,1)S(1)} %all_to_all.10.rows_ref, bf16[1,2048,512]{2,1,0:T(8,128)(2,1)S(1)} %copy-done.1, bf16[1,2048,512]{2,1,0:T(8,128)(2,1)S(1)} %copy-done.2, bf16[1,512,2048]{2,1,0:T(8,128)(2,1)S(1)} %copy-done.3), custom_call_target="tpu_custom_call" | custom-call | tf_op jit(solution)/shard_map/experts/pallas_call | solution.py:508
  62.3 18.4 %all_to_all.11.back_ref = bf16[32,64,128]{2,1,0:T(8,128)(2,1)S(1)} all-to-all(bf16[32,64,128]{2,1,0:T(8,128)(2,1)S(1)} %experts.1), channel_id=1, replica_groups=mesh['ctx'=4,'exp'=8] {'ctx','exp'}, dimensions={0} | all-to-all | bytes 1048576 | tf_op jit(solution)/shard_map/from_experts/all_to_all | solution.py:515
  80.7 0.0 copy-done.7
  80.7 0.0 copy-done.10
  80.7 1.5 %combine.1 = bf16[1,128,2048]{2,1,0:T(8,128)(2,1)} custom-call(f32[128,2048]{1,0:T(8,128)S(1)} %get-tuple-element.54.hidden_ref, f32[128,128]{1,0:T(8,128)S(1)} %get-tuple-element.55.table_ref, bf16[32,64,128]{2,1,0:T(8,128)(2,1)S(1)} %all_to_all.11.back_ref, s32[1,128]{1,0:T(1,128)S(1)} %copy-done.10, f32[1,2048]{1,0:T(1,128)S(1)} %bitcast.8), custom_call_target="tpu_custom_call" | custom-call | tf_op jit(solution)/shard_map/combine/pallas_call | solution.py:517
Async XLA Ops:
  0.0 23.8 %collective-permute-start.7 = (bf16[512,2048]{1,0:T(8,128)(2,1)}, bf16[512,2048]{1,0:T(8,128)(2,1)S(1)}, u32[]{:S(2)}, u32[]{:S(2)}) collective-permute-start(bf16[512,2048]{1,0:T(8,128)(2,1)} %refs_3_.1), channel_id=1, source_target_pairs={{0,8},{8,0},{16,24},{24,16},{1,9},{9,1},{17,25},{25,17},{2,10},{10... | collective-permute-start | bytes 6291464 | tf_op jit(solution)/shard_map/late_exchange/ppermute | solution.py:74
  2.2 4.5 %collective-permute-start = (bf16[144,256]{1,0:T(8,128)(2,1)S(1)}, bf16[144,256]{1,0:T(8,128)(2,1)S(1)}, u32[]{:S(2)}, u32[]{:S(2)}) collective-permute-start(bf16[144,256]{1,0:T(8,128)(2,1)S(1)} %get-tuple-element.32), channel_id=1, source_target_pairs={{0,8},{8,0},{16,24},{24,16},{1,9},{9,1},{17,25},{25,17},{2,10},{10... | collective-permute-start | bytes 221192 | tf_op jit(solution)/shard_map/heads_exchange/ppermute | solution.py:74
  2.3 5.6 %collective-permute-start.1 = (bf16[144,256]{1,0:T(8,128)(2,1)S(1)}, bf16[144,256]{1,0:T(8,128)(2,1)S(1)}, u32[]{:S(2)}, u32[]{:S(2)}) collective-permute-start(bf16[144,256]{1,0:T(8,128)(2,1)S(1)} %get-tuple-element.33), channel_id=1, source_target_pairs={{0,16},{8,24},{16,0},{24,8},{1,17},{9,25},{17,1},{25,9},{2,18},{10... | collective-permute-start | bytes 221192 | tf_op jit(solution)/shard_map/heads_exchange/ppermute | solution.py:74
  5.2 4.6 %collective-permute-start.2 = (bf16[144,256]{1,0:T(8,128)(2,1)S(1)}, bf16[144,256]{1,0:T(8,128)(2,1)S(1)}, u32[]{:S(2)}, u32[]{:S(2)}) collective-permute-start(bf16[144,256]{1,0:T(8,128)(2,1)S(1)} %get-tuple-element.34), channel_id=1, source_target_pairs={{0,24},{8,16},{16,8},{24,0},{1,25},{9,17},{17,9},{25,1},{2,26},{10... | collective-permute-start | bytes 221192 | tf_op jit(solution)/shard_map/heads_exchange/ppermute | solution.py:74
  5.2 12.0 %collective-permute-start.4 = (bf16[128,768]{1,0:T(8,128)(2,1)S(1)}, bf16[128,768]{1,0:T(8,128)(2,1)S(1)}, u32[]{:S(2)}, u32[]{:S(2)}) collective-permute-start(bf16[128,768]{1,0:T(8,128)(2,1)S(1)} %get-tuple-element.43), channel_id=1, source_target_pairs={{0,16},{8,24},{16,0},{24,8},{1,17},{9,25},{17,1},{25,9},{2,18},{10... | collective-permute-start | bytes 589832 | tf_op jit(solution)/shard_map/heads_exchange/ppermute | solution.py:74
  6.7 11.6 %collective-permute-start.5 = (bf16[128,768]{1,0:T(8,128)(2,1)S(1)}, bf16[128,768]{1,0:T(8,128)(2,1)S(1)}, u32[]{:S(2)}, u32[]{:S(2)}) collective-permute-start(bf16[128,768]{1,0:T(8,128)(2,1)S(1)} %get-tuple-element.44), channel_id=1, source_target_pairs={{0,24},{8,16},{16,8},{24,0},{1,25},{9,17},{17,9},{25,1},{2,26},{10... | collective-permute-start | bytes 589832 | tf_op jit(solution)/shard_map/heads_exchange/ppermute | solution.py:74
  9.8 8.4 %copy-start.11 = (f32[128]{0:T(128)S(1)}, f32[128]{0:T(128)}, u32[]{:S(2)}) copy-start(f32[128]{0:T(128)} %param.23) | copy-start | bytes 1540
  9.8 8.4 %collective-permute-start.3 = (bf16[128,768]{1,0:T(8,128)(2,1)S(1)}, bf16[128,768]{1,0:T(8,128)(2,1)S(1)}, u32[]{:S(2)}, u32[]{:S(2)}) collective-permute-start(bf16[128,768]{1,0:T(8,128)(2,1)S(1)} %get-tuple-element.42), channel_id=1, source_target_pairs={{0,8},{8,0},{16,24},{24,16},{1,9},{9,1},{17,25},{25,17},{2,10},{10... | collective-permute-start | bytes 589832 | tf_op jit(solution)/shard_map/late_exchange/ppermute | solution.py:74
  9.9 13.9 %collective-permute-start.8 = (bf16[128,1024]{1,0:T(8,128)(2,1)S(1)}, bf16[128,1024]{1,0:T(8,128)(2,1)S(1)}, u32[]{:S(2)}, u32[]{:S(2)}) collective-permute-start(bf16[128,1024]{1,0:T(8,128)(2,1)S(1)} %get-tuple-element.53), channel_id=1, source_target_pairs={{0,16},{8,24},{16,0},{24,8},{1,17},{9,25},{17,1},{25,9},{2,18},{10... | collective-permute-start | bytes 786440 | tf_op jit(solution)/shard_map/late_exchange/ppermute | solution.py:74
  18.2 5.6 %copy-start = (bf16[512,2048]{1,0:T(8,128)(2,1)S(1)}, bf16[512,2048]{1,0:T(8,128)(2,1)}, u32[]{:S(2)}) copy-start(bf16[512,2048]{1,0:T(8,128)(2,1)} %refs_3_.1) | copy-start | bytes 6291460
  21.0 2.8 %collective-permute-start.6 = (bf16[2,128,512]{2,1,0:T(8,128)(2,1)S(1)}, bf16[2,128,512]{2,1,0:T(8,128)(2,1)S(1)}, u32[]{:S(2)}, u32[]{:S(2)}) collective-permute-start(bf16[2,128,512]{2,1,0:T(8,128)(2,1)S(1)} %get-tuple-element.50), channel_id=1, source_target_pairs={{0,8},{8,0},{16,24},{24,16},{1,9},{9,1},{17,25},{25,17},{2,10},{10... | collective-permute-start | bytes 786440 | tf_op jit(solution)/shard_map/far_projection/ppermute | solution.py:74
  23.8 2.2 %copy-start.4 = (bf16[1,128,2048]{2,1,0:T(8,128)(2,1)S(1)}, bf16[1,128,2048]{2,1,0:T(8,128)(2,1)}, u32[]{:S(2)}) copy-start(bf16[1,128,2048]{2,1,0:T(8,128)(2,1)} %gate_ref.2) | copy-start | bytes 1572868
  23.8 2.2 %copy-start.5 = (bf16[1,128,2048]{2,1,0:T(8,128)(2,1)S(1)}, bf16[1,128,2048]{2,1,0:T(8,128)(2,1)}, u32[]{:S(2)}) copy-start(bf16[1,128,2048]{2,1,0:T(8,128)(2,1)} %residual_ref.1) | copy-start | bytes 1572868
  23.8 2.2 %copy-start.8 = (s32[1,128,10]{1,0,2:T(1,128)S(1)}, s32[1,128,10]{1,0,2:T(1,128)}, u32[]{:S(2)}) copy-start(s32[1,128,10]{1,0,2:T(1,128)} %param.27) | copy-start | bytes 15364
  23.8 2.2 %copy-start.9 = (f32[1,128,10]{1,0,2:T(1,128)S(1)}, f32[1,128,10]{1,0,2:T(1,128)}, u32[]{:S(2)}) copy-start(f32[1,128,10]{1,0,2:T(1,128)} %param.28) | copy-start | bytes 15364
  24.7 14.0 %collective-permute-start.9 = (bf16[128,2048]{1,0:T(8,128)(2,1)S(1)}, bf16[128,2048]{1,0:T(8,128)(2,1)S(1)}, u32[]{:S(2)}, u32[]{:S(2)}) collective-permute-start(bf16[128,2048]{1,0:T(8,128)(2,1)S(1)} %far_projection.1), channel_id=1, source_target_pairs={{0,16},{8,24},{16,0},{24,8},{1,17},{9,25},{17,1},{25,9},{2,18},{10... | collective-permute-start | bytes 1572872 | tf_op jit(solution)/shard_map/projection_sum/ppermute | solution.py:74
  26.0 12.6 %copy-start.6 = (f32[2048]{0:T(1024)S(1)}, f32[2048]{0:T(1024)}, u32[]{:S(2)}) copy-start(f32[2048]{0:T(1024)} %param.26) | copy-start | bytes 24580
  26.1 34.6 %copy-start.2 = (bf16[1,2048,512]{2,1,0:T(8,128)(2,1)S(1)}, bf16[1,2048,512]{2,1,0:T(8,128)(2,1)}, u32[]{:S(2)}) copy-start(bf16[1,2048,512]{2,1,0:T(8,128)(2,1)} %up_ref.1) | copy-start | bytes 6291460
  26.1 34.5 %copy-start.3 = (bf16[1,512,2048]{2,1,0:T(8,128)(2,1)S(1)}, bf16[1,512,2048]{2,1,0:T(8,128)(2,1)}, u32[]{:S(2)}) copy-start(bf16[1,512,2048]{2,1,0:T(8,128)(2,1)} %down_ref.1) | copy-start | bytes 6291460
  26.9 33.7 %copy-start.1 = (bf16[1,2048,512]{2,1,0:T(8,128)(2,1)S(1)}, bf16[1,2048,512]{2,1,0:T(8,128)(2,1)}, u32[]{:S(2)}) copy-start(bf16[1,2048,512]{2,1,0:T(8,128)(2,1)} %gate_ref.3) | copy-start | bytes 6291460
  60.6 20.1 %copy-start.7 = (f32[2048]{0:T(1024)S(1)}, f32[2048]{0:T(1024)}, u32[]{:S(2)}) copy-start(f32[2048]{0:T(1024)} %param.33) | copy-start | bytes 24580
  60.6 20.1 %copy-start.10 = (s32[1,128]{1,0:T(1,128)S(1)}, s32[1,128]{1,0:T(1,128)}, u32[]{:S(2)}) copy-start(s32[1,128]{1,0:T(1,128)} %mask_ref.1) | copy-start | bytes 1540

commit v5 on v4

--- a/solution.py
+++ b/solution.py
@@ -325,11 +325,9 @@
 
 
 def dispatch_kernel(base_ref, gain_ref, picker_ref, *refs):
-    part_refs = refs[:-3]
-    hidden_ref, rows_ref, flat_ref = refs[-3:]
+    part_refs = refs[:-2]
+    hidden_ref, rows_ref = refs[-2:]
     width = hidden_ref.shape[1]
-    slots = picker_ref.shape[0]
-    chunks = width // LANES
     squares = 0.0
     step = 512
     for c in range(0, width, step):
@@ -342,44 +340,35 @@
     picker = picker_ref[...]
     for c in range(0, width, step):
         normed = (hidden_ref[:, c : c + step] * scale * gain_ref[:, c : c + step]).astype(bf16)
-        rows = mm(picker, normed)
-        for i in range(step // LANES):
-            flat_ref[pl.ds(c // LANES + i, slots, stride=chunks), :] = rows[:, i * LANES : (i + 1) * LANES]
-    rows_ref[...] = flat_ref[...].astype(bf16).reshape(rows_ref.shape)
-
-
-def expert_kernel(rows_ref, gate_ref, up_ref, down_ref, out_ref, flat_ref, x_ref):
-    slots = flat_ref.shape[0] * LANES // x_ref.shape[1]
-    width = x_ref.shape[1]
-    chunks = width // LANES
-    flat_ref[...] = rows_ref[...].reshape(flat_ref.shape).astype(f32)
-    for c in range(chunks):
-        x_ref[:, c * LANES : (c + 1) * LANES] = flat_ref[pl.ds(c, slots, stride=chunks), :].astype(bf16)
-    tile = 128
+        rows = mm(picker, normed).astype(bf16)
+        rows_ref[:, :, c : c + step] = rows.reshape(*rows_ref.shape[:2], step)
+
+
+def expert_kernel(rows_ref, gate_ref, up_ref, down_ref, out_ref):
+    sources, cap, width = rows_ref.shape
+    tile = min(sources, 128 // cap)
 
     def one(t, carry):
-        x = x_ref[pl.ds(pl.multiple_of(t * tile, tile), tile), :]
+        here = pl.ds(t * tile, tile)
+        x = rows_ref[here].reshape(tile * cap, width)
         gate = mm(x, gate_ref[0])
         up = mm(x, up_ref[0])
         act = (gate / (1.0 + jnp.exp(-gate)) * up).astype(bf16)
         step = 512
         for c in range(0, width, step):
-            y = mm(act, down_ref[0, :, c : c + step])
-            for i in range(step // LANES):
-                flat_ref[pl.ds(t * tile * chunks + c // LANES + i, tile, stride=chunks), :] = y[
-                    :, i * LANES : (i + 1) * LANES
-                ]
+            y = mm(act, down_ref[0, :, c : c + step]).astype(bf16)
+            out_ref[here, :, c : c + step] = y.reshape(tile, cap, step)
         return carry
 
-    lax.fori_loop(0, slots // tile, one, 0)
-    out_ref[...] = flat_ref[...].astype(bf16).reshape(out_ref.shape)
-
-
-def combine_kernel(hidden_ref, table_ref, back_ref, mask_ref, dir_ref, out_ref, flat_ref, sum_ref):
+    if sources == tile:
+        one(0, 0)
+    else:
+        lax.fori_loop(0, sources // tile, one, 0)
+
+
+def combine_kernel(hidden_ref, table_ref, back_ref, mask_ref, dir_ref, out_ref, sum_ref):
     tokens, width = hidden_ref.shape
     slots = table_ref.shape[0]
-    chunks = width // LANES
-    flat_ref[...] = back_ref[...].reshape(flat_ref.shape).astype(f32)
     table = jnp.concatenate(split2(table_ref[...]), axis=0)
     direction = dir_ref[...]
     unit = direction / jnp.sqrt(jnp.sum(direction * direction, axis=1, keepdims=True) + EPS)
@@ -388,9 +377,7 @@
     along = 0.0
     step = 256
     for c in range(0, width, step):
-        back = jnp.concatenate(
-            [flat_ref[pl.ds(c // LANES + i, slots, stride=chunks), :].astype(bf16) for i in range(step // LANES)], axis=1
-        )
+        back = back_ref[:, :, c : c + step].reshape(slots, step)
         total = hidden_ref[:, c : c + step] + mm_tn(table, jnp.concatenate([back, back], axis=0))
         sum_ref[:, c : c + step] = total
         along = along + jnp.sum(total * unit[:, c : c + step], axis=1, keepdims=True)
@@ -423,7 +410,6 @@
     kw, vw = keys.shape[2] // n, values.shape[2] // n
     chips = n // 2
     slots = devices * CAP
-    chunks = width // LANES
     shape = jax.ShapeDtypeStruct
 
     local = vw // DK
@@ -498,8 +484,7 @@
     with jax.named_scope("dispatch"):
         hidden, rows = pl.pallas_call(
             dispatch_kernel,
-            out_shape=[shape((tokens, width), f32), shape((devices, CAP * chunks, LANES), bf16)],
-            scratch_shapes=[pltpu.VMEM((slots * chunks, LANES), f32)],
+            out_shape=[shape((tokens, width), f32), shape((devices, CAP, width), bf16)],
             compiler_params=compiler_params(24),
         )(base, ffn_gain.reshape(1, -1), picker, *parts)
     with jax.named_scope("to_experts"):
@@ -507,8 +492,7 @@
     with jax.named_scope("experts"):
         done = pl.pallas_call(
             expert_kernel,
-            out_shape=shape((devices, CAP * chunks, LANES), bf16),
-            scratch_shapes=[pltpu.VMEM((slots * chunks, LANES), f32), pltpu.VMEM((slots, width), bf16)],
+            out_shape=shape((devices, CAP, width), bf16),
             compiler_params=compiler_params(24),
         )(came, w_gate, w_up, w_down)
     with jax.named_scope("from_experts"):
@@ -517,10 +501,7 @@
         return pl.pallas_call(
             combine_kernel,
             out_shape=shape((1, tokens, width), bf16),
-            scratch_shapes=[
-                pltpu.VMEM((slots * chunks, LANES), f32),
-                pltpu.VMEM((tokens, width), f32),
-            ],
+            scratch_shapes=[pltpu.VMEM((tokens, width), f32)],
             compiler_params=compiler_params(24),
         )(hidden, table, back, ablate_mask, direction.reshape(1, -1))
 

time: 82.4 us -> 81.4 us (0.988)
  Pallas kernels: 15.5 us -> 14.5 us
where the time goes in v5:
time: 81.4 us; the launch traced here: 81.3 us
  blocking collectives  39.6 us (49%)
  waiting for transfers between devices  18.1 us (22%)
  Pallas kernels  14.5 us (18%)
  starting transfers between devices  8.77 us (11%)
    all_to_all x1, blocking collectives, local_part(): came = lax.all_to_all(rows, ('ctx', 'exp'), 0, 0, tiled=True)  21.2 us
    all_to_all x1, blocking collectives, local_part(): back = lax.all_to_all(done, ('ctx', 'exp'), 0, 0, tiled=True)  18.4 us
    ppermute x10, waiting for transfers between devices, send(): return lax.ppermute(x, 'ctx', pairs)  18.1 us
    ppermute x10, starting transfers between devices, send(): return lax.ppermute(x, 'ctx', pairs)  8.77 us
    pallas_call x1, Pallas kernels, local_part(): pl.pallas_call(functools.partial(inverse_kernel, n, local), out_shape=[wi...  5.48 us
    pallas_call x1, Pallas kernels, local_part(): pl.pallas_call(functools.partial(state_kernel, n, kw, vw), out_shape=[sha...  2.78 us
    pallas_call x1, Pallas kernels, local_part(): pl.pallas_call(functools.partial(pack_kernel, n, kw, vw), out_shape=[keye...  1.71 us
  transfers between devices with their start and end apart: 10, of which 5 were waited for; matrix products, arithmetic and copies ran while one was open for 0% of the time, Pallas kernels for 13%

profile of v5, /device:TPU:0, one launch (start us, length us, event | category | flops | bytes accessed | tf_op | source)
XLA Modules:
  0.0 81.3 jit_solution(5385387852399420716)
XLA Ops:
  0.0 0.5 collective-permute-start.7
  0.5 1.7 %pack.1 = (bf16[144,256]{1,0:T(8,128)(2,1)S(1)}, bf16[144,256]{1,0:T(8,128)(2,1)S(1)}, bf16[144,256]{1,0:T(8,128)(2,1)S(1)}, bf16[144,256]{1,0:T(8,128)(2,1)S(1)...) custom-call(bf16[1,128,1024]{2,1,0:T(8,128)(2,1)} %k_ref.1, ...), custom_call_target="tpu_custom_call" | custom-call | tf_op jit(solution)/shard_map/pack/pallas_call | solution.py:419
  2.2 0.1 collective-permute-start
  2.3 2.9 %collective-permute-start.1 = (bf16[144,256]{1,0:T(8,128)(2,1)S(1)}, bf16[144,256]{1,0:T(8,128)(2,1)S(1)}, u32[]{:S(2)}, u32[]{:S(2)}) collective-permute-start(bf16[144,256]{1,0:T(8,128)(2,1)S(1)} %get-tuple-element.33), channel_id=1, source_target_pairs={{0,16},{8,24},{16,0},{24,8},{1,17},{9,25},{17,1},{25,9},{2,18},{10... | collective-permute-start | bytes 221192 | tf_op jit(solution)/shard_map/heads_exchange/ppermute | solution.py:74
  5.2 0.0 collective-permute-start.2
  5.2 1.4 %collective-permute-start.4 = (bf16[128,768]{1,0:T(8,128)(2,1)S(1)}, bf16[128,768]{1,0:T(8,128)(2,1)S(1)}, u32[]{:S(2)}, u32[]{:S(2)}) collective-permute-start(bf16[128,768]{1,0:T(8,128)(2,1)S(1)} %get-tuple-element.43), channel_id=1, source_target_pairs={{0,16},{8,24},{16,0},{24,8},{1,17},{9,25},{17,1},{25,9},{2,18},{10... | collective-permute-start | bytes 589832 | tf_op jit(solution)/shard_map/heads_exchange/ppermute | solution.py:74
  6.7 0.0 collective-permute-done.refs_1_
  6.7 0.3 collective-permute-start.5
  7.0 0.9 %collective-permute-done.1.refs_2_ = bf16[144,256]{1,0:T(8,128)(2,1)S(1)} collective-permute-done((bf16[144,256]{1,0:T(8,128)(2,1)S(1)}, bf16[144,256]{1,0:T(8,128)(2,1)S(1)}, u32[]{:S(2)}, u32[]{:S(2)}) %collective-permute-start.1) | collective-permute-done | bytes 73760 | tf_op jit(solution)/shard_map/heads_exchange/ppermute | solution.py:74
  7.9 1.9 %collective-permute-done.2.refs_3_ = bf16[144,256]{1,0:T(8,128)(2,1)S(1)} collective-permute-done((bf16[144,256]{1,0:T(8,128)(2,1)S(1)}, bf16[144,256]{1,0:T(8,128)(2,1)S(1)}, u32[]{:S(2)}, u32[]{:S(2)}) %collective-permute-start.2) | collective-permute-done | bytes 73760 | tf_op jit(solution)/shard_map/heads_exchange/ppermute | solution.py:74
  9.8 0.0 copy-start.11
  9.8 0.1 collective-permute-start.3
  9.9 1.9 %collective-permute-start.8 = (bf16[128,1024]{1,0:T(8,128)(2,1)S(1)}, bf16[128,1024]{1,0:T(8,128)(2,1)S(1)}, u32[]{:S(2)}, u32[]{:S(2)}) collective-permute-start(bf16[128,1024]{1,0:T(8,128)(2,1)S(1)} %get-tuple-element.53), channel_id=1, source_target_pairs={{0,16},{8,24},{16,0},{24,8},{1,17},{9,25},{17,1},{25,9},{2,18},{10... | collective-permute-start | bytes 786440 | tf_op jit(solution)/shard_map/late_exchange/ppermute | solution.py:74
  11.8 5.5 %block_inverses.1 = (bf16[4,4,128,256]{3,2,1,0:T(8,128)(2,1)S(1)}, bf16[4,4,128,256]{3,2,1,0:T(8,128)(2,1)S(1)}, bf16[4,4,128,256]{3,2,1,0:T(8,128)(2,1)S(1)}, f32[4,4,8,128]{3,2,1,0:T(8,128)S(1)}) custom-call(bf16[144,256]{1,0:T(8,128)(2,1)S(1)} %get-tuple-element.37.refs_0_, bf16[144,256]{1,0:T(8,128)(2,1)S(1)} %collective-permute-done.refs_1_, ...), custom_call_target="tpu_custom_call" | custom-call | flops 6000000000 | bytes 1000000 | tf_op jit(solution)/shard_map/block_inverses/pallas_call | solution.py:435
  17.3 0.0 collective-permute-done.4.refs_6_
  17.3 1.0 %collective-permute-done.5.refs_7_ = bf16[128,768]{1,0:T(8,128)(2,1)S(1)} collective-permute-done((bf16[128,768]{1,0:T(8,128)(2,1)S(1)}, bf16[128,768]{1,0:T(8,128)(2,1)S(1)}, u32[]{:S(2)}, u32[]{:S(2)}) %collective-permute-start.5) | collective-permute-done | bytes 196640 | tf_op jit(solution)/shard_map/heads_exchange/ppermute | solution.py:74
  18.2 0.0 collective-permute-done.3.refs_5_
  18.2 0.0 copy-done.11
  18.2 0.0 copy-start
  18.2 2.8 %states.1 = (f32[2,128,512]{2,1,0:T(8,128)S(1)}, bf16[2,128,512]{2,1,0:T(8,128)(2,1)S(1)}) custom-call(bf16[144,256]{1,0:T(8,128)(2,1)S(1)} %get-tuple-element.37.refs_0_, bf16[144,256]{1,0:T(8,128)(2,1)S(1)} %collective-permute-done.refs_1_, bf16[144,256]{1,0:T(8,128)(2,1)S(1)} %collective-permute-done.1.refs_2_, ...), custom_call_target="tpu_custom_call" | custom-call | flops 4000000000 | bytes 1000000 | tf_op jit(solution)/shard_map/states/pallas_call | solution.py:448
  21.0 0.1 collective-permute-start.6
  21.2 2.6 %collective-permute-done.8.refs_0_ = bf16[128,1024]{1,0:T(8,128)(2,1)S(1)} collective-permute-done((bf16[128,1024]{1,0:T(8,128)(2,1)S(1)}, bf16[128,1024]{1,0:T(8,128)(2,1)S(1)}, u32[]{:S(2)}, u32[]{:S(2)}) %collective-permute-start.8) | collective-permute-done | bytes 262176 | tf_op jit(solution)/shard_map/late_exchange/ppermute | solution.py:74
  23.8 0.0 collective-permute-done.6.other_ref.refs_2_
  23.8 0.0 collective-permute-done.7.proj_other_ref.refs_4_
  23.8 0.0 copy-done
  23.8 0.0 copy-start.4
  23.8 0.0 copy-start.5
  23.8 0.0 copy-start.8
  23.8 0.0 copy-start.9
  23.9 0.8 far_projection.1
  24.7 1.4 %collective-permute-start.9 = (bf16[128,2048]{1,0:T(8,128)(2,1)S(1)}, bf16[128,2048]{1,0:T(8,128)(2,1)S(1)}, u32[]{:S(2)}, u32[]{:S(2)}) collective-permute-start(bf16[128,2048]{1,0:T(8,128)(2,1)S(1)} %far_projection.1), channel_id=1, source_target_pairs={{0,16},{8,24},{16,0},{24,8},{1,17},{9,25},{17,1},{25,9},{2,18},{10... | collective-permute-start | bytes 1572872 | tf_op jit(solution)/shard_map/projection_sum/ppermute | solution.py:74
  26.0 0.0 copy-done.4
  26.0 0.0 copy-done.5
  26.0 0.0 copy-done.8
  26.0 0.0 copy-done.9
  26.0 0.0 copy-start.6
  26.1 0.0 copy-start.2
  26.1 0.0 copy-start.3
  26.1 0.9 %home.1 = (f32[128,2048]{1,0:T(8,128)S(1)}, bf16[128,128]{1,0:T(8,128)(2,1)S(1)}, f32[128,128]{1,0:T(8,128)S(1)}) custom-call(bf16[1,128,2048]{2,1,0:T(8,128)(2,1)S(1)} %copy-done.5, bf16[1,128,2048]{2,1,0:T(8,128)(2,1)S(1)} %copy-done.4, f32[2,128,512]{2,1,0:T(8,128)S(1)} %get-tuple-element.49.keep_ref.refs_1_, ...), custom_call_target="tpu_custom_call" | custom-call | flops 1000 | bytes 1000 | tf_op jit(solution)/shard_map/home/pallas_call | solution.py:469
  26.9 0.0 copy-start.1
  27.0 11.7 %collective-permute-done.9.refs_0_ = bf16[128,2048]{1,0:T(8,128)(2,1)S(1)} collective-permute-done((bf16[128,2048]{1,0:T(8,128)(2,1)S(1)}, bf16[128,2048]{1,0:T(8,128)(2,1)S(1)}, u32[]{:S(2)}, u32[]{:S(2)}) %collective-permute-start.9) | collective-permute-done | bytes 524320 | tf_op jit(solution)/shard_map/projection_sum/ppermute | solution.py:74
  38.7 0.0 copy-done.6
  38.7 0.5 dispatch.1
  39.2 21.2 %all_to_all.10.rows_ref = bf16[32,4,2048]{2,1,0:T(4,128)(2,1)S(1)} all-to-all(bf16[32,4,2048]{2,1,0:T(4,128)(2,1)S(1)} %get-tuple-element.56), channel_id=1, replica_groups=mesh['ctx'=4,'exp'=8] {'ctx','exp'}, dimensions={0} | all-to-all | bytes 1048576 | tf_op jit(solution)/shard_map/to_experts/all_to_all | solution.py:491
  60.4 0.0 copy-done.2
  60.4 0.0 copy-done.3
  60.4 0.0 copy-done.1
  60.4 0.0 copy-start.7
  60.4 0.0 copy-start.10
  60.4 1.1 %experts.1 = bf16[32,4,2048]{2,1,0:T(4,128)(2,1)S(1)} custom-call(bf16[32,4,2048]{2,1,0:T(4,128)(2,1)S(1)} %all_to_all.10.rows_ref, bf16[1,2048,512]{2,1,0:T(8,128)(2,1)S(1)} %copy-done.1, bf16[1,2048,512]{2,1,0:T(8,128)(2,1)S(1)} %copy-done.2, bf16[1,512,2048]{2,1,0:T(8,128)(2,1)S(1)} %copy-done.3), custom_call_target="tpu_custom_call" | custom-call | tf_op jit(solution)/shard_map/experts/pallas_call | solution.py:493
  61.5 18.4 %all_to_all.11.back_ref = bf16[32,4,2048]{2,1,0:T(4,128)(2,1)S(1)} all-to-all(bf16[32,4,2048]{2,1,0:T(4,128)(2,1)S(1)} %experts.1), channel_id=1, replica_groups=mesh['ctx'=4,'exp'=8] {'ctx','exp'}, dimensions={0} | all-to-all | bytes 1048576 | tf_op jit(solution)/shard_map/from_experts/all_to_all | solution.py:499
  80.0 0.0 copy-done.7
  80.0 0.0 copy-done.10
  80.0 1.3 %combine.1 = bf16[1,128,2048]{2,1,0:T(8,128)(2,1)} custom-call(f32[128,2048]{1,0:T(8,128)S(1)} %get-tuple-element.54.hidden_ref, f32[128,128]{1,0:T(8,128)S(1)} %get-tuple-element.55.table_ref, bf16[32,4,2048]{2,1,0:T(4,128)(2,1)S(1)} %all_to_all.11.back_ref, s32[1,128]{1,0:T(1,128)S(1)} %copy-done.10, f32[1,2048]{1,0:T(1,128)S(1)} %bitcast.8), custom_call_target="tpu_custom_call" | custom-call | tf_op jit(solution)/shard_map/combine/pallas_call | solution.py:501
Async XLA Ops:
  0.0 23.8 %collective-permute-start.7 = (bf16[512,2048]{1,0:T(8,128)(2,1)}, bf16[512,2048]{1,0:T(8,128)(2,1)S(1)}, u32[]{:S(2)}, u32[]{:S(2)}) collective-permute-start(bf16[512,2048]{1,0:T(8,128)(2,1)} %refs_3_.1), channel_id=1, source_target_pairs={{0,8},{8,0},{16,24},{24,16},{1,9},{9,1},{17,25},{25,17},{2,10},{10... | collective-permute-start | bytes 6291464 | tf_op jit(solution)/shard_map/late_exchange/ppermute | solution.py:74
  2.2 4.5 %collective-permute-start = (bf16[144,256]{1,0:T(8,128)(2,1)S(1)}, bf16[144,256]{1,0:T(8,128)(2,1)S(1)}, u32[]{:S(2)}, u32[]{:S(2)}) collective-permute-start(bf16[144,256]{1,0:T(8,128)(2,1)S(1)} %get-tuple-element.32), channel_id=1, source_target_pairs={{0,8},{8,0},{16,24},{24,16},{1,9},{9,1},{17,25},{25,17},{2,10},{10... | collective-permute-start | bytes 221192 | tf_op jit(solution)/shard_map/heads_exchange/ppermute | solution.py:74
  2.3 5.6 %collective-permute-start.1 = (bf16[144,256]{1,0:T(8,128)(2,1)S(1)}, bf16[144,256]{1,0:T(8,128)(2,1)S(1)}, u32[]{:S(2)}, u32[]{:S(2)}) collective-permute-start(bf16[144,256]{1,0:T(8,128)(2,1)S(1)} %get-tuple-element.33), channel_id=1, source_target_pairs={{0,16},{8,24},{16,0},{24,8},{1,17},{9,25},{17,1},{25,9},{2,18},{10... | collective-permute-start | bytes 221192 | tf_op jit(solution)/shard_map/heads_exchange/ppermute | solution.py:74
  5.2 4.6 %collective-permute-start.2 = (bf16[144,256]{1,0:T(8,128)(2,1)S(1)}, bf16[144,256]{1,0:T(8,128)(2,1)S(1)}, u32[]{:S(2)}, u32[]{:S(2)}) collective-permute-start(bf16[144,256]{1,0:T(8,128)(2,1)S(1)} %get-tuple-element.34), channel_id=1, source_target_pairs={{0,24},{8,16},{16,8},{24,0},{1,25},{9,17},{17,9},{25,1},{2,26},{10... | collective-permute-start | bytes 221192 | tf_op jit(solution)/shard_map/heads_exchange/ppermute | solution.py:74
  5.2 12.0 %collective-permute-start.4 = (bf16[128,768]{1,0:T(8,128)(2,1)S(1)}, bf16[128,768]{1,0:T(8,128)(2,1)S(1)}, u32[]{:S(2)}, u32[]{:S(2)}) collective-permute-start(bf16[128,768]{1,0:T(8,128)(2,1)S(1)} %get-tuple-element.43), channel_id=1, source_target_pairs={{0,16},{8,24},{16,0},{24,8},{1,17},{9,25},{17,1},{25,9},{2,18},{10... | collective-permute-start | bytes 589832 | tf_op jit(solution)/shard_map/heads_exchange/ppermute | solution.py:74
  6.7 11.6 %collective-permute-start.5 = (bf16[128,768]{1,0:T(8,128)(2,1)S(1)}, bf16[128,768]{1,0:T(8,128)(2,1)S(1)}, u32[]{:S(2)}, u32[]{:S(2)}) collective-permute-start(bf16[128,768]{1,0:T(8,128)(2,1)S(1)} %get-tuple-element.44), channel_id=1, source_target_pairs={{0,24},{8,16},{16,8},{24,0},{1,25},{9,17},{17,9},{25,1},{2,26},{10... | collective-permute-start | bytes 589832 | tf_op jit(solution)/shard_map/heads_exchange/ppermute | solution.py:74
  9.8 8.4 %copy-start.11 = (f32[128]{0:T(128)S(1)}, f32[128]{0:T(128)}, u32[]{:S(2)}) copy-start(f32[128]{0:T(128)} %param.23) | copy-start | bytes 1540
  9.8 8.4 %collective-permute-start.3 = (bf16[128,768]{1,0:T(8,128)(2,1)S(1)}, bf16[128,768]{1,0:T(8,128)(2,1)S(1)}, u32[]{:S(2)}, u32[]{:S(2)}) collective-permute-start(bf16[128,768]{1,0:T(8,128)(2,1)S(1)} %get-tuple-element.42), channel_id=1, source_target_pairs={{0,8},{8,0},{16,24},{24,16},{1,9},{9,1},{17,25},{25,17},{2,10},{10... | collective-permute-start | bytes 589832 | tf_op jit(solution)/shard_map/late_exchange/ppermute | solution.py:74
  9.9 13.9 %collective-permute-start.8 = (bf16[128,1024]{1,0:T(8,128)(2,1)S(1)}, bf16[128,1024]{1,0:T(8,128)(2,1)S(1)}, u32[]{:S(2)}, u32[]{:S(2)}) collective-permute-start(bf16[128,1024]{1,0:T(8,128)(2,1)S(1)} %get-tuple-element.53), channel_id=1, source_target_pairs={{0,16},{8,24},{16,0},{24,8},{1,17},{9,25},{17,1},{25,9},{2,18},{10... | collective-permute-start | bytes 786440 | tf_op jit(solution)/shard_map/late_exchange/ppermute | solution.py:74
  18.2 5.6 %copy-start = (bf16[512,2048]{1,0:T(8,128)(2,1)S(1)}, bf16[512,2048]{1,0:T(8,128)(2,1)}, u32[]{:S(2)}) copy-start(bf16[512,2048]{1,0:T(8,128)(2,1)} %refs_3_.1) | copy-start | bytes 6291460
  21.0 2.8 %collective-permute-start.6 = (bf16[2,128,512]{2,1,0:T(8,128)(2,1)S(1)}, bf16[2,128,512]{2,1,0:T(8,128)(2,1)S(1)}, u32[]{:S(2)}, u32[]{:S(2)}) collective-permute-start(bf16[2,128,512]{2,1,0:T(8,128)(2,1)S(1)} %get-tuple-element.50), channel_id=1, source_target_pairs={{0,8},{8,0},{16,24},{24,16},{1,9},{9,1},{17,25},{25,17},{2,10},{10... | collective-permute-start | bytes 786440 | tf_op jit(solution)/shard_map/far_projection/ppermute | solution.py:74
  23.8 2.2 %copy-start.4 = (bf16[1,128,2048]{2,1,0:T(8,128)(2,1)S(1)}, bf16[1,128,2048]{2,1,0:T(8,128)(2,1)}, u32[]{:S(2)}) copy-start(bf16[1,128,2048]{2,1,0:T(8,128)(2,1)} %gate_ref.2) | copy-start | bytes 1572868
  23.8 2.2 %copy-start.5 = (bf16[1,128,2048]{2,1,0:T(8,128)(2,1)S(1)}, bf16[1,128,2048]{2,1,0:T(8,128)(2,1)}, u32[]{:S(2)}) copy-start(bf16[1,128,2048]{2,1,0:T(8,128)(2,1)} %residual_ref.1) | copy-start | bytes 1572868
  23.8 2.2 %copy-start.8 = (s32[1,128,10]{1,0,2:T(1,128)S(1)}, s32[1,128,10]{1,0,2:T(1,128)}, u32[]{:S(2)}) copy-start(s32[1,128,10]{1,0,2:T(1,128)} %param.27) | copy-start | bytes 15364
  23.8 2.2 %copy-start.9 = (f32[1,128,10]{1,0,2:T(1,128)S(1)}, f32[1,128,10]{1,0,2:T(1,128)}, u32[]{:S(2)}) copy-start(f32[1,128,10]{1,0,2:T(1,128)} %param.28) | copy-start | bytes 15364
  24.7 14.0 %collective-permute-start.9 = (bf16[128,2048]{1,0:T(8,128)(2,1)S(1)}, bf16[128,2048]{1,0:T(8,128)(2,1)S(1)}, u32[]{:S(2)}, u32[]{:S(2)}) collective-permute-start(bf16[128,2048]{1,0:T(8,128)(2,1)S(1)} %far_projection.1), channel_id=1, source_target_pairs={{0,16},{8,24},{16,0},{24,8},{1,17},{9,25},{17,1},{25,9},{2,18},{10... | collective-permute-start | bytes 1572872 | tf_op jit(solution)/shard_map/projection_sum/ppermute | solution.py:74
  26.0 12.6 %copy-start.6 = (f32[2048]{0:T(1024)S(1)}, f32[2048]{0:T(1024)}, u32[]{:S(2)}) copy-start(f32[2048]{0:T(1024)} %param.26) | copy-start | bytes 24580
  26.1 34.3 %copy-start.2 = (bf16[1,2048,512]{2,1,0:T(8,128)(2,1)S(1)}, bf16[1,2048,512]{2,1,0:T(8,128)(2,1)}, u32[]{:S(2)}) copy-start(bf16[1,2048,512]{2,1,0:T(8,128)(2,1)} %up_ref.1) | copy-start | bytes 6291460
  26.1 34.3 %copy-start.3 = (bf16[1,512,2048]{2,1,0:T(8,128)(2,1)S(1)}, bf16[1,512,2048]{2,1,0:T(8,128)(2,1)}, u32[]{:S(2)}) copy-start(bf16[1,512,2048]{2,1,0:T(8,128)(2,1)} %down_ref.1) | copy-start | bytes 6291460
  26.9 33.4 %copy-start.1 = (bf16[1,2048,512]{2,1,0:T(8,128)(2,1)S(1)}, bf16[1,2048,512]{2,1,0:T(8,128)(2,1)}, u32[]{:S(2)}) copy-start(bf16[1,2048,512]{2,1,0:T(8,128)(2,1)} %gate_ref.3) | copy-start | bytes 6291460
  60.4 19.6 %copy-start.7 = (f32[2048]{0:T(1024)S(1)}, f32[2048]{0:T(1024)}, u32[]{:S(2)}) copy-start(f32[2048]{0:T(1024)} %param.33) | copy-start | bytes 24580
  60.4 19.6 %copy-start.10 = (s32[1,128]{1,0:T(1,128)S(1)}, s32[1,128]{1,0:T(1,128)}, u32[]{:S(2)}) copy-start(s32[1,128]{1,0:T(1,128)} %mask_ref.1) | copy-start | bytes 1540

commit v6 on v5

--- a/solution.py
+++ b/solution.py
@@ -80,10 +80,7 @@
     me = lax.axis_index("ctx")
     tokens = k_ref.shape[1]
     heads = d_ref.shape[1]
-    ones = (iota((tokens, tokens), 0) <= iota((tokens, tokens), 1)).astype(bf16)
-    logs = jnp.log(d_ref[0])
-    sums = sum(mm(piece, ones) for piece in reversed(split3(logs)))
-    pieces = [p.astype(f32) for p in (*split3(sums), *split3(w_ref[0]))]
+    pieces = [p.astype(f32) for p in (*split3(d_ref[0]), *split3(w_ref[0]))]
     rates = jnp.concatenate(pieces, axis=0).astype(bf16)
     rows = AUX * kw // LANES
     row, entry = iota((rows, 6 * heads), 0), iota((rows, 6 * heads), 1)
@@ -131,21 +128,29 @@
 
 def inverse_kernel(n, local, *refs):
     keyed = refs[:n]
-    value_ref, erase_ref, key_ref, row_ref = refs[n:]
+    value_ref, erase_ref, key_ref, row_ref, down_ref = refs[n:]
     me = lax.axis_index("ctx")
     tokens = value_ref.shape[2]
     group = local * DK // keyed[0].shape[1]
     row, col = iota((tokens, tokens), 0), iota((tokens, tokens), 1)
     apart = lax.bitwise_xor(row, col)
     eye = (row == col).astype(f32)
+    ones = (row >= col).astype(bf16)
     systems, scales = [], []
     for i, route in enumerate(routes(n)):
         block = moved(me, route, n, back=True)
         aux, total = head_rates(local, keyed[i], tokens)
         as_cols, as_rows = mm_tn(aux, total), mm_tn(total, aux)
-        down, up = jnp.exp(as_rows), jnp.exp(-as_rows)
-        left = jnp.exp(as_rows[:, tokens - 1 :] - as_rows)
-        down_cols = jnp.exp(as_cols)
+        decays = jnp.where(iota((8, tokens), 0) < local, as_rows[0:8], 1.0)
+        logs = [piece.astype(f32) for piece in split3(jnp.log(decays))]
+        logs = jnp.concatenate(logs, axis=0).astype(bf16)
+        sums = mm_nt(logs, ones)
+        sums = sums[16:24] + sums[8:16] + sums[0:8]
+        sum_cols = mm_nt(ones, logs)
+        down, up = jnp.exp(sums), jnp.exp(-sums)
+        left = jnp.exp(sums[:, tokens - 1 :] - sums)
+        down_cols = jnp.exp(sum_cols[:, 16:24] + sum_cols[:, 8:16] + sum_cols[:, 0:8])
+        down_ref[block] = jnp.concatenate([down_cols, jnp.zeros((tokens, LANES - 8), f32)], axis=1)
         for g in range(local // group):
             k = keyed[i][0:tokens, g * DK : (g + 1) * DK]
             k_t = k.astype(f32).T
@@ -201,7 +206,7 @@
 
 def state_kernel(n, kw, vw, *refs):
     keyed, asked = refs[:n], refs[n : 2 * n]
-    value_ref, erase_ref, key_ref, row_ref, gain_ref, keep_ref, give_ref, out_ref, kx_ref, qv_ref = refs[2 * n :]
+    value_ref, erase_ref, key_ref, row_ref, down_ref, gain_ref, keep_ref, give_ref, out_ref, kx_ref, qv_ref = refs[2 * n :]
     me = lax.axis_index("ctx")
     tokens = value_ref.shape[2]
     local = vw // DK
@@ -215,8 +220,7 @@
     gain = gain_ref[...]
 
     def prepare(block):
-        aux, total = head_rates(local, kx_ref.at[block], tokens)
-        down_cols = jnp.exp(mm_tn(aux, total))
+        down_cols = down_ref[block]
         made = []
         for g in range(local // group):
             k = kx_ref[block, 0:tokens, g * DK : (g + 1) * DK]
@@ -291,6 +295,7 @@
 
 
 def home_kernel(
+    n,
     residual_ref,
     gate_ref,
     keep_ref,
@@ -310,7 +315,8 @@
         base_ref[:, here] = residual_ref[0, :, here].astype(f32) + part
     slots, tokens = table_ref.shape
     slot = iota((slots, tokens), 0)
-    expert = slot // CAP
+    place = slot // CAP
+    expert = lax.rem(place, n) * (slots // CAP // n) + place // n
     named = jnp.zeros((slots, tokens), f32)
     weight = jnp.zeros((slots, tokens), f32)
     for j in range(ids_ref.shape[0]):
@@ -434,7 +440,7 @@
         wide = shape((n, local, tokens, 2 * tokens), bf16)
         inverses = pl.pallas_call(
             functools.partial(inverse_kernel, n, local),
-            out_shape=[wide, wide, shape((n, local, DK, 2 * tokens), bf16), shape((n, local, 8, tokens), f32)],
+            out_shape=[wide, wide, shape((n, local, DK, 2 * tokens), bf16), shape((n, local, 8, tokens), f32), shape((n, tokens, LANES), f32)],
             compiler_params=compiler_params(16),
             cost_estimate=pl.CostEstimate(flops=6 * 10**9, bytes_accessed=10**6, transcendentals=0),
         )(*keyed)
@@ -467,7 +473,7 @@
         parts = [send(part, (j, 0), n) for j, part in enumerate(sums, 1)]
     with jax.named_scope("home"):
         base, picker, table = pl.pallas_call(
-            home_kernel,
+            functools.partial(home_kernel, n),
             out_shape=[shape((tokens, width), f32), shape((slots, tokens), bf16), shape((slots, tokens), f32)],
             compiler_params=compiler_params(16),
             cost_estimate=pl.CostEstimate(flops=1000, bytes_accessed=1000, transcendentals=0),
@@ -488,7 +494,7 @@
             compiler_params=compiler_params(24),
         )(base, ffn_gain.reshape(1, -1), picker, *parts)
     with jax.named_scope("to_experts"):
-        came = lax.all_to_all(rows, ("ctx", "exp"), 0, 0, tiled=True)
+        came = lax.all_to_all(rows, ("exp", "ctx"), 0, 0, tiled=True)
     with jax.named_scope("experts"):
         done = pl.pallas_call(
             expert_kernel,
@@ -496,7 +502,7 @@
             compiler_params=compiler_params(24),
         )(came, w_gate, w_up, w_down)
     with jax.named_scope("from_experts"):
-        back = lax.all_to_all(done, ("ctx", "exp"), 0, 0, tiled=True)
+        back = lax.all_to_all(done, ("exp", "ctx"), 0, 0, tiled=True)
     with jax.named_scope("combine"):
         return pl.pallas_call(
             combine_kernel,

time: 81.4 us -> 80.3 us (0.986)
  blocking collectives: 39.6 us -> 38.7 us
    all_to_all x2, blocking collectives: 39.6 us -> 38.7 us  [the longest x1 20.3 us: local_part(): came = lax.all_to_all(rows, ('exp', 'ctx'), 0, 0, tiled=True)]
  transfers between devices with their start and end apart: 10 -> 10, of which waited for: 5 -> 5; matrix products, arithmetic and copies ran while one was open for 0% -> 0% of each run, Pallas kernels for 13% -> 14%
where the time goes in v6:
time: 80.3 us; the launch traced here: 80.2 us
  blocking collectives  38.7 us (48%)
  waiting for transfers between devices  17.8 us (22%)
  Pallas kernels  14.6 us (18%)
  starting transfers between devices  8.85 us (11%)
    all_to_all x1, blocking collectives, local_part(): came = lax.all_to_all(rows, ('exp', 'ctx'), 0, 0, tiled=True)  20.3 us
    all_to_all x1, blocking collectives, local_part(): back = lax.all_to_all(done, ('exp', 'ctx'), 0, 0, tiled=True)  18.4 us
    ppermute x10, waiting for transfers between devices, send(): return lax.ppermute(x, 'ctx', pairs)  17.8 us
    ppermute x10, starting transfers between devices, send(): return lax.ppermute(x, 'ctx', pairs)  8.85 us
    pallas_call x1, Pallas kernels, local_part(): pl.pallas_call(functools.partial(inverse_kernel, n, local), out_shape=[wi...  5.81 us
    pallas_call x1, Pallas kernels, local_part(): pl.pallas_call(functools.partial(state_kernel, n, kw, vw), out_shape=[sha...  2.68 us
  transfers between devices with their start and end apart: 10, of which 5 were waited for; matrix products, arithmetic and copies ran while one was open for 0% of the time, Pallas kernels for 14%

profile of v6, /device:TPU:0, one launch (start us, length us, event | category | flops | bytes accessed | tf_op | source)
XLA Modules:
  0.0 80.2 jit_solution(13637635011418970523)
XLA Ops:
  0.0 0.5 collective-permute-start.7
  0.5 1.5 %pack.1 = (bf16[144,256]{1,0:T(8,128)(2,1)S(1)}, bf16[144,256]{1,0:T(8,128)(2,1)S(1)}, bf16[144,256]{1,0:T(8,128)(2,1)S(1)}, bf16[144,256]{1,0:T(8,128)(2,1)S(1)...) custom-call(bf16[1,128,1024]{2,1,0:T(8,128)(2,1)} %k_ref.1, ...), custom_call_target="tpu_custom_call" | custom-call | tf_op jit(solution)/shard_map/pack/pallas_call | solution.py:425
  2.0 0.1 collective-permute-start
  2.1 2.9 %collective-permute-start.1 = (bf16[144,256]{1,0:T(8,128)(2,1)S(1)}, bf16[144,256]{1,0:T(8,128)(2,1)S(1)}, u32[]{:S(2)}, u32[]{:S(2)}) collective-permute-start(bf16[144,256]{1,0:T(8,128)(2,1)S(1)} %get-tuple-element.34), channel_id=1, source_target_pairs={{0,16},{8,24},{16,0},{24,8},{1,17},{9,25},{17,1},{25,9},{2,18},{10... | collective-permute-start | bytes 221192 | tf_op jit(solution)/shard_map/heads_exchange/ppermute | solution.py:74
  5.1 0.0 collective-permute-start.2
  5.1 1.4 %collective-permute-start.4 = (bf16[128,768]{1,0:T(8,128)(2,1)S(1)}, bf16[128,768]{1,0:T(8,128)(2,1)S(1)}, u32[]{:S(2)}, u32[]{:S(2)}) collective-permute-start(bf16[128,768]{1,0:T(8,128)(2,1)S(1)} %get-tuple-element.44), channel_id=1, source_target_pairs={{0,16},{8,24},{16,0},{24,8},{1,17},{9,25},{17,1},{25,9},{2,18},{10... | collective-permute-start | bytes 589832 | tf_op jit(solution)/shard_map/heads_exchange/ppermute | solution.py:74
  6.5 0.0 collective-permute-done.refs_1_
  6.5 0.4 collective-permute-start.5
  6.9 0.8 collective-permute-done.1.refs_2_
  7.7 1.9 %collective-permute-done.2.refs_3_ = bf16[144,256]{1,0:T(8,128)(2,1)S(1)} collective-permute-done((bf16[144,256]{1,0:T(8,128)(2,1)S(1)}, bf16[144,256]{1,0:T(8,128)(2,1)S(1)}, u32[]{:S(2)}, u32[]{:S(2)}) %collective-permute-start.2) | collective-permute-done | bytes 73760 | tf_op jit(solution)/shard_map/heads_exchange/ppermute | solution.py:74
  9.6 0.0 copy-start.11
  9.6 0.1 collective-permute-start.3
  9.7 1.9 %collective-permute-start.8 = (bf16[128,1024]{1,0:T(8,128)(2,1)S(1)}, bf16[128,1024]{1,0:T(8,128)(2,1)S(1)}, u32[]{:S(2)}, u32[]{:S(2)}) collective-permute-start(bf16[128,1024]{1,0:T(8,128)(2,1)S(1)} %get-tuple-element.55), channel_id=1, source_target_pairs={{0,16},{8,24},{16,0},{24,8},{1,17},{9,25},{17,1},{25,9},{2,18},{10... | collective-permute-start | bytes 786440 | tf_op jit(solution)/shard_map/late_exchange/ppermute | solution.py:74
  11.6 5.8 %block_inverses.1 = (bf16[4,4,128,256]{3,2,1,0:T(8,128)(2,1)S(1)}, bf16[4,4,128,256]{3,2,1,0:T(8,128)(2,1)S(1)}, bf16[4,4,128,256]{3,2,1,0:T(8,128)(2,1)S(1)}, f...) custom-call(bf16[144,256]{1,0:T(8,128)(2,1)S(1)} %get-tuple-element.38.refs_0_, ...), custom_call_target="tpu_custom_call" | custom-call | flops 6000000000 | bytes 1000000 | tf_op jit(solution)/shard_map/block_inverses/pallas_call | solution.py:441
  17.4 0.0 collective-permute-done.4.refs_6_
  17.4 0.6 collective-permute-done.5.refs_7_
  18.1 0.0 collective-permute-done.3.refs_5_
  18.1 0.0 copy-done.11
  18.1 0.0 copy-start
  18.1 2.7 %states.1 = (f32[2,128,512]{2,1,0:T(8,128)S(1)}, bf16[2,128,512]{2,1,0:T(8,128)(2,1)S(1)}) custom-call(bf16[144,256]{1,0:T(8,128)(2,1)S(1)} %get-tuple-element.38.refs_0_, bf16[144,256]{1,0:T(8,128)(2,1)S(1)} %collective-permute-done.refs_1_, bf16[144,256]{1,0:T(8,128)(2,1)S(1)} %collective-permute-done.1.refs_2_, ...), custom_call_target="tpu_custom_call" | custom-call | flops 4000000000 | bytes 1000000 | tf_op jit(solution)/shard_map/states/pallas_call | solution.py:454
  20.8 0.1 collective-permute-start.6
  20.9 2.7 %collective-permute-done.8.refs_0_ = bf16[128,1024]{1,0:T(8,128)(2,1)S(1)} collective-permute-done((bf16[128,1024]{1,0:T(8,128)(2,1)S(1)}, bf16[128,1024]{1,0:T(8,128)(2,1)S(1)}, u32[]{:S(2)}, u32[]{:S(2)}) %collective-permute-start.8) | collective-permute-done | bytes 262176 | tf_op jit(solution)/shard_map/late_exchange/ppermute | solution.py:74
  23.6 0.0 collective-permute-done.6.other_ref.refs_2_
  23.6 0.0 collective-permute-done.7.proj_other_ref.refs_4_
  23.6 0.0 copy-done
  23.7 0.0 copy-start.4
  23.7 0.0 copy-start.5
  23.7 0.0 copy-start.8
  23.7 0.0 copy-start.9
  23.7 0.8 far_projection.1
  24.5 1.4 %collective-permute-start.9 = (bf16[128,2048]{1,0:T(8,128)(2,1)S(1)}, bf16[128,2048]{1,0:T(8,128)(2,1)S(1)}, u32[]{:S(2)}, u32[]{:S(2)}) collective-permute-start(bf16[128,2048]{1,0:T(8,128)(2,1)S(1)} %far_projection.1), channel_id=1, source_target_pairs={{0,16},{8,24},{16,0},{24,8},{1,17},{9,25},{17,1},{25,9},{2,18},{10... | collective-permute-start | bytes 1572872 | tf_op jit(solution)/shard_map/projection_sum/ppermute | solution.py:74
  25.9 0.0 copy-done.4
  25.9 0.0 copy-done.5
  25.9 0.0 copy-done.8
  25.9 0.0 copy-done.9
  25.9 0.0 copy-start.6
  25.9 0.0 copy-start.2
  25.9 0.0 copy-start.3
  25.9 0.9 %home.1 = (f32[128,2048]{1,0:T(8,128)S(1)}, bf16[128,128]{1,0:T(8,128)(2,1)S(1)}, f32[128,128]{1,0:T(8,128)S(1)}) custom-call(bf16[1,128,2048]{2,1,0:T(8,128)(2,1)S(1)} %copy-done.5, bf16[1,128,2048]{2,1,0:T(8,128)(2,1)S(1)} %copy-done.4, f32[2,128,512]{2,1,0:T(8,128)S(1)} %get-tuple-element.51.keep_ref.refs_1_, ...), custom_call_target="tpu_custom_call" | custom-call | flops 1000 | bytes 1000 | tf_op jit(solution)/shard_map/home/pallas_call | solution.py:475
  26.8 0.0 copy-start.1
  26.8 11.7 %collective-permute-done.9.refs_0_ = bf16[128,2048]{1,0:T(8,128)(2,1)S(1)} collective-permute-done((bf16[128,2048]{1,0:T(8,128)(2,1)S(1)}, bf16[128,2048]{1,0:T(8,128)(2,1)S(1)}, u32[]{:S(2)}, u32[]{:S(2)}) %collective-permute-start.9) | collective-permute-done | bytes 524320 | tf_op jit(solution)/shard_map/projection_sum/ppermute | solution.py:74
  38.5 0.0 copy-done.6
  38.5 0.5 dispatch.1
  39.0 20.3 %all_to_all.10.rows_ref = bf16[32,4,2048]{2,1,0:T(4,128)(2,1)S(1)} all-to-all(bf16[32,4,2048]{2,1,0:T(4,128)(2,1)S(1)} %get-tuple-element.58), channel_id=1, replica_groups=mesh['ctx'=4,'exp'=8] {'exp','ctx'}, dimensions={0} | all-to-all | bytes 1048576 | tf_op jit(solution)/shard_map/to_experts/all_to_all | solution.py:497
  59.3 0.0 copy-done.2
  59.3 0.0 copy-done.3
  59.3 0.0 copy-done.1
  59.3 0.0 copy-start.7
  59.3 0.0 copy-start.10
  59.3 1.1 %experts.1 = bf16[32,4,2048]{2,1,0:T(4,128)(2,1)S(1)} custom-call(bf16[32,4,2048]{2,1,0:T(4,128)(2,1)S(1)} %all_to_all.10.rows_ref, bf16[1,2048,512]{2,1,0:T(8,128)(2,1)S(1)} %copy-done.1, bf16[1,2048,512]{2,1,0:T(8,128)(2,1)S(1)} %copy-done.2, bf16[1,512,2048]{2,1,0:T(8,128)(2,1)S(1)} %copy-done.3), custom_call_target="tpu_custom_call" | custom-call | tf_op jit(solution)/shard_map/experts/pallas_call | solution.py:499
  60.5 18.4 %all_to_all.11.back_ref = bf16[32,4,2048]{2,1,0:T(4,128)(2,1)S(1)} all-to-all(bf16[32,4,2048]{2,1,0:T(4,128)(2,1)S(1)} %experts.1), channel_id=1, replica_groups=mesh['ctx'=4,'exp'=8] {'exp','ctx'}, dimensions={0} | all-to-all | bytes 1048576 | tf_op jit(solution)/shard_map/from_experts/all_to_all | solution.py:505
  78.9 0.0 copy-done.7
  78.9 0.0 copy-done.10
  78.9 1.3 %combine.1 = bf16[1,128,2048]{2,1,0:T(8,128)(2,1)} custom-call(f32[128,2048]{1,0:T(8,128)S(1)} %get-tuple-element.56.hidden_ref, f32[128,128]{1,0:T(8,128)S(1)} %get-tuple-element.57.table_ref, bf16[32,4,2048]{2,1,0:T(4,128)(2,1)S(1)} %all_to_all.11.back_ref, s32[1,128]{1,0:T(1,128)S(1)} %copy-done.10, f32[1,2048]{1,0:T(1,128)S(1)} %bitcast.8), custom_call_target="tpu_custom_call" | custom-call | tf_op jit(solution)/shard_map/combine/pallas_call | solution.py:507
Async XLA Ops:
  0.0 23.6 %collective-permute-start.7 = (bf16[512,2048]{1,0:T(8,128)(2,1)}, bf16[512,2048]{1,0:T(8,128)(2,1)S(1)}, u32[]{:S(2)}, u32[]{:S(2)}) collective-permute-start(bf16[512,2048]{1,0:T(8,128)(2,1)} %refs_3_.1), channel_id=1, source_target_pairs={{0,8},{8,0},{16,24},{24,16},{1,9},{9,1},{17,25},{25,17},{2,10},{10... | collective-permute-start | bytes 6291464 | tf_op jit(solution)/shard_map/late_exchange/ppermute | solution.py:74
  2.0 4.5 %collective-permute-start = (bf16[144,256]{1,0:T(8,128)(2,1)S(1)}, bf16[144,256]{1,0:T(8,128)(2,1)S(1)}, u32[]{:S(2)}, u32[]{:S(2)}) collective-permute-start(bf16[144,256]{1,0:T(8,128)(2,1)S(1)} %get-tuple-element.33), channel_id=1, source_target_pairs={{0,8},{8,0},{16,24},{24,16},{1,9},{9,1},{17,25},{25,17},{2,10},{10... | collective-permute-start | bytes 221192 | tf_op jit(solution)/shard_map/heads_exchange/ppermute | solution.py:74
  2.1 5.6 %collective-permute-start.1 = (bf16[144,256]{1,0:T(8,128)(2,1)S(1)}, bf16[144,256]{1,0:T(8,128)(2,1)S(1)}, u32[]{:S(2)}, u32[]{:S(2)}) collective-permute-start(bf16[144,256]{1,0:T(8,128)(2,1)S(1)} %get-tuple-element.34), channel_id=1, source_target_pairs={{0,16},{8,24},{16,0},{24,8},{1,17},{9,25},{17,1},{25,9},{2,18},{10... | collective-permute-start | bytes 221192 | tf_op jit(solution)/shard_map/heads_exchange/ppermute | solution.py:74
  5.1 4.6 %collective-permute-start.2 = (bf16[144,256]{1,0:T(8,128)(2,1)S(1)}, bf16[144,256]{1,0:T(8,128)(2,1)S(1)}, u32[]{:S(2)}, u32[]{:S(2)}) collective-permute-start(bf16[144,256]{1,0:T(8,128)(2,1)S(1)} %get-tuple-element.35), channel_id=1, source_target_pairs={{0,24},{8,16},{16,8},{24,0},{1,25},{9,17},{17,9},{25,1},{2,26},{10... | collective-permute-start | bytes 221192 | tf_op jit(solution)/shard_map/heads_exchange/ppermute | solution.py:74
  5.1 12.3 %collective-permute-start.4 = (bf16[128,768]{1,0:T(8,128)(2,1)S(1)}, bf16[128,768]{1,0:T(8,128)(2,1)S(1)}, u32[]{:S(2)}, u32[]{:S(2)}) collective-permute-start(bf16[128,768]{1,0:T(8,128)(2,1)S(1)} %get-tuple-element.44), channel_id=1, source_target_pairs={{0,16},{8,24},{16,0},{24,8},{1,17},{9,25},{17,1},{25,9},{2,18},{10... | collective-permute-start | bytes 589832 | tf_op jit(solution)/shard_map/heads_exchange/ppermute | solution.py:74
  6.5 11.6 %collective-permute-start.5 = (bf16[128,768]{1,0:T(8,128)(2,1)S(1)}, bf16[128,768]{1,0:T(8,128)(2,1)S(1)}, u32[]{:S(2)}, u32[]{:S(2)}) collective-permute-start(bf16[128,768]{1,0:T(8,128)(2,1)S(1)} %get-tuple-element.45), channel_id=1, source_target_pairs={{0,24},{8,16},{16,8},{24,0},{1,25},{9,17},{17,9},{25,1},{2,26},{10... | collective-permute-start | bytes 589832 | tf_op jit(solution)/shard_map/heads_exchange/ppermute | solution.py:74
  9.6 8.4 %copy-start.11 = (f32[128]{0:T(128)S(1)}, f32[128]{0:T(128)}, u32[]{:S(2)}) copy-start(f32[128]{0:T(128)} %param.23) | copy-start | bytes 1540
  9.6 8.4 %collective-permute-start.3 = (bf16[128,768]{1,0:T(8,128)(2,1)S(1)}, bf16[128,768]{1,0:T(8,128)(2,1)S(1)}, u32[]{:S(2)}, u32[]{:S(2)}) collective-permute-start(bf16[128,768]{1,0:T(8,128)(2,1)S(1)} %get-tuple-element.43), channel_id=1, source_target_pairs={{0,8},{8,0},{16,24},{24,16},{1,9},{9,1},{17,25},{25,17},{2,10},{10... | collective-permute-start | bytes 589832 | tf_op jit(solution)/shard_map/late_exchange/ppermute | solution.py:74
  9.7 13.9 %collective-permute-start.8 = (bf16[128,1024]{1,0:T(8,128)(2,1)S(1)}, bf16[128,1024]{1,0:T(8,128)(2,1)S(1)}, u32[]{:S(2)}, u32[]{:S(2)}) collective-permute-start(bf16[128,1024]{1,0:T(8,128)(2,1)S(1)} %get-tuple-element.55), channel_id=1, source_target_pairs={{0,16},{8,24},{16,0},{24,8},{1,17},{9,25},{17,1},{25,9},{2,18},{10... | collective-permute-start | bytes 786440 | tf_op jit(solution)/shard_map/late_exchange/ppermute | solution.py:74
  18.1 5.6 %copy-start = (bf16[512,2048]{1,0:T(8,128)(2,1)S(1)}, bf16[512,2048]{1,0:T(8,128)(2,1)}, u32[]{:S(2)}) copy-start(bf16[512,2048]{1,0:T(8,128)(2,1)} %refs_3_.1) | copy-start | bytes 6291460
  20.8 2.9 %collective-permute-start.6 = (bf16[2,128,512]{2,1,0:T(8,128)(2,1)S(1)}, bf16[2,128,512]{2,1,0:T(8,128)(2,1)S(1)}, u32[]{:S(2)}, u32[]{:S(2)}) collective-permute-start(bf16[2,128,512]{2,1,0:T(8,128)(2,1)S(1)} %get-tuple-element.52), channel_id=1, source_target_pairs={{0,8},{8,0},{16,24},{24,16},{1,9},{9,1},{17,25},{25,17},{2,10},{10... | collective-permute-start | bytes 786440 | tf_op jit(solution)/shard_map/far_projection/ppermute | solution.py:74
  23.7 2.2 %copy-start.4 = (bf16[1,128,2048]{2,1,0:T(8,128)(2,1)S(1)}, bf16[1,128,2048]{2,1,0:T(8,128)(2,1)}, u32[]{:S(2)}) copy-start(bf16[1,128,2048]{2,1,0:T(8,128)(2,1)} %gate_ref.2) | copy-start | bytes 1572868
  23.7 2.2 %copy-start.5 = (bf16[1,128,2048]{2,1,0:T(8,128)(2,1)S(1)}, bf16[1,128,2048]{2,1,0:T(8,128)(2,1)}, u32[]{:S(2)}) copy-start(bf16[1,128,2048]{2,1,0:T(8,128)(2,1)} %residual_ref.1) | copy-start | bytes 1572868
  23.7 2.2 %copy-start.8 = (s32[1,128,10]{1,0,2:T(1,128)S(1)}, s32[1,128,10]{1,0,2:T(1,128)}, u32[]{:S(2)}) copy-start(s32[1,128,10]{1,0,2:T(1,128)} %param.27) | copy-start | bytes 15364
  23.7 2.2 %copy-start.9 = (f32[1,128,10]{1,0,2:T(1,128)S(1)}, f32[1,128,10]{1,0,2:T(1,128)}, u32[]{:S(2)}) copy-start(f32[1,128,10]{1,0,2:T(1,128)} %param.28) | copy-start | bytes 15364
  24.5 14.0 %collective-permute-start.9 = (bf16[128,2048]{1,0:T(8,128)(2,1)S(1)}, bf16[128,2048]{1,0:T(8,128)(2,1)S(1)}, u32[]{:S(2)}, u32[]{:S(2)}) collective-permute-start(bf16[128,2048]{1,0:T(8,128)(2,1)S(1)} %far_projection.1), channel_id=1, source_target_pairs={{0,16},{8,24},{16,0},{24,8},{1,17},{9,25},{17,1},{25,9},{2,18},{10... | collective-permute-start | bytes 1572872 | tf_op jit(solution)/shard_map/projection_sum/ppermute | solution.py:74
  25.9 12.6 %copy-start.6 = (f32[2048]{0:T(1024)S(1)}, f32[2048]{0:T(1024)}, u32[]{:S(2)}) copy-start(f32[2048]{0:T(1024)} %param.26) | copy-start | bytes 24580
  25.9 33.4 %copy-start.2 = (bf16[1,2048,512]{2,1,0:T(8,128)(2,1)S(1)}, bf16[1,2048,512]{2,1,0:T(8,128)(2,1)}, u32[]{:S(2)}) copy-start(bf16[1,2048,512]{2,1,0:T(8,128)(2,1)} %up_ref.1) | copy-start | bytes 6291460
  25.9 33.4 %copy-start.3 = (bf16[1,512,2048]{2,1,0:T(8,128)(2,1)S(1)}, bf16[1,512,2048]{2,1,0:T(8,128)(2,1)}, u32[]{:S(2)}) copy-start(bf16[1,512,2048]{2,1,0:T(8,128)(2,1)} %down_ref.1) | copy-start | bytes 6291460
  26.8 32.5 %copy-start.1 = (bf16[1,2048,512]{2,1,0:T(8,128)(2,1)S(1)}, bf16[1,2048,512]{2,1,0:T(8,128)(2,1)}, u32[]{:S(2)}) copy-start(bf16[1,2048,512]{2,1,0:T(8,128)(2,1)} %gate_ref.3) | copy-start | bytes 6291460
  59.3 19.6 %copy-start.7 = (f32[2048]{0:T(1024)S(1)}, f32[2048]{0:T(1024)}, u32[]{:S(2)}) copy-start(f32[2048]{0:T(1024)} %param.33) | copy-start | bytes 24580
  59.3 19.6 %copy-start.10 = (s32[1,128]{1,0:T(1,128)S(1)}, s32[1,128]{1,0:T(1,128)}, u32[]{:S(2)}) copy-start(s32[1,128]{1,0:T(1,128)} %mask_ref.1) | copy-start | bytes 1540

commit v7 on v6

--- a/solution.py
+++ b/solution.py
@@ -74,9 +74,9 @@
     return lax.ppermute(x, "ctx", pairs)
 
 
-def pack_kernel(n, kw, vw, k_ref, w_ref, d_ref, q_ref, v_ref, g_ref, *outs):
+def pack_kernel(n, kw, vw, k_ref, w_ref, d_ref, q_ref, v_ref, *outs):
     local = vw // DK
-    keyed, asked, gated = outs[:n], outs[n : 2 * n], outs[2 * n :]
+    keyed, asked = outs[:n], outs[n:]
     me = lax.axis_index("ctx")
     tokens = k_ref.shape[1]
     heads = d_ref.shape[1]
@@ -94,9 +94,17 @@
             keyed[i][tokens:, at * LANES : (at + 1) * LANES] = aux[at * AUX : (at + 1) * AUX].astype(bf16)
         asked[i][:, 0:kw] = q_ref[0, :, kat]
         asked[i][:, kw:] = v_ref[0, :, pl.ds(pl.multiple_of(to * vw, LANES), vw)]
+
+
+def pack_late_kernel(n, vw, g_ref, proj_ref, *outs):
+    me = lax.axis_index("ctx")
+    gated, pieces = outs[: n // 2 - 1], outs[n // 2 - 1 :]
     for j, out in enumerate(gated):
         chip = lax.rem(me // 2 + j + 1, n // 2)
         out[...] = g_ref[0, :, pl.ds(pl.multiple_of(chip * 2 * vw, LANES), 2 * vw)]
+    for i, piece in enumerate(pieces):
+        columns = piece.shape[1]
+        piece[...] = proj_ref[:, i * columns : (i + 1) * columns]
 
 
 def head_rates(local, keyed, tokens):
@@ -274,24 +282,26 @@
         give_ref[j] = out_ref[moved(me, (j, 1), n)].astype(bf16)
 
 
-def chip_projection(me, keep, other, gate_ref, start, proj_ref, proj_other_ref, columns):
+def chip_projection(me, keep, other, gate_ref, start, proj_ref, proj_other_refs, first=0):
     vw = keep.shape[1]
     mixed = []
     for heads, core in ((keep, lax.rem(me, 2)), (other, 1 - lax.rem(me, 2))):
         gate = gate_ref[:, pl.ds(pl.multiple_of(start + core * vw, LANES), vw)].astype(f32)
         mixed.append((heads.astype(f32) * (gate / (1.0 + jnp.exp(-gate)))).astype(bf16))
-    for at in range(0, proj_ref.shape[1], columns):
-        here = slice(at, at + columns)
-        yield here, mm(mixed[0], proj_ref[:, here]) + mm(mixed[1], proj_other_ref[:, here])
-
-
-def far_kernel(n, *refs):
+    columns = proj_other_refs[0].shape[1]
+    for i, proj_other_ref in enumerate(proj_other_refs, first):
+        here = slice(i * columns, (i + 1) * columns)
+        yield here, mm(mixed[0], proj_ref[:, here]) + mm(mixed[1], proj_other_ref[...])
+
+
+def far_kernel(n, first, *refs):
     gated = refs[: n // 2 - 1]
-    keep_ref, other_ref, proj_ref, proj_other_ref, *sums = refs[n // 2 - 1 :]
+    keep_ref, other_ref, *refs = refs[n // 2 - 1 :]
+    proj_ref, proj_other_ref, *sums = refs
     me = lax.axis_index("ctx")
     for j, (gate_ref, out) in enumerate(zip(gated, sums), 1):
-        for here, part in chip_projection(me, keep_ref[j], other_ref[j], gate_ref, 0, proj_ref, proj_other_ref, 512):
-            out[:, here] = part.astype(bf16)
+        for _, part in chip_projection(me, keep_ref[j], other_ref[j], gate_ref, 0, proj_ref, [proj_other_ref], first):
+            out[...] = part.astype(bf16)
 
 
 def home_kernel(
@@ -300,19 +310,22 @@
     gate_ref,
     keep_ref,
     other_ref,
-    proj_ref,
-    proj_other_ref,
     ids_ref,
     weight_ref,
-    base_ref,
-    picker_ref,
-    table_ref,
+    *refs,
 ):
+    proj_ref, *proj_other_refs = refs[:3]
+    first_refs, (base_ref, picker_ref, table_ref) = refs[3:-3], refs[-3:]
     me = lax.axis_index("ctx")
     start = me // 2 * 2 * keep_ref.shape[2]
     gate_ref = gate_ref.at[0]
-    for here, part in chip_projection(me, keep_ref[0], other_ref[0], gate_ref, start, proj_ref, proj_other_ref, 512):
-        base_ref[:, here] = residual_ref[0, :, here].astype(f32) + part
+    parts = chip_projection(me, keep_ref[0], other_ref[0], gate_ref, start, proj_ref, proj_other_refs)
+    for i, (here, part) in enumerate(parts):
+        total = residual_ref[0, :, here].astype(f32) + part
+        if i == 0:
+            for first in first_refs:
+                total = total + first[...].astype(f32)
+        base_ref[:, here] = total
     slots, tokens = table_ref.shape
     slot = iota((slots, tokens), 0)
     place = slot // CAP
@@ -338,8 +351,10 @@
     step = 512
     for c in range(0, width, step):
         total = base_ref[:, c : c + step]
-        for part in part_refs:
-            total = total + part[:, c : c + step].astype(f32)
+        at = c - (width - part_refs[0].shape[1])
+        if at >= 0:
+            for part in part_refs:
+                total = total + part[:, at : at + step].astype(f32)
         hidden_ref[:, c : c + step] = total
         squares = squares + jnp.sum(total * total, axis=1, keepdims=True)
     scale = lax.rsqrt(squares * (1.0 / width) + EPS)
@@ -425,11 +440,17 @@
         packed = pl.pallas_call(
             functools.partial(pack_kernel, n, kw, vw),
             out_shape=[keyed_shape] * n
-            + [shape((tokens, kw + vw), bf16)] * n
-            + [shape((tokens, 2 * vw), bf16)] * (chips - 1),
+            + [shape((tokens, kw + vw), bf16)] * n,
             compiler_params=compiler_params(16),
-        )(*in_hbm(keys, write_rate.transpose(0, 2, 1), decay.transpose(0, 2, 1), queries, values, out_gate))
-        keyed, asked, gated = list(packed[:n]), list(packed[n : 2 * n]), packed[2 * n :]
+        )(*in_hbm(keys, write_rate.transpose(0, 2, 1), decay.transpose(0, 2, 1), queries, values))
+        keyed, asked = list(packed[:n]), list(packed[n:])
+    with jax.named_scope("pack_late"):
+        late = pl.pallas_call(
+            functools.partial(pack_late_kernel, n, vw),
+            out_shape=[shape((tokens, 2 * vw), bf16)] * (chips - 1) + [shape((out_proj.shape[0], width // 2), bf16)] * 2,
+            compiler_params=compiler_params(16),
+        )(*in_hbm(out_gate, out_proj))
+        gated, pieces = late[: chips - 1], late[chips - 1 :]
     with jax.named_scope("heads_exchange"):
         order = [i for i, route in enumerate(ways) if route[0]] + [1]
         for i in order:
@@ -445,11 +466,10 @@
             cost_estimate=pl.CostEstimate(flops=6 * 10**9, bytes_accessed=10**6, transcendentals=0),
         )(*keyed)
     with jax.named_scope("late_exchange"):
-        proj = out_proj
         keyed, asked[1], gated = lax.optimization_barrier((keyed, asked[1], gated))
         asked[1] = send(asked[1], ways[1], n)
         gated = [send(gate, (j, 0), n) for j, gate in enumerate(gated, 1)]
-        proj_other = send(proj, (0, 1), n)
+        proj_other = [send(piece, (0, 1), n) for piece in pieces]
     with jax.named_scope("states"):
         keep, give = pl.pallas_call(
             functools.partial(state_kernel, n, kw, vw),
@@ -462,37 +482,42 @@
             compiler_params=compiler_params(16),
             cost_estimate=pl.CostEstimate(flops=4 * 10**9, bytes_accessed=10**6, transcendentals=0),
         )(*keyed, *asked, *inverses, head_gain.reshape(1, -1))
-    with jax.named_scope("far_projection"):
-        other = send(give, (0, 1), n)
-        sums = pl.pallas_call(
-            functools.partial(far_kernel, n),
-            out_shape=[shape((tokens, width), bf16)] * (chips - 1),
-            compiler_params=compiler_params(16),
-        )(*gated, keep, other, out_proj, proj_other)
-    with jax.named_scope("projection_sum"):
-        parts = [send(part, (j, 0), n) for j, part in enumerate(sums, 1)]
+    other = send(give, (0, 1), n)
+    parts = []
+    for i, piece in enumerate(proj_other):
+        with jax.named_scope("far_projection"):
+            sums = pl.pallas_call(
+                functools.partial(far_kernel, n, i),
+                out_shape=[shape((tokens, width // 2), bf16)] * (chips - 1),
+                compiler_params=compiler_params(16),
+                cost_estimate=pl.CostEstimate(flops=1000, bytes_accessed=1000, transcendentals=0),
+            )(*gated, keep, other, out_proj, piece)
+        keep = lax.optimization_barrier((sums, keep))[1]
+        with jax.named_scope("projection_sum"):
+            parts.append([send(part, (j, 0), n) for j, part in enumerate(sums, 1)])
     with jax.named_scope("home"):
         base, picker, table = pl.pallas_call(
             functools.partial(home_kernel, n),
             out_shape=[shape((tokens, width), f32), shape((slots, tokens), bf16), shape((slots, tokens), f32)],
             compiler_params=compiler_params(16),
-            cost_estimate=pl.CostEstimate(flops=1000, bytes_accessed=1000, transcendentals=0),
+            cost_estimate=pl.CostEstimate(flops=6 * 10**9, bytes_accessed=1000, transcendentals=0),
         )(
             residual,
             out_gate,
             keep,
             other,
-            out_proj,
-            proj_other,
             expert_ids.transpose(2, 0, 1),
             route_weight.transpose(2, 0, 1),
+            out_proj,
+            *proj_other,
+            *parts[0],
         )
     with jax.named_scope("dispatch"):
         hidden, rows = pl.pallas_call(
             dispatch_kernel,
             out_shape=[shape((tokens, width), f32), shape((devices, CAP, width), bf16)],
             compiler_params=compiler_params(24),
-        )(base, ffn_gain.reshape(1, -1), picker, *parts)
+        )(base, ffn_gain.reshape(1, -1), picker, *parts[1])
     with jax.named_scope("to_experts"):
         came = lax.all_to_all(rows, ("exp", "ctx"), 0, 0, tiled=True)
     with jax.named_scope("experts"):

time: 80.3 us -> 80.1 us (level)
  waiting for transfers between devices: 17.8 us -> 13.2 us
  Pallas kernels: 14.6 us -> 16.6 us
  starting transfers between devices: 8.85 us -> 10.1 us
  blocking collectives: 38.7 us -> 39.8 us
    ppermute x10 -> x12, waiting for transfers between devices: 17.8 us -> 13.2 us  [send(): return lax.ppermute(x, 'ctx', pairs)]
    pallas_call x1 -> x3, Pallas kernels: 0.79 us -> 2.98 us  [the longest x1 1.92 us: local_part(): pl.pallas_call(functools.partial(pack_late_kernel, n, vw), out_shape=[sha...]
    ppermute x10 -> x12, starting transfers between devices: 8.85 us -> 10.1 us  [send(): return lax.ppermute(x, 'ctx', pairs)]
    all_to_all x1, blocking collectives: 20.3 us -> 21.4 us  [local_part(): came = lax.all_to_all(rows, ('exp', 'ctx'), 0, 0, tiled=True)]
  transfers between devices with their start and end apart: 10 -> 12, of which waited for: 5 -> 4; matrix products, arithmetic and copies ran while one was open for 0% -> 0% of each run, Pallas kernels for 14% -> 15%
where the time goes in v7:
time: 80.1 us; the launch traced here: 79.9 us
  blocking collectives  39.8 us (50%)
  Pallas kernels  16.6 us (21%)
  waiting for transfers between devices  13.2 us (16%)
  starting transfers between devices  10.1 us (13%)
    all_to_all x1, blocking collectives, local_part(): came = lax.all_to_all(rows, ('exp', 'ctx'), 0, 0, tiled=True)  21.4 us
    all_to_all x1, blocking collectives, local_part(): back = lax.all_to_all(done, ('exp', 'ctx'), 0, 0, tiled=True)  18.4 us
    ppermute x12, waiting for transfers between devices, send(): return lax.ppermute(x, 'ctx', pairs)  13.2 us
    ppermute x12, starting transfers between devices, send(): return lax.ppermute(x, 'ctx', pairs)  10.1 us
    pallas_call x1, Pallas kernels, local_part(): pl.pallas_call(functools.partial(inverse_kernel, n, local), out_shape=[wi...  5.83 us
    pallas_call x1, Pallas kernels, local_part(): pl.pallas_call(functools.partial(state_kernel, n, kw, vw), out_shape=[sha...  2.68 us
    pallas_call x1, Pallas kernels, local_part(): pl.pallas_call(functools.partial(pack_late_kernel, n, vw), out_shape=[sha...  1.92 us
  transfers between devices with their start and end apart: 12, of which 4 were waited for; matrix products, arithmetic and copies ran while one was open for 0% of the time, Pallas kernels for 15%

profile of v7, /device:TPU:0, one launch (start us, length us, event | category | flops | bytes accessed | tf_op | source)
XLA Modules:
  0.0 79.9 jit_solution(1135629830629502731)
XLA Ops:
  0.0 1.4 %pack.1 = (bf16[144,256]{1,0:T(8,128)(2,1)S(1)}, bf16[144,256]{1,0:T(8,128)(2,1)S(1)}, bf16[144,256]{1,0:T(8,128)(2,1)S(1)}, bf16[144,256]{1,0:T(8,128)(2,1)S(1)...) custom-call(bf16[1,128,1024]{2,1,0:T(8,128)(2,1)} %k_ref.1, ...), custom_call_target="tpu_custom_call" | custom-call | tf_op jit(solution)/shard_map/pack/pallas_call | solution.py:440
  1.4 0.5 collective-permute-start
  1.9 2.6 %collective-permute-start.1 = (bf16[144,256]{1,0:T(8,128)(2,1)S(1)}, bf16[144,256]{1,0:T(8,128)(2,1)S(1)}, u32[]{:S(2)}, u32[]{:S(2)}) collective-permute-start(bf16[144,256]{1,0:T(8,128)(2,1)S(1)} %get-tuple-element.38), channel_id=1, source_target_pairs={{0,16},{8,24},{16,0},{24,8},{1,17},{9,25},{17,1},{25,9},{2,18},{10... | collective-permute-start | bytes 221192 | tf_op jit(solution)/shard_map/heads_exchange/ppermute | solution.py:74
  4.5 0.1 collective-permute-start.2
  4.5 1.7 %collective-permute-start.5 = (bf16[128,768]{1,0:T(8,128)(2,1)S(1)}, bf16[128,768]{1,0:T(8,128)(2,1)S(1)}, u32[]{:S(2)}, u32[]{:S(2)}) collective-permute-start(bf16[128,768]{1,0:T(8,128)(2,1)S(1)} %get-tuple-element.49), channel_id=1, source_target_pairs={{0,16},{8,24},{16,0},{24,8},{1,17},{9,25},{17,1},{25,9},{2,18},{10... | collective-permute-start | bytes 589832 | tf_op jit(solution)/shard_map/heads_exchange/ppermute | solution.py:74
  6.3 0.0 collective-permute-start.6
  6.3 1.9 %pack_late.1 = (bf16[128,1024]{1,0:T(8,128)(2,1)S(1)}, bf16[512,1024]{1,0:T(8,128)(2,1)S(1)}, bf16[512,1024]{1,0:T(8,128)(2,1)S(1)}) custom-call(bf16[1,128,2048]{2,1,0:T(8,128)(2,1)} %gate_ref.2, bf16[512,2048]{1,0:T(8,128)(2,1)} %refs_0_.1), custom_call_target="tpu_custom_call" | custom-call | tf_op jit(solution)/shard_map/pack_late/pallas_call | solution.py:448
  8.2 0.0 collective-permute-done.refs_1_
  8.2 0.5 collective-permute-start.8
  8.7 0.0 collective-permute-done.1.refs_2_
  8.7 0.1 collective-permute-start.9
  8.8 0.0 collective-permute-done.2.refs_3_
  8.8 0.0 copy-start.11
  8.8 0.4 collective-permute-start.4
  9.2 5.8 %block_inverses.1 = (bf16[4,4,128,256]{3,2,1,0:T(8,128)(2,1)S(1)}, bf16[4,4,128,256]{3,2,1,0:T(8,128)(2,1)S(1)}, bf16[4,4,128,256]{3,2,1,0:T(8,128)(2,1)S(1)}, f...) custom-call(bf16[144,256]{1,0:T(8,128)(2,1)S(1)} %get-tuple-element.43.refs_0_, ...), custom_call_target="tpu_custom_call" | custom-call | flops 6000000000 | bytes 1000000 | tf_op jit(solution)/shard_map/block_inverses/pallas_call | solution.py:462
  15.0 0.0 collective-permute-done.5.refs_6_
  15.0 1.8 %collective-permute-start.3 = (bf16[128,1024]{1,0:T(8,128)(2,1)S(1)}, bf16[128,1024]{1,0:T(8,128)(2,1)S(1)}, u32[]{:S(2)}, u32[]{:S(2)}) collective-permute-start(bf16[128,1024]{1,0:T(8,128)(2,1)S(1)} %get-tuple-element.42), channel_id=1, source_target_pairs={{0,16},{8,24},{16,0},{24,8},{1,17},{9,25},{17,1},{25,9},{2,18},{10... | collective-permute-start | bytes 786440 | tf_op jit(solution)/shard_map/late_exchange/ppermute | solution.py:74
  16.8 0.3 collective-permute-done.6.refs_7_
  17.1 0.0 collective-permute-done.4.refs_5_
  17.1 0.0 copy-done.11
  17.1 0.0 copy-start
  17.1 2.7 %states.1 = (f32[2,128,512]{2,1,0:T(8,128)S(1)}, bf16[2,128,512]{2,1,0:T(8,128)(2,1)S(1)}) custom-call(bf16[144,256]{1,0:T(8,128)(2,1)S(1)} %get-tuple-element.43.refs_0_, bf16[144,256]{1,0:T(8,128)(2,1)S(1)} %collective-permute-done.refs_1_, bf16[144,256]{1,0:T(8,128)(2,1)S(1)} %collective-permute-done.1.refs_2_, ...), custom_call_target="tpu_custom_call" | custom-call | flops 4000000000 | bytes 1000000 | tf_op jit(solution)/shard_map/states/pallas_call | solution.py:474
  19.8 0.2 collective-permute-start.7
  20.1 3.4 %collective-permute-done.3.refs_0_ = bf16[128,1024]{1,0:T(8,128)(2,1)S(1)} collective-permute-done((bf16[128,1024]{1,0:T(8,128)(2,1)S(1)}, bf16[128,1024]{1,0:T(8,128)(2,1)S(1)}, u32[]{:S(2)}, u32[]{:S(2)}) %collective-permute-start.3) | collective-permute-done | bytes 262176 | tf_op jit(solution)/shard_map/late_exchange/ppermute | solution.py:74
  23.4 0.0 collective-permute-done.7.refs_2_.other_ref
  23.4 0.0 collective-permute-done.8.refs_4_.refs_1_
  23.4 0.0 copy-done
  23.4 0.5 far_projection.2
  24.0 0.0 copy-start.4
  24.0 0.0 copy-start.8
  24.0 0.0 copy-start.9
  24.0 0.0 copy-start.10
  24.0 1.8 %collective-permute-start.10 = (bf16[128,1024]{1,0:T(8,128)(2,1)S(1)}, bf16[128,1024]{1,0:T(8,128)(2,1)S(1)}, u32[]{:S(2)}, u32[]{:S(2)}) collective-permute-start(bf16[128,1024]{1,0:T(8,128)(2,1)S(1)} %far_projection.2), channel_id=1, source_target_pairs={{0,16},{8,24},{16,0},{24,8},{1,17},{9,25},{17,1},{25,9},{2,18},{10... | collective-permute-start | bytes 786440 | tf_op jit(solution)/shard_map/projection_sum/ppermute | solution.py:74
  25.8 0.0 collective-permute-done.9.refs_4_.refs_2_
  25.8 0.5 far_projection.3
  26.4 0.4 collective-permute-start.11
  26.7 6.6 %collective-permute-done.10.refs_3_ = bf16[128,1024]{1,0:T(8,128)(2,1)S(1)} collective-permute-done((bf16[128,1024]{1,0:T(8,128)(2,1)S(1)}, bf16[128,1024]{1,0:T(8,128)(2,1)S(1)}, u32[]{:S(2)}, u32[]{:S(2)}) %collective-permute-start.10) | collective-permute-done | bytes 262176 | tf_op jit(solution)/shard_map/projection_sum/ppermute | solution.py:74
  33.3 0.0 copy-done.4
  33.3 0.0 copy-done.8
  33.3 0.0 copy-done.9
  33.3 0.0 copy-done.10
  33.3 0.0 copy-start.5
  33.4 0.0 copy-start.2
  33.4 0.0 copy-start.3
  33.4 0.9 %home.1 = (f32[128,2048]{1,0:T(8,128)S(1)}, bf16[128,128]{1,0:T(8,128)(2,1)S(1)}, f32[128,128]{1,0:T(8,128)S(1)}) custom-call(bf16[1,128,2048]{2,1,0:T(8,128)(2,1)S(1)} %copy-done.8, bf16[1,128,2048]{2,1,0:T(8,128)(2,1)S(1)} %copy-done.4, f32[2,128,512]{2,1,0:T(8,128)S(1)} %get-tuple-element.61.refs_1_.keep_ref, ...), custom_call_target="tpu_custom_call" | custom-call | flops 6000000000 | bytes 1000 | tf_op jit(solution)/shard_map/home/pallas_call | solution.py:499
  34.3 0.0 copy-start.1
  34.3 2.9 %collective-permute-done.11.refs_0_ = bf16[128,1024]{1,0:T(8,128)(2,1)S(1)} collective-permute-done((bf16[128,1024]{1,0:T(8,128)(2,1)S(1)}, bf16[128,1024]{1,0:T(8,128)(2,1)S(1)}, u32[]{:S(2)}, u32[]{:S(2)}) %collective-permute-start.11) | collective-permute-done | bytes 262176 | tf_op jit(solution)/shard_map/projection_sum/ppermute | solution.py:74
  37.2 0.0 copy-done.5
  37.2 0.5 dispatch.1
  37.7 21.4 %all_to_all.10.rows_ref = bf16[32,4,2048]{2,1,0:T(4,128)(2,1)S(1)} all-to-all(bf16[32,4,2048]{2,1,0:T(4,128)(2,1)S(1)} %get-tuple-element.66), channel_id=1, replica_groups=mesh['ctx'=4,'exp'=8] {'exp','ctx'}, dimensions={0} | all-to-all | bytes 1048576 | tf_op jit(solution)/shard_map/to_experts/all_to_all | solution.py:522
  59.1 0.0 copy-done.2
  59.1 0.0 copy-done.3
  59.1 0.0 copy-done.1
  59.1 0.0 copy-start.6
  59.1 0.0 copy-start.7
  59.1 1.1 %experts.1 = bf16[32,4,2048]{2,1,0:T(4,128)(2,1)S(1)} custom-call(bf16[32,4,2048]{2,1,0:T(4,128)(2,1)S(1)} %all_to_all.10.rows_ref, bf16[1,2048,512]{2,1,0:T(8,128)(2,1)S(1)} %copy-done.1, bf16[1,2048,512]{2,1,0:T(8,128)(2,1)S(1)} %copy-done.2, bf16[1,512,2048]{2,1,0:T(8,128)(2,1)S(1)} %copy-done.3), custom_call_target="tpu_custom_call" | custom-call | tf_op jit(solution)/shard_map/experts/pallas_call | solution.py:524
  60.2 18.4 %all_to_all.11.back_ref = bf16[32,4,2048]{2,1,0:T(4,128)(2,1)S(1)} all-to-all(bf16[32,4,2048]{2,1,0:T(4,128)(2,1)S(1)} %experts.1), channel_id=1, replica_groups=mesh['ctx'=4,'exp'=8] {'exp','ctx'}, dimensions={0} | all-to-all | bytes 1048576 | tf_op jit(solution)/shard_map/from_experts/all_to_all | solution.py:530
  78.6 0.0 copy-done.6
  78.6 0.0 copy-done.7
  78.6 1.3 %combine.1 = bf16[1,128,2048]{2,1,0:T(8,128)(2,1)} custom-call(f32[128,2048]{1,0:T(8,128)S(1)} %get-tuple-element.64.hidden_ref, f32[128,128]{1,0:T(8,128)S(1)} %get-tuple-element.65.table_ref, bf16[32,4,2048]{2,1,0:T(4,128)(2,1)S(1)} %all_to_all.11.back_ref, s32[1,128]{1,0:T(1,128)S(1)} %copy-done.7, f32[1,2048]{1,0:T(1,128)S(1)} %bitcast.8), custom_call_target="tpu_custom_call" | custom-call | tf_op jit(solution)/shard_map/combine/pallas_call | solution.py:532
Async XLA Ops:
  1.4 6.8 %collective-permute-start = (bf16[144,256]{1,0:T(8,128)(2,1)S(1)}, bf16[144,256]{1,0:T(8,128)(2,1)S(1)}, u32[]{:S(2)}, u32[]{:S(2)}) collective-permute-start(bf16[144,256]{1,0:T(8,128)(2,1)S(1)} %get-tuple-element.37), channel_id=1, source_target_pairs={{0,8},{8,0},{16,24},{24,16},{1,9},{9,1},{17,25},{25,17},{2,10},{10... | collective-permute-start | bytes 221192 | tf_op jit(solution)/shard_map/heads_exchange/ppermute | solution.py:74
  1.9 6.8 %collective-permute-start.1 = (bf16[144,256]{1,0:T(8,128)(2,1)S(1)}, bf16[144,256]{1,0:T(8,128)(2,1)S(1)}, u32[]{:S(2)}, u32[]{:S(2)}) collective-permute-start(bf16[144,256]{1,0:T(8,128)(2,1)S(1)} %get-tuple-element.38), channel_id=1, source_target_pairs={{0,16},{8,24},{16,0},{24,8},{1,17},{9,25},{17,1},{25,9},{2,18},{10... | collective-permute-start | bytes 221192 | tf_op jit(solution)/shard_map/heads_exchange/ppermute | solution.py:74
  4.5 4.3 %collective-permute-start.2 = (bf16[144,256]{1,0:T(8,128)(2,1)S(1)}, bf16[144,256]{1,0:T(8,128)(2,1)S(1)}, u32[]{:S(2)}, u32[]{:S(2)}) collective-permute-start(bf16[144,256]{1,0:T(8,128)(2,1)S(1)} %get-tuple-element.39), channel_id=1, source_target_pairs={{0,24},{8,16},{16,8},{24,0},{1,25},{9,17},{17,9},{25,1},{2,26},{10... | collective-permute-start | bytes 221192 | tf_op jit(solution)/shard_map/heads_exchange/ppermute | solution.py:74
  4.5 10.5 %collective-permute-start.5 = (bf16[128,768]{1,0:T(8,128)(2,1)S(1)}, bf16[128,768]{1,0:T(8,128)(2,1)S(1)}, u32[]{:S(2)}, u32[]{:S(2)}) collective-permute-start(bf16[128,768]{1,0:T(8,128)(2,1)S(1)} %get-tuple-element.49), channel_id=1, source_target_pairs={{0,16},{8,24},{16,0},{24,8},{1,17},{9,25},{17,1},{25,9},{2,18},{10... | collective-permute-start | bytes 589832 | tf_op jit(solution)/shard_map/heads_exchange/ppermute | solution.py:74
  6.3 10.8 %collective-permute-start.6 = (bf16[128,768]{1,0:T(8,128)(2,1)S(1)}, bf16[128,768]{1,0:T(8,128)(2,1)S(1)}, u32[]{:S(2)}, u32[]{:S(2)}) collective-permute-start(bf16[128,768]{1,0:T(8,128)(2,1)S(1)} %get-tuple-element.50), channel_id=1, source_target_pairs={{0,24},{8,16},{16,8},{24,0},{1,25},{9,17},{17,9},{25,1},{2,26},{10... | collective-permute-start | bytes 589832 | tf_op jit(solution)/shard_map/heads_exchange/ppermute | solution.py:74
  8.2 15.2 %collective-permute-start.8 = (bf16[512,1024]{1,0:T(8,128)(2,1)S(1)}, bf16[512,1024]{1,0:T(8,128)(2,1)S(1)}, u32[]{:S(2)}, u32[]{:S(2)}) collective-permute-start(bf16[512,1024]{1,0:T(8,128)(2,1)S(1)} %get-tuple-element.58), channel_id=1, source_target_pairs={{0,8},{8,0},{16,24},{24,16},{1,9},{9,1},{17,25},{25,17},{2,10},{10... | collective-permute-start | bytes 3145736 | tf_op jit(solution)/shard_map/late_exchange/ppermute | solution.py:74
  8.7 17.1 %collective-permute-start.9 = (bf16[512,1024]{1,0:T(8,128)(2,1)S(1)}, bf16[512,1024]{1,0:T(8,128)(2,1)S(1)}, u32[]{:S(2)}, u32[]{:S(2)}) collective-permute-start(bf16[512,1024]{1,0:T(8,128)(2,1)S(1)} %get-tuple-element.60), channel_id=1, source_target_pairs={{0,8},{8,0},{16,24},{24,16},{1,9},{9,1},{17,25},{25,17},{2,10},{10... | collective-permute-start | bytes 3145736 | tf_op jit(solution)/shard_map/late_exchange/ppermute | solution.py:74
  8.8 8.3 %copy-start.11 = (f32[128]{0:T(128)S(1)}, f32[128]{0:T(128)}, u32[]{:S(2)}) copy-start(f32[128]{0:T(128)} %param.23) | copy-start | bytes 1540
  8.8 8.3 %collective-permute-start.4 = (bf16[128,768]{1,0:T(8,128)(2,1)S(1)}, bf16[128,768]{1,0:T(8,128)(2,1)S(1)}, u32[]{:S(2)}, u32[]{:S(2)}) collective-permute-start(bf16[128,768]{1,0:T(8,128)(2,1)S(1)} %get-tuple-element.48), channel_id=1, source_target_pairs={{0,8},{8,0},{16,24},{24,16},{1,9},{9,1},{17,25},{25,17},{2,10},{10... | collective-permute-start | bytes 589832 | tf_op jit(solution)/shard_map/late_exchange/ppermute | solution.py:74
  15.0 8.4 %collective-permute-start.3 = (bf16[128,1024]{1,0:T(8,128)(2,1)S(1)}, bf16[128,1024]{1,0:T(8,128)(2,1)S(1)}, u32[]{:S(2)}, u32[]{:S(2)}) collective-permute-start(bf16[128,1024]{1,0:T(8,128)(2,1)S(1)} %get-tuple-element.42), channel_id=1, source_target_pairs={{0,16},{8,24},{16,0},{24,8},{1,17},{9,25},{17,1},{25,9},{2,18},{10... | collective-permute-start | bytes 786440 | tf_op jit(solution)/shard_map/late_exchange/ppermute | solution.py:74
  17.1 6.3 %copy-start = (bf16[512,2048]{1,0:T(8,128)(2,1)S(1)}, bf16[512,2048]{1,0:T(8,128)(2,1)}, u32[]{:S(2)}) copy-start(bf16[512,2048]{1,0:T(8,128)(2,1)} %refs_0_.1) | copy-start | bytes 6291460
  19.8 3.6 %collective-permute-start.7 = (bf16[2,128,512]{2,1,0:T(8,128)(2,1)S(1)}, bf16[2,128,512]{2,1,0:T(8,128)(2,1)S(1)}, u32[]{:S(2)}, u32[]{:S(2)}) collective-permute-start(bf16[2,128,512]{2,1,0:T(8,128)(2,1)S(1)} %get-tuple-element.57), channel_id=1, source_target_pairs={{0,8},{8,0},{16,24},{24,16},{1,9},{9,1},{17,25},{25,17},{2,10},{10... | collective-permute-start | bytes 786440 | tf_op jit(solution)/shard_map/ppermute | solution.py:74
  24.0 9.4 %copy-start.4 = (bf16[1,128,2048]{2,1,0:T(8,128)(2,1)S(1)}, bf16[1,128,2048]{2,1,0:T(8,128)(2,1)}, u32[]{:S(2)}) copy-start(bf16[1,128,2048]{2,1,0:T(8,128)(2,1)} %gate_ref.2) | copy-start | bytes 1572868
  24.0 9.3 %copy-start.8 = (bf16[1,128,2048]{2,1,0:T(8,128)(2,1)S(1)}, bf16[1,128,2048]{2,1,0:T(8,128)(2,1)}, u32[]{:S(2)}) copy-start(bf16[1,128,2048]{2,1,0:T(8,128)(2,1)} %residual_ref.1) | copy-start | bytes 1572868
  24.0 9.3 %copy-start.9 = (s32[1,128,10]{1,0,2:T(1,128)S(1)}, s32[1,128,10]{1,0,2:T(1,128)}, u32[]{:S(2)}) copy-start(s32[1,128,10]{1,0,2:T(1,128)} %param.27) | copy-start | bytes 15364
  24.0 9.3 %copy-start.10 = (f32[1,128,10]{1,0,2:T(1,128)S(1)}, f32[1,128,10]{1,0,2:T(1,128)}, u32[]{:S(2)}) copy-start(f32[1,128,10]{1,0,2:T(1,128)} %param.28) | copy-start | bytes 15364
  24.0 9.3 %collective-permute-start.10 = (bf16[128,1024]{1,0:T(8,128)(2,1)S(1)}, bf16[128,1024]{1,0:T(8,128)(2,1)S(1)}, u32[]{:S(2)}, u32[]{:S(2)}) collective-permute-start(bf16[128,1024]{1,0:T(8,128)(2,1)S(1)} %far_projection.2), channel_id=1, source_target_pairs={{0,16},{8,24},{16,0},{24,8},{1,17},{9,25},{17,1},{25,9},{2,18},{10... | collective-permute-start | bytes 786440 | tf_op jit(solution)/shard_map/projection_sum/ppermute | solution.py:74
  26.4 10.8 %collective-permute-start.11 = (bf16[128,1024]{1,0:T(8,128)(2,1)S(1)}, bf16[128,1024]{1,0:T(8,128)(2,1)S(1)}, u32[]{:S(2)}, u32[]{:S(2)}) collective-permute-start(bf16[128,1024]{1,0:T(8,128)(2,1)S(1)} %far_projection.3), channel_id=1, source_target_pairs={{0,16},{8,24},{16,0},{24,8},{1,17},{9,25},{17,1},{25,9},{2,18},{10... | collective-permute-start | bytes 786440 | tf_op jit(solution)/shard_map/projection_sum/ppermute | solution.py:74
  33.3 3.9 %copy-start.5 = (f32[2048]{0:T(1024)S(1)}, f32[2048]{0:T(1024)}, u32[]{:S(2)}) copy-start(f32[2048]{0:T(1024)} %param.26) | copy-start | bytes 24580
  33.4 25.7 %copy-start.2 = (bf16[1,2048,512]{2,1,0:T(8,128)(2,1)S(1)}, bf16[1,2048,512]{2,1,0:T(8,128)(2,1)}, u32[]{:S(2)}) copy-start(bf16[1,2048,512]{2,1,0:T(8,128)(2,1)} %up_ref.1) | copy-start | bytes 6291460
  33.4 25.7 %copy-start.3 = (bf16[1,512,2048]{2,1,0:T(8,128)(2,1)S(1)}, bf16[1,512,2048]{2,1,0:T(8,128)(2,1)}, u32[]{:S(2)}) copy-start(bf16[1,512,2048]{2,1,0:T(8,128)(2,1)} %down_ref.1) | copy-start | bytes 6291460
  34.3 24.8 %copy-start.1 = (bf16[1,2048,512]{2,1,0:T(8,128)(2,1)S(1)}, bf16[1,2048,512]{2,1,0:T(8,128)(2,1)}, u32[]{:S(2)}) copy-start(bf16[1,2048,512]{2,1,0:T(8,128)(2,1)} %gate_ref.3) | copy-start | bytes 6291460
  59.1 19.6 %copy-start.6 = (f32[2048]{0:T(1024)S(1)}, f32[2048]{0:T(1024)}, u32[]{:S(2)}) copy-start(f32[2048]{0:T(1024)} %param.33) | copy-start | bytes 24580
  59.1 19.6 %copy-start.7 = (s32[1,128]{1,0:T(1,128)S(1)}, s32[1,128]{1,0:T(1,128)}, u32[]{:S(2)}) copy-start(s32[1,128]{1,0:T(1,128)} %mask_ref.1) | copy-start | bytes 1540

commit v8 on v7

--- a/solution.py
+++ b/solution.py
@@ -396,7 +396,7 @@
     eye = iota((tokens, tokens), 0) == iota((tokens, tokens), 1)
     mask = jnp.sum(jnp.where(eye, mask_ref[...].astype(f32), 0.0), axis=1, keepdims=True)
     along = 0.0
-    step = 256
+    step = 512
     for c in range(0, width, step):
         back = back_ref[:, :, c : c + step].reshape(slots, step)
         total = hidden_ref[:, c : c + step] + mm_tn(table, jnp.concatenate([back, back], axis=0))

time: 80.1 us -> 80.1 us (level)
  no operation moved by 1% of the time
where the time goes in v8:
time: 80.1 us; the launch traced here: 79.9 us
  blocking collectives  39.8 us (50%)
  Pallas kernels  16.6 us (21%)
  waiting for transfers between devices  13.2 us (16%)
  starting transfers between devices  10.1 us (13%)
    all_to_all x1, blocking collectives, local_part(): came = lax.all_to_all(rows, ('exp', 'ctx'), 0, 0, tiled=True)  21.4 us
    all_to_all x1, blocking collectives, local_part(): back = lax.all_to_all(done, ('exp', 'ctx'), 0, 0, tiled=True)  18.4 us
    ppermute x12, waiting for transfers between devices, send(): return lax.ppermute(x, 'ctx', pairs)  13.2 us
    ppermute x12, starting transfers between devices, send(): return lax.ppermute(x, 'ctx', pairs)  10.1 us
    pallas_call x1, Pallas kernels, local_part(): pl.pallas_call(functools.partial(inverse_kernel, n, local), out_shape=[wi...  5.83 us
    pallas_call x1, Pallas kernels, local_part(): pl.pallas_call(functools.partial(state_kernel, n, kw, vw), out_shape=[sha...  2.68 us
    pallas_call x1, Pallas kernels, local_part(): pl.pallas_call(functools.partial(pack_late_kernel, n, vw), out_shape=[sha...  1.92 us
  transfers between devices with their start and end apart: 12, of which 4 were waited for; matrix products, arithmetic and copies ran while one was open for 0% of the time, Pallas kernels for 15%

profile of v8, /device:TPU:0, one launch (start us, length us, event | category | flops | bytes accessed | tf_op | source)
XLA Modules:
  0.0 79.9 jit_solution(18399360803380497454)
XLA Ops:
  0.0 1.4 %pack.1 = (bf16[144,256]{1,0:T(8,128)(2,1)S(1)}, bf16[144,256]{1,0:T(8,128)(2,1)S(1)}, bf16[144,256]{1,0:T(8,128)(2,1)S(1)}, bf16[144,256]{1,0:T(8,128)(2,1)S(1)...) custom-call(bf16[1,128,1024]{2,1,0:T(8,128)(2,1)} %k_ref.1, ...), custom_call_target="tpu_custom_call" | custom-call | tf_op jit(solution)/shard_map/pack/pallas_call | solution.py:440
  1.4 0.5 collective-permute-start
  1.9 2.6 %collective-permute-start.1 = (bf16[144,256]{1,0:T(8,128)(2,1)S(1)}, bf16[144,256]{1,0:T(8,128)(2,1)S(1)}, u32[]{:S(2)}, u32[]{:S(2)}) collective-permute-start(bf16[144,256]{1,0:T(8,128)(2,1)S(1)} %get-tuple-element.38), channel_id=1, source_target_pairs={{0,16},{8,24},{16,0},{24,8},{1,17},{9,25},{17,1},{25,9},{2,18},{10... | collective-permute-start | bytes 221192 | tf_op jit(solution)/shard_map/heads_exchange/ppermute | solution.py:74
  4.5 0.1 collective-permute-start.2
  4.5 1.7 %collective-permute-start.5 = (bf16[128,768]{1,0:T(8,128)(2,1)S(1)}, bf16[128,768]{1,0:T(8,128)(2,1)S(1)}, u32[]{:S(2)}, u32[]{:S(2)}) collective-permute-start(bf16[128,768]{1,0:T(8,128)(2,1)S(1)} %get-tuple-element.49), channel_id=1, source_target_pairs={{0,16},{8,24},{16,0},{24,8},{1,17},{9,25},{17,1},{25,9},{2,18},{10... | collective-permute-start | bytes 589832 | tf_op jit(solution)/shard_map/heads_exchange/ppermute | solution.py:74
  6.3 0.0 collective-permute-start.6
  6.3 1.9 %pack_late.1 = (bf16[128,1024]{1,0:T(8,128)(2,1)S(1)}, bf16[512,1024]{1,0:T(8,128)(2,1)S(1)}, bf16[512,1024]{1,0:T(8,128)(2,1)S(1)}) custom-call(bf16[1,128,2048]{2,1,0:T(8,128)(2,1)} %gate_ref.2, bf16[512,2048]{1,0:T(8,128)(2,1)} %refs_0_.1), custom_call_target="tpu_custom_call" | custom-call | tf_op jit(solution)/shard_map/pack_late/pallas_call | solution.py:448
  8.2 0.0 collective-permute-done.refs_1_
  8.2 0.5 collective-permute-start.8
  8.7 0.0 collective-permute-done.1.refs_2_
  8.7 0.1 collective-permute-start.9
  8.8 0.0 collective-permute-done.2.refs_3_
  8.8 0.0 copy-start.11
  8.8 0.4 collective-permute-start.4
  9.2 5.8 %block_inverses.1 = (bf16[4,4,128,256]{3,2,1,0:T(8,128)(2,1)S(1)}, bf16[4,4,128,256]{3,2,1,0:T(8,128)(2,1)S(1)}, bf16[4,4,128,256]{3,2,1,0:T(8,128)(2,1)S(1)}, f...) custom-call(bf16[144,256]{1,0:T(8,128)(2,1)S(1)} %get-tuple-element.43.refs_0_, ...), custom_call_target="tpu_custom_call" | custom-call | flops 6000000000 | bytes 1000000 | tf_op jit(solution)/shard_map/block_inverses/pallas_call | solution.py:462
  15.0 0.0 collective-permute-done.5.refs_6_
  15.0 1.8 %collective-permute-start.3 = (bf16[128,1024]{1,0:T(8,128)(2,1)S(1)}, bf16[128,1024]{1,0:T(8,128)(2,1)S(1)}, u32[]{:S(2)}, u32[]{:S(2)}) collective-permute-start(bf16[128,1024]{1,0:T(8,128)(2,1)S(1)} %get-tuple-element.42), channel_id=1, source_target_pairs={{0,16},{8,24},{16,0},{24,8},{1,17},{9,25},{17,1},{25,9},{2,18},{10... | collective-permute-start | bytes 786440 | tf_op jit(solution)/shard_map/late_exchange/ppermute | solution.py:74
  16.8 0.3 collective-permute-done.6.refs_7_
  17.1 0.0 collective-permute-done.4.refs_5_
  17.1 0.0 copy-done.11
  17.1 0.0 copy-start
  17.1 2.7 %states.1 = (f32[2,128,512]{2,1,0:T(8,128)S(1)}, bf16[2,128,512]{2,1,0:T(8,128)(2,1)S(1)}) custom-call(bf16[144,256]{1,0:T(8,128)(2,1)S(1)} %get-tuple-element.43.refs_0_, bf16[144,256]{1,0:T(8,128)(2,1)S(1)} %collective-permute-done.refs_1_, bf16[144,256]{1,0:T(8,128)(2,1)S(1)} %collective-permute-done.1.refs_2_, ...), custom_call_target="tpu_custom_call" | custom-call | flops 4000000000 | bytes 1000000 | tf_op jit(solution)/shard_map/states/pallas_call | solution.py:474
  19.8 0.2 collective-permute-start.7
  20.1 3.4 %collective-permute-done.3.refs_0_ = bf16[128,1024]{1,0:T(8,128)(2,1)S(1)} collective-permute-done((bf16[128,1024]{1,0:T(8,128)(2,1)S(1)}, bf16[128,1024]{1,0:T(8,128)(2,1)S(1)}, u32[]{:S(2)}, u32[]{:S(2)}) %collective-permute-start.3) | collective-permute-done | bytes 262176 | tf_op jit(solution)/shard_map/late_exchange/ppermute | solution.py:74
  23.4 0.0 collective-permute-done.7.refs_2_.other_ref
  23.4 0.0 collective-permute-done.8.refs_4_.refs_1_
  23.4 0.0 copy-done
  23.4 0.5 far_projection.2
  24.0 0.0 copy-start.4
  24.0 0.0 copy-start.8
  24.0 0.0 copy-start.9
  24.0 0.0 copy-start.10
  24.0 1.8 %collective-permute-start.10 = (bf16[128,1024]{1,0:T(8,128)(2,1)S(1)}, bf16[128,1024]{1,0:T(8,128)(2,1)S(1)}, u32[]{:S(2)}, u32[]{:S(2)}) collective-permute-start(bf16[128,1024]{1,0:T(8,128)(2,1)S(1)} %far_projection.2), channel_id=1, source_target_pairs={{0,16},{8,24},{16,0},{24,8},{1,17},{9,25},{17,1},{25,9},{2,18},{10... | collective-permute-start | bytes 786440 | tf_op jit(solution)/shard_map/projection_sum/ppermute | solution.py:74
  25.8 0.0 collective-permute-done.9.refs_4_.refs_2_
  25.8 0.5 far_projection.3
  26.4 0.4 collective-permute-start.11
  26.7 6.6 %collective-permute-done.10.refs_3_ = bf16[128,1024]{1,0:T(8,128)(2,1)S(1)} collective-permute-done((bf16[128,1024]{1,0:T(8,128)(2,1)S(1)}, bf16[128,1024]{1,0:T(8,128)(2,1)S(1)}, u32[]{:S(2)}, u32[]{:S(2)}) %collective-permute-start.10) | collective-permute-done | bytes 262176 | tf_op jit(solution)/shard_map/projection_sum/ppermute | solution.py:74
  33.3 0.0 copy-done.4
  33.3 0.0 copy-done.8
  33.3 0.0 copy-done.9
  33.3 0.0 copy-done.10
  33.3 0.0 copy-start.5
  33.4 0.0 copy-start.2
  33.4 0.0 copy-start.3
  33.4 0.9 %home.1 = (f32[128,2048]{1,0:T(8,128)S(1)}, bf16[128,128]{1,0:T(8,128)(2,1)S(1)}, f32[128,128]{1,0:T(8,128)S(1)}) custom-call(bf16[1,128,2048]{2,1,0:T(8,128)(2,1)S(1)} %copy-done.8, bf16[1,128,2048]{2,1,0:T(8,128)(2,1)S(1)} %copy-done.4, f32[2,128,512]{2,1,0:T(8,128)S(1)} %get-tuple-element.61.refs_1_.keep_ref, ...), custom_call_target="tpu_custom_call" | custom-call | flops 6000000000 | bytes 1000 | tf_op jit(solution)/shard_map/home/pallas_call | solution.py:499
  34.3 0.0 copy-start.1
  34.3 2.9 %collective-permute-done.11.refs_0_ = bf16[128,1024]{1,0:T(8,128)(2,1)S(1)} collective-permute-done((bf16[128,1024]{1,0:T(8,128)(2,1)S(1)}, bf16[128,1024]{1,0:T(8,128)(2,1)S(1)}, u32[]{:S(2)}, u32[]{:S(2)}) %collective-permute-start.11) | collective-permute-done | bytes 262176 | tf_op jit(solution)/shard_map/projection_sum/ppermute | solution.py:74
  37.2 0.0 copy-done.5
  37.2 0.5 dispatch.1
  37.7 21.4 %all_to_all.10.rows_ref = bf16[32,4,2048]{2,1,0:T(4,128)(2,1)S(1)} all-to-all(bf16[32,4,2048]{2,1,0:T(4,128)(2,1)S(1)} %get-tuple-element.66), channel_id=1, replica_groups=mesh['ctx'=4,'exp'=8] {'exp','ctx'}, dimensions={0} | all-to-all | bytes 1048576 | tf_op jit(solution)/shard_map/to_experts/all_to_all | solution.py:522
  59.1 0.0 copy-done.2
  59.1 0.0 copy-done.3
  59.1 0.0 copy-done.1
  59.1 0.0 copy-start.6
  59.1 0.0 copy-start.7
  59.1 1.1 %experts.1 = bf16[32,4,2048]{2,1,0:T(4,128)(2,1)S(1)} custom-call(bf16[32,4,2048]{2,1,0:T(4,128)(2,1)S(1)} %all_to_all.10.rows_ref, bf16[1,2048,512]{2,1,0:T(8,128)(2,1)S(1)} %copy-done.1, bf16[1,2048,512]{2,1,0:T(8,128)(2,1)S(1)} %copy-done.2, bf16[1,512,2048]{2,1,0:T(8,128)(2,1)S(1)} %copy-done.3), custom_call_target="tpu_custom_call" | custom-call | tf_op jit(solution)/shard_map/experts/pallas_call | solution.py:524
  60.2 18.4 %all_to_all.11.back_ref = bf16[32,4,2048]{2,1,0:T(4,128)(2,1)S(1)} all-to-all(bf16[32,4,2048]{2,1,0:T(4,128)(2,1)S(1)} %experts.1), channel_id=1, replica_groups=mesh['ctx'=4,'exp'=8] {'exp','ctx'}, dimensions={0} | all-to-all | bytes 1048576 | tf_op jit(solution)/shard_map/from_experts/all_to_all | solution.py:530
  78.6 0.0 copy-done.6
  78.6 0.0 copy-done.7
  78.6 1.3 %combine.1 = bf16[1,128,2048]{2,1,0:T(8,128)(2,1)} custom-call(f32[128,2048]{1,0:T(8,128)S(1)} %get-tuple-element.64.hidden_ref, f32[128,128]{1,0:T(8,128)S(1)} %get-tuple-element.65.table_ref, bf16[32,4,2048]{2,1,0:T(4,128)(2,1)S(1)} %all_to_all.11.back_ref, s32[1,128]{1,0:T(1,128)S(1)} %copy-done.7, f32[1,2048]{1,0:T(1,128)S(1)} %bitcast.8), custom_call_target="tpu_custom_call" | custom-call | tf_op jit(solution)/shard_map/combine/pallas_call | solution.py:532
Async XLA Ops:
  1.4 6.8 %collective-permute-start = (bf16[144,256]{1,0:T(8,128)(2,1)S(1)}, bf16[144,256]{1,0:T(8,128)(2,1)S(1)}, u32[]{:S(2)}, u32[]{:S(2)}) collective-permute-start(bf16[144,256]{1,0:T(8,128)(2,1)S(1)} %get-tuple-element.37), channel_id=1, source_target_pairs={{0,8},{8,0},{16,24},{24,16},{1,9},{9,1},{17,25},{25,17},{2,10},{10... | collective-permute-start | bytes 221192 | tf_op jit(solution)/shard_map/heads_exchange/ppermute | solution.py:74
  1.9 6.8 %collective-permute-start.1 = (bf16[144,256]{1,0:T(8,128)(2,1)S(1)}, bf16[144,256]{1,0:T(8,128)(2,1)S(1)}, u32[]{:S(2)}, u32[]{:S(2)}) collective-permute-start(bf16[144,256]{1,0:T(8,128)(2,1)S(1)} %get-tuple-element.38), channel_id=1, source_target_pairs={{0,16},{8,24},{16,0},{24,8},{1,17},{9,25},{17,1},{25,9},{2,18},{10... | collective-permute-start | bytes 221192 | tf_op jit(solution)/shard_map/heads_exchange/ppermute | solution.py:74
  4.5 4.3 %collective-permute-start.2 = (bf16[144,256]{1,0:T(8,128)(2,1)S(1)}, bf16[144,256]{1,0:T(8,128)(2,1)S(1)}, u32[]{:S(2)}, u32[]{:S(2)}) collective-permute-start(bf16[144,256]{1,0:T(8,128)(2,1)S(1)} %get-tuple-element.39), channel_id=1, source_target_pairs={{0,24},{8,16},{16,8},{24,0},{1,25},{9,17},{17,9},{25,1},{2,26},{10... | collective-permute-start | bytes 221192 | tf_op jit(solution)/shard_map/heads_exchange/ppermute | solution.py:74
  4.5 10.5 %collective-permute-start.5 = (bf16[128,768]{1,0:T(8,128)(2,1)S(1)}, bf16[128,768]{1,0:T(8,128)(2,1)S(1)}, u32[]{:S(2)}, u32[]{:S(2)}) collective-permute-start(bf16[128,768]{1,0:T(8,128)(2,1)S(1)} %get-tuple-element.49), channel_id=1, source_target_pairs={{0,16},{8,24},{16,0},{24,8},{1,17},{9,25},{17,1},{25,9},{2,18},{10... | collective-permute-start | bytes 589832 | tf_op jit(solution)/shard_map/heads_exchange/ppermute | solution.py:74
  6.3 10.8 %collective-permute-start.6 = (bf16[128,768]{1,0:T(8,128)(2,1)S(1)}, bf16[128,768]{1,0:T(8,128)(2,1)S(1)}, u32[]{:S(2)}, u32[]{:S(2)}) collective-permute-start(bf16[128,768]{1,0:T(8,128)(2,1)S(1)} %get-tuple-element.50), channel_id=1, source_target_pairs={{0,24},{8,16},{16,8},{24,0},{1,25},{9,17},{17,9},{25,1},{2,26},{10... | collective-permute-start | bytes 589832 | tf_op jit(solution)/shard_map/heads_exchange/ppermute | solution.py:74
  8.2 15.2 %collective-permute-start.8 = (bf16[512,1024]{1,0:T(8,128)(2,1)S(1)}, bf16[512,1024]{1,0:T(8,128)(2,1)S(1)}, u32[]{:S(2)}, u32[]{:S(2)}) collective-permute-start(bf16[512,1024]{1,0:T(8,128)(2,1)S(1)} %get-tuple-element.58), channel_id=1, source_target_pairs={{0,8},{8,0},{16,24},{24,16},{1,9},{9,1},{17,25},{25,17},{2,10},{10... | collective-permute-start | bytes 3145736 | tf_op jit(solution)/shard_map/late_exchange/ppermute | solution.py:74
  8.7 17.1 %collective-permute-start.9 = (bf16[512,1024]{1,0:T(8,128)(2,1)S(1)}, bf16[512,1024]{1,0:T(8,128)(2,1)S(1)}, u32[]{:S(2)}, u32[]{:S(2)}) collective-permute-start(bf16[512,1024]{1,0:T(8,128)(2,1)S(1)} %get-tuple-element.60), channel_id=1, source_target_pairs={{0,8},{8,0},{16,24},{24,16},{1,9},{9,1},{17,25},{25,17},{2,10},{10... | collective-permute-start | bytes 3145736 | tf_op jit(solution)/shard_map/late_exchange/ppermute | solution.py:74
  8.8 8.3 %copy-start.11 = (f32[128]{0:T(128)S(1)}, f32[128]{0:T(128)}, u32[]{:S(2)}) copy-start(f32[128]{0:T(128)} %param.23) | copy-start | bytes 1540
  8.8 8.3 %collective-permute-start.4 = (bf16[128,768]{1,0:T(8,128)(2,1)S(1)}, bf16[128,768]{1,0:T(8,128)(2,1)S(1)}, u32[]{:S(2)}, u32[]{:S(2)}) collective-permute-start(bf16[128,768]{1,0:T(8,128)(2,1)S(1)} %get-tuple-element.48), channel_id=1, source_target_pairs={{0,8},{8,0},{16,24},{24,16},{1,9},{9,1},{17,25},{25,17},{2,10},{10... | collective-permute-start | bytes 589832 | tf_op jit(solution)/shard_map/late_exchange/ppermute | solution.py:74
  15.0 8.4 %collective-permute-start.3 = (bf16[128,1024]{1,0:T(8,128)(2,1)S(1)}, bf16[128,1024]{1,0:T(8,128)(2,1)S(1)}, u32[]{:S(2)}, u32[]{:S(2)}) collective-permute-start(bf16[128,1024]{1,0:T(8,128)(2,1)S(1)} %get-tuple-element.42), channel_id=1, source_target_pairs={{0,16},{8,24},{16,0},{24,8},{1,17},{9,25},{17,1},{25,9},{2,18},{10... | collective-permute-start | bytes 786440 | tf_op jit(solution)/shard_map/late_exchange/ppermute | solution.py:74
  17.1 6.3 %copy-start = (bf16[512,2048]{1,0:T(8,128)(2,1)S(1)}, bf16[512,2048]{1,0:T(8,128)(2,1)}, u32[]{:S(2)}) copy-start(bf16[512,2048]{1,0:T(8,128)(2,1)} %refs_0_.1) | copy-start | bytes 6291460
  19.8 3.6 %collective-permute-start.7 = (bf16[2,128,512]{2,1,0:T(8,128)(2,1)S(1)}, bf16[2,128,512]{2,1,0:T(8,128)(2,1)S(1)}, u32[]{:S(2)}, u32[]{:S(2)}) collective-permute-start(bf16[2,128,512]{2,1,0:T(8,128)(2,1)S(1)} %get-tuple-element.57), channel_id=1, source_target_pairs={{0,8},{8,0},{16,24},{24,16},{1,9},{9,1},{17,25},{25,17},{2,10},{10... | collective-permute-start | bytes 786440 | tf_op jit(solution)/shard_map/ppermute | solution.py:74
  24.0 9.4 %copy-start.4 = (bf16[1,128,2048]{2,1,0:T(8,128)(2,1)S(1)}, bf16[1,128,2048]{2,1,0:T(8,128)(2,1)}, u32[]{:S(2)}) copy-start(bf16[1,128,2048]{2,1,0:T(8,128)(2,1)} %gate_ref.2) | copy-start | bytes 1572868
  24.0 9.3 %copy-start.8 = (bf16[1,128,2048]{2,1,0:T(8,128)(2,1)S(1)}, bf16[1,128,2048]{2,1,0:T(8,128)(2,1)}, u32[]{:S(2)}) copy-start(bf16[1,128,2048]{2,1,0:T(8,128)(2,1)} %residual_ref.1) | copy-start | bytes 1572868
  24.0 9.3 %copy-start.9 = (s32[1,128,10]{1,0,2:T(1,128)S(1)}, s32[1,128,10]{1,0,2:T(1,128)}, u32[]{:S(2)}) copy-start(s32[1,128,10]{1,0,2:T(1,128)} %param.27) | copy-start | bytes 15364
  24.0 9.3 %copy-start.10 = (f32[1,128,10]{1,0,2:T(1,128)S(1)}, f32[1,128,10]{1,0,2:T(1,128)}, u32[]{:S(2)}) copy-start(f32[1,128,10]{1,0,2:T(1,128)} %param.28) | copy-start | bytes 15364
  24.0 9.3 %collective-permute-start.10 = (bf16[128,1024]{1,0:T(8,128)(2,1)S(1)}, bf16[128,1024]{1,0:T(8,128)(2,1)S(1)}, u32[]{:S(2)}, u32[]{:S(2)}) collective-permute-start(bf16[128,1024]{1,0:T(8,128)(2,1)S(1)} %far_projection.2), channel_id=1, source_target_pairs={{0,16},{8,24},{16,0},{24,8},{1,17},{9,25},{17,1},{25,9},{2,18},{10... | collective-permute-start | bytes 786440 | tf_op jit(solution)/shard_map/projection_sum/ppermute | solution.py:74
  26.4 10.8 %collective-permute-start.11 = (bf16[128,1024]{1,0:T(8,128)(2,1)S(1)}, bf16[128,1024]{1,0:T(8,128)(2,1)S(1)}, u32[]{:S(2)}, u32[]{:S(2)}) collective-permute-start(bf16[128,1024]{1,0:T(8,128)(2,1)S(1)} %far_projection.3), channel_id=1, source_target_pairs={{0,16},{8,24},{16,0},{24,8},{1,17},{9,25},{17,1},{25,9},{2,18},{10... | collective-permute-start | bytes 786440 | tf_op jit(solution)/shard_map/projection_sum/ppermute | solution.py:74
  33.3 3.9 %copy-start.5 = (f32[2048]{0:T(1024)S(1)}, f32[2048]{0:T(1024)}, u32[]{:S(2)}) copy-start(f32[2048]{0:T(1024)} %param.26) | copy-start | bytes 24580
  33.4 25.7 %copy-start.2 = (bf16[1,2048,512]{2,1,0:T(8,128)(2,1)S(1)}, bf16[1,2048,512]{2,1,0:T(8,128)(2,1)}, u32[]{:S(2)}) copy-start(bf16[1,2048,512]{2,1,0:T(8,128)(2,1)} %up_ref.1) | copy-start | bytes 6291460
  33.4 25.7 %copy-start.3 = (bf16[1,512,2048]{2,1,0:T(8,128)(2,1)S(1)}, bf16[1,512,2048]{2,1,0:T(8,128)(2,1)}, u32[]{:S(2)}) copy-start(bf16[1,512,2048]{2,1,0:T(8,128)(2,1)} %down_ref.1) | copy-start | bytes 6291460
  34.3 24.8 %copy-start.1 = (bf16[1,2048,512]{2,1,0:T(8,128)(2,1)S(1)}, bf16[1,2048,512]{2,1,0:T(8,128)(2,1)}, u32[]{:S(2)}) copy-start(bf16[1,2048,512]{2,1,0:T(8,128)(2,1)} %gate_ref.3) | copy-start | bytes 6291460
  59.1 19.6 %copy-start.6 = (f32[2048]{0:T(1024)S(1)}, f32[2048]{0:T(1024)}, u32[]{:S(2)}) copy-start(f32[2048]{0:T(1024)} %param.33) | copy-start | bytes 24580
  59.1 19.6 %copy-start.7 = (s32[1,128]{1,0:T(1,128)S(1)}, s32[1,128]{1,0:T(1,128)}, u32[]{:S(2)}) copy-start(s32[1,128]{1,0:T(1,128)} %mask_ref.1) | copy-start | bytes 1540
